TPU v7x, 128 devices: a whole 4x4x4 slice. The times are simulated.
128 devices in a mesh: dp: 8 (over z, x_lo), row: 2 (over x_hi), col: 8 (over y, core).
Axes of the slice: x: 4 (x_hi: 2, x_lo: 2; x = x_hi * 2 + x_lo), y: 4, z: 4, core: 2. Of those that a mesh axis runs over, the one named last changes fastest.
Arguments:
- inputs: bfloat16 [16512, 1024], P(('dp', 'col'), 'row'), may hold values from -6 to 6
- w_qkv: bfloat16 [1, 1024, 3072], P(None, 'row', 'col'), may hold values from -0.1875 to 0.1875
- qv_bias: bfloat16 [1, 8, 2, 1, 128], P(None, 'col', 'row'), may hold values from -0.059814453 to 0.059814453
- w_out: bfloat16 [1, 1024, 1024], P(None, 'col', 'row'), may hold values from -6 to 6
- w_fc1: bfloat16 [1, 1024, 4096], P(None, 'row', 'col'), may hold values from -0.1875 to 0.1875
- fc1_bias: bfloat16 [1, 8, 2, 256], P(None, 'col', 'row'), may hold values from -1.796875 to 1.796875
- w_fc2: bfloat16 [1, 4096, 1024], P(None, 'col', 'row'), may hold values from -0.09375 to 0.09375
- ln_gain: bfloat16 [1, 2, 1024], P(None, None, 'row'), may hold values from 0.5 to 1.5
- ln_bias: bfloat16 [1, 2, 1024], P(None, None, 'row'), may hold values from -1.1953125 to 1.1953125
- layer_scale: bfloat16 [1, 2, 1024], P(None, None, 'row'), may hold values from 0.5 to 1.5
- branch_bias: bfloat16 [1, 2, 1024], P(None, None, 'row'), may hold values from -1.1953125 to 1.1953125
- cotangent: bfloat16 [16512, 1024], P(('dp', 'col'), 'row'), may hold values from -6 to 6
Outputs:
- output: float32 [16512, 1024], P(('dp', 'col'), 'row')
- input_grad: float32 [16512, 1024], P(('dp', 'col'), 'row')
- grad_w_qkv: float32 [1, 1024, 3072], P(None, 'row', 'col')
- grad_qv_bias: float32 [1, 8, 2, 1, 128], P(None, 'col', 'row')
- grad_w_out: float32 [1, 1024, 1024], P(None, 'col', 'row')
- grad_w_fc1: float32 [1, 1024, 4096], P(None, 'row', 'col')
- grad_fc1_bias: float32 [1, 8, 2, 256], P(None, 'col', 'row')
- grad_w_fc2: float32 [1, 4096, 1024], P(None, 'col', 'row')
- grad_ln_gain: float32 [1, 2, 1024], P(None, None, 'row')
- grad_ln_bias: float32 [1, 2, 1024], P(None, None, 'row')
- grad_layer_scale: float32 [1, 2, 1024], P(None, None, 'row')
- grad_branch_bias: float32 [1, 2, 1024], P(None, None, 'row')
All inputs are finite; a program needn't handle non-finite values.
Results may differ from a plain program's by a relative error of at most 0.0098.
Values may be sent and summed in bfloat16 or wider, within the bound.
No kernel may reach another device: no remote copies, remote signals or barrier semaphores. Data moves between devices by JAX's collectives and lax.ppermute only.
A program may use at most 128 MiB of HBM per device.

v0:
```python
import math

import jax
import jax.numpy as jnp
from jax import lax
from jax.experimental import pallas as pl
from jax.experimental.pallas import tpu as pltpu
from jax.sharding import Mesh, PartitionSpec as P

D = 1024
HD = 64
SEQ = 1025
EPSILON = 1e-06
MASKED = -1000000000.0

HALF = 129
ROWS = 136
SLOTS = 8
NY = 4
NZ = 4

F32 = jnp.float32
BF = jnp.bfloat16
GROUP = ("xh", "y", "c")


def is_home(r, y):
    return y // 2 == r


def group_index(r, y, c):
    return (r * NY + y % NY) * 2 + c


def entry_pairs():
    places = [(r, y, c) for r in range(2) for y in range(NY) for c in range(2)]
    first, second = [], []
    for r, y, c in places:
        me = group_index(r, y, c)
        if is_home(r, y):
            first.append((me, group_index(r, y + 2, c)))
        else:
            first.append((me, group_index(1 - r, y, c)))
            second.append((me, group_index(1 - r, y + 2, c)))
    return first, second


ENTRY_FIRST, ENTRY_SECOND = entry_pairs()
EXIT_FIRST = [(b, a) for a, b in ENTRY_FIRST]
EXIT_SECOND = [(b, a) for a, b in ENTRY_SECOND]


def swap(value, axis):
    return lax.ppermute(value, axis, [(0, 1), (1, 0)])


def pull(value, axis, distance):
    return lax.ppermute(value, axis, [((i + distance) % 4, i) for i in range(4)])


def after(value, *earlier):
    return lax.optimization_barrier((value,) + earlier)[0]


def place_in(block, spare, home):
    first = jnp.concatenate([block[:HALF], spare], axis=0)
    second = jnp.concatenate([block[HALF:], spare], axis=0)
    moved = lax.ppermute(jnp.where(home, second, first), GROUP, ENTRY_FIRST)
    crossed = lax.ppermute(second, GROUP, ENTRY_SECOND)
    return jnp.where(home, first, moved), jnp.where(home, moved, crossed)


def place_out(values, home):
    own, other = values[:HALF, : D // 2], values[:HALF, D // 2 :].astype(BF)
    moved = lax.ppermute(jnp.where(home, other, own.astype(BF)), GROUP, EXIT_FIRST)
    crossed = lax.ppermute(other, GROUP, EXIT_SECOND)
    moved, crossed = moved.astype(F32), crossed.astype(F32)
    return jnp.concatenate([jnp.where(home, own, moved), jnp.where(home, moved, crossed)], axis=0)


def gather(piece):
    near = jnp.concatenate([piece] + [pull(piece, "y", d) for d in (1, 2, 3)], axis=0)
    return near, swap(near, "c")


def scatter_begin(halves, weight, contract):
    near, far = halves
    far = swap(dot(far, weight, contract).astype(BF), "c")
    summed = dot(near, weight, contract) + far.astype(F32)
    return summed[:ROWS], [summed[d * ROWS : (d + 1) * ROWS].astype(BF) for d in (1, 2, 3)]


def scatter_end(total, pieces):
    for d, piece in zip((1, 2, 3), pieces):
        total = total + pull(piece, "y", -d).astype(F32)
    return total


def image_sum(own, other):
    return own + swap(other.astype(BF), "xh").astype(F32)


def replica_scatter(values):
    rows = values.shape[0] // NZ
    z = lax.axis_index("z")

    def chunk(d):
        return lax.dynamic_slice_in_dim(values, ((z + d) % NZ) * rows, rows, 0)

    total = chunk(0)
    for d in (1, 2, 3):
        total = total + pull(chunk(d).astype(BF), "z", -d).astype(F32)
    return total.astype(BF)


def replica_gather(total):
    z = lax.axis_index("z")
    total = (total.astype(F32) + swap(total, "xl").astype(F32)).astype(BF)
    pieces = [total] + [pull(total, "z", d) for d in (1, 2, 3)]

    def slot(k):
        d = (k - z) % NZ
        low = jnp.where(d == 0, pieces[0], pieces[1])
        return jnp.where(d < 2, low, jnp.where(d == 2, pieces[2], pieces[3])).astype(F32)

    return jnp.concatenate([slot(k) for k in range(NZ)], axis=0)


def column_sum(values):
    values = values + swap(values, "c")
    opposite, later, earlier = (pull(values, "y", d) for d in (2, 1, 3))
    return (values + opposite) + (later + earlier)


def dot(first, second, contract):
    return lax.dot_general(
        first, second, (((contract[0],), (contract[1],)), ((), ())), preferred_element_type=F32
    )


def norm(values, gain, shift):
    center = jnp.mean(values, axis=1, keepdims=True)
    moved = values - center
    inverse = lax.rsqrt(jnp.mean(moved * moved, axis=1, keepdims=True) + EPSILON)
    scaled = moved * inverse
    return (scaled * gain + shift).astype(BF), scaled, inverse


def norm_pull(grad, scaled, inverse, gain):
    weighted = grad * gain
    mean = jnp.mean(weighted, axis=1, keepdims=True)
    inner = jnp.mean(weighted * scaled, axis=1, keepdims=True)
    return inverse * (weighted - mean - scaled * inner)


BLOCK = 272


def chances(query, key, mask):
    scores = dot(query * (1.0 / math.sqrt(HD)), key, (1, 1))
    scores = jnp.where(mask > 0, scores, MASKED)
    weights = jnp.exp(scores - jnp.max(scores, axis=1, keepdims=True))
    return weights * (1.0 / jnp.sum(weights, axis=1, keepdims=True))


def attend_kernel(mask_ref, packed_ref, out_ref):
    mask = mask_ref[...]
    for head in range(2):
        part = [slice(128 * s + HD * head, 128 * s + HD * (head + 1)) for s in range(3)]
        key, value = packed_ref[:, part[1]], packed_ref[:, part[2]]
        for block in range(SLOTS * ROWS // BLOCK):
            rows = slice(block * BLOCK, (block + 1) * BLOCK)
            chance = chances(packed_ref[rows, part[0]], key, mask).astype(BF)
            out_ref[rows, part[0]] = dot(chance, value, (1, 0)).astype(BF)


def attend_pull_kernel(mask_ref, packed_ref, grad_ref, out_ref):
    mask = mask_ref[...]
    factor = 1.0 / math.sqrt(HD)
    for head in range(2):
        part = [slice(128 * s + HD * head, 128 * s + HD * (head + 1)) for s in range(3)]
        key, value = packed_ref[:, part[1]], packed_ref[:, part[2]]
        key_grad = jnp.zeros((SLOTS * ROWS, HD), F32)
        value_grad = jnp.zeros((SLOTS * ROWS, HD), F32)
        for block in range(SLOTS * ROWS // BLOCK):
            rows = slice(block * BLOCK, (block + 1) * BLOCK)
            query, grad = packed_ref[rows, part[0]], grad_ref[rows, part[0]]
            chance = chances(query, key, mask)
            chance_grad = dot(grad, value, (1, 1))
            inner = jnp.sum(chance_grad * chance, axis=1, keepdims=True)
            score_grad = (chance * (chance_grad - inner)).astype(BF)
            out_ref[rows, part[0]] = (dot(score_grad, key, (1, 0)) * factor).astype(BF)
            key_grad = key_grad + dot(score_grad, query, (0, 0))
            value_grad = value_grad + dot(chance.astype(BF), grad, (0, 0))
        out_ref[:, part[1]] = (key_grad * factor).astype(BF)
        out_ref[:, part[2]] = value_grad.astype(BF)


def local_kernel(kernel, width, micros, *operands):
    return pl.pallas_call(
        kernel,
        out_shape=jax.ShapeDtypeStruct((SLOTS * ROWS, width), BF),
        in_specs=[pl.BlockSpec(memory_space=pltpu.VMEM)] * len(operands),
        out_specs=pl.BlockSpec(memory_space=pltpu.VMEM),
        compiler_params=pltpu.CompilerParams(vmem_limit_bytes=32 * 1024 * 1024),
        cost_estimate=pl.CostEstimate(
            flops=micros * 1000000000, bytes_accessed=micros * 3000000, transcendentals=0
        ),
    )(*operands)


def attend(packed, mask):
    return local_kernel(attend_kernel, 2 * HD, 8, mask, packed)


def attend_pull(packed, mask, mixture_grad):
    return local_kernel(attend_pull_kernel, 6 * HD, 12, mask, packed, mixture_grad)


def shards(
    inputs,
    w_qkv,
    qv_bias,
    w_out,
    w_fc1,
    fc1_bias,
    w_fc2,
    ln_gain,
    ln_bias,
    layer_scale,
    branch_bias,
    cotangent,
):
    r, y, c = (lax.axis_index(name) for name in GROUP)
    home = is_home(r, y)

    def in_order(mine, other):
        return jnp.where(r == 0, jnp.concatenate([mine, other]), jnp.concatenate([other, mine]))

    def pick(pair):
        return jnp.where(r == 0, pair[0], pair[1]), jnp.where(r == 0, pair[1], pair[0])

    own_rows = [ln_gain[0], ln_bias[0], layer_scale[0], branch_bias[0]]
    own_rows = jnp.concatenate(own_rows, axis=0)
    small = jnp.concatenate([qv_bias.reshape(-1), fc1_bias.reshape(-1)])
    spare = ROWS - HALF
    spare_rows = jnp.pad(own_rows[spare:], ((0, spare - 1), (0, 0)))
    spare_rows = jnp.concatenate([own_rows[:spare], spare_rows], axis=1)
    block = jnp.concatenate([inputs, cotangent], axis=1)
    mine, theirs = place_in(block, spare_rows, home)
    real = jnp.arange(ROWS)[:, None] < HALF
    x = jnp.concatenate([mine[:, : D // 2], theirs[:, : D // 2]], axis=1)
    x = jnp.where(real, x.astype(F32), 0.0)
    upstream = jnp.concatenate([mine[:, D // 2 :], theirs[:, D // 2 :]], axis=1)
    upstream = jnp.where(real, upstream.astype(F32), 0.0)
    rows = jnp.concatenate([own_rows[:spare], theirs[HALF:, : D // 2]], axis=1).astype(F32)
    gains, shifts, scales, first_bias = rows[0:2], rows[2:4], rows[4:6], rows[6:7]
    second_bias = theirs[HALF : HALF + 1, D // 2 :]
    second_bias = jnp.concatenate([own_rows[spare:], second_bias], axis=1).astype(F32)

    out_columns = w_out[0].reshape(128, 4, 128).transpose(1, 0, 2).reshape(D // 2, 128)
    first_weights = jnp.concatenate([w_qkv[0], out_columns], axis=1)
    small_row = jnp.pad(small[None], ((0, 15), (0, 128)))
    first_weights = jnp.concatenate([first_weights, small_row], axis=0)
    first_weights = swap(after(first_weights, theirs), "xh")
    small_other = first_weights[D // 2, :384]
    qkv_weight = jnp.concatenate([w_qkv[0], first_weights[: D // 2, :384]], axis=0)
    qkv_weight = qkv_weight.reshape(D, 2, 3, HD).transpose(0, 2, 1, 3).reshape(D, 6 * HD)
    out_other = first_weights[: D // 2, 384:].reshape(4, 128, 128).transpose(1, 0, 2)
    out_block = jnp.concatenate([w_out[0], out_other.reshape(128, D // 2)], axis=1)
    fc1_other = swap(after(w_fc1[0], first_weights), "xh")
    fc2_other = swap(after(w_fc2[0], fc1_other), "xh")
    fc1_weight = jnp.concatenate([w_fc1[0], fc1_other], axis=0)
    fc2_weight = jnp.concatenate([w_fc2[0], fc2_other], axis=1)
    normed, scaled_first, inverse_first = norm(x, gains[0], shifts[0])
    normed_first = gather(normed)
    head_bias = in_order(small[:128], small_other[:128]).astype(F32).reshape(2, 2, HD)
    zeros = jnp.zeros((128,), F32)
    full_bias = jnp.concatenate([head_bias[:, 0].reshape(-1), zeros, head_bias[:, 1].reshape(-1)])
    unit_bias = in_order(small[128:], small_other[128:]).astype(F32)

    packed = [(dot(half, qkv_weight, (1, 0)) + full_bias).astype(BF) for half in normed_first]
    packed = jnp.concatenate(packed, axis=0)
    position = jnp.arange(SLOTS * ROWS)
    slot, local = position // ROWS, position % ROWS
    owner_y, owner_c = (y + slot % NY) % NY, c ^ (slot // NY)
    last = (owner_y == (2 * r + 3) % NY) & (owner_c == 1)
    mask = local < jnp.where(last, HALF - (8 * HALF - SEQ), HALF)
    mask = mask.astype(F32)[None]
    last_grad = (upstream * scales[1]).astype(BF)
    last_full = gather(after(last_grad, normed_first[0]))
    mixture = attend(after(packed, fc1_other, last_full[0]), mask)
    half_rows = NY * ROWS
    mixture_halves = mixture[:half_rows], mixture[half_rows:]
    begun, sent = scatter_begin(mixture_halves, out_block, (1, 0))
    branch_first = scatter_end(begun, sent) + first_bias
    x = x + scales[0] * branch_first

    normed, scaled_second, inverse_second = norm(x, gains[1], shifts[1])
    normed_second = gather(after(normed, fc2_other, last_full[1]))
    active, hidden_grad = [], []
    for half, grad in zip(normed_second, last_full):
        hidden = dot(half, fc1_weight, (1, 0)) + unit_bias
        spread = 0.5 * (1.0 + lax.erf(hidden * (1.0 / math.sqrt(2.0))))
        active.append((hidden * spread).astype(BF))
        slope = jnp.exp(-0.5 * hidden * hidden) * (1.0 / math.sqrt(2.0 * math.pi))
        slope = spread + hidden * slope
        hidden_grad.append((dot(grad, fc2_weight, (1, 1)) * slope).astype(BF))
    begun, sent = scatter_begin(hidden_grad, fc1_weight, (1, 1))
    normed_grad = scatter_end(begun, sent)
    fc2_grad = sum(dot(one, two, (0, 0)) for one, two in zip(active, last_full))
    fc1_grad = sum(dot(one, two, (0, 0)) for one, two in zip(normed_second, hidden_grad))
    unit_grad = sum(jnp.sum(half.astype(F32), axis=0) for half in hidden_grad)
    fc2_sum = image_sum(fc2_grad[:, : D // 2], after(fc2_grad[:, D // 2 :].astype(BF), *sent))
    fc1_sum = image_sum(fc1_grad[: D // 2], after(fc1_grad[D // 2 :].astype(BF), fc2_sum))
    scale_second = jnp.sum(fc2_weight.astype(F32) * fc2_grad, axis=0) / scales[1]
    scale_second = scale_second + second_bias[0] * jnp.sum(upstream, axis=0)

    upstream = upstream + norm_pull(normed_grad, scaled_second, inverse_second, gains[1])
    first_grad = after((upstream * scales[0]).astype(BF), fc2_sum)
    vectors = [
        jnp.sum(normed_grad * scaled_second, axis=0),
        jnp.sum(normed_grad, axis=0),
        jnp.sum(upstream * branch_first, axis=0),
        scale_second,
    ]
    carried = jnp.concatenate([first_grad[:HALF], jnp.stack(vectors).astype(BF)], axis=0)
    carried = gather(jnp.pad(carried, ((0, spare - 4), (0, 0))))
    real = jnp.arange(NY * ROWS)[:, None] % ROWS < HALF
    first_full = [jnp.where(real, half, jnp.zeros((), BF)) for half in carried]
    spares = [half.reshape(NY, ROWS, D)[:, HALF : HALF + 4].astype(F32) for half in carried]
    vectors = sum(jnp.sum(half, axis=0) for half in spares)
    bias_first = sum(jnp.sum(half.astype(F32), axis=0, keepdims=True) for half in first_full)
    bias_second = sum(jnp.sum(half.astype(F32), axis=0, keepdims=True) for half in last_full)
    vectors = jnp.concatenate([vectors, bias_first, bias_second], axis=0)

    mixture_grad = [dot(half, out_block, (1, 1)).astype(BF) for half in first_full]
    fc_sum = jnp.concatenate([fc1_sum, fc2_sum], axis=0)
    mixture_grad = after(jnp.concatenate(mixture_grad, axis=0), fc_sum)
    out_grad = sum(dot(one, two, (0, 0)) for one, two in zip(first_full, mixture_halves))
    packed_grad = attend_pull(packed, mask, mixture_grad)
    packed_halves = packed_grad[:half_rows], packed_grad[half_rows:]
    begun, sent = scatter_begin(packed_halves, qkv_weight, (1, 1))
    arrived = [pull(piece, "y", -d) for d, piece in zip((1, 2, 3), sent)]
    normed_grad = begun + sum(piece.astype(F32) for piece in arrived)
    packed_grad = after(packed_grad, *sent)
    packed_halves = packed_grad[:half_rows], packed_grad[half_rows:]
    qkv_grad = sum(dot(one, two, (0, 0)) for one, two in zip(normed_first, packed_halves))
    totals = jnp.sum(packed_grad.astype(F32), axis=0)
    wide_weight = qkv_weight.astype(F32)
    shift_part = jnp.sum(wide_weight * totals, axis=1)
    product = jnp.sum(wide_weight * qkv_grad, axis=1)
    gain_part = (product - shifts[0] * shift_part) / gains[0]
    late = jnp.concatenate([qkv_grad, out_grad], axis=1)
    head_grad = totals.reshape(3, 2, HD)
    head_grad = jnp.stack([head_grad[0], head_grad[2]], axis=1).reshape(2, 128)
    head_own, head_other = pick(head_grad)
    unit_own, unit_other = pick(unit_grad.reshape(2, 256))
    zeros = jnp.zeros((128,), F32)
    own = jnp.concatenate([unit_own, head_own, zeros])[None]
    other = jnp.concatenate([unit_other, head_other, zeros])[None]
    late_own = jnp.concatenate([late[: D // 2], vectors[:, : D // 2], own], axis=0)
    late_other = jnp.concatenate([late[D // 2 :], vectors[:, D // 2 :], other], axis=0)
    late_other = late_other.astype(BF)
    late = image_sum(late_own, late_other)
    fc_sum = replica_gather(replica_scatter(after(fc_sum, arrived[0])))
    active = [after(half, late_other) for half in active]
    branch_second, pieces = scatter_begin(active, fc2_weight, (1, 0))
    normed_grad = after(normed_grad, *pieces)
    branch_second = scatter_end(branch_second, after(pieces, normed_grad)) + second_bias
    output = place_out(x + scales[1] * branch_second, home)
    final = column_sum(after(jnp.stack([gain_part, shift_part]), normed_grad))
    final = final[:, : D // 2] + swap(final[:, D // 2 :], "xh")
    late = jnp.concatenate([late, final, jnp.zeros((32 - 9, D // 2), F32)], axis=0)
    first_pull = norm_pull(normed_grad, scaled_first, inverse_first, gains[0])
    input_grad = place_out(upstream + first_pull, home)
    late = replica_gather(replica_scatter(after(late, fc_sum, branch_second, first_pull)))

    qkv_grad = late[: D // 2, :384].reshape(D // 2, 3, 2, HD).transpose(0, 2, 1, 3)
    out_grad = late[: D // 2, 384:].T
    vectors = late[D // 2 : D // 2 + 9]
    small = vectors[6]
    return (
        output,
        input_grad,
        qkv_grad.reshape(1, D // 2, 384),
        small[256:384].reshape(1, 1, 1, 1, -1),
        out_grad[None],
        fc_sum[None, : D // 2],
        small[:256].reshape(1, 1, 1, -1),
        fc_sum[None, D // 2 :],
        jnp.stack([vectors[7], vectors[0]])[None],
        jnp.stack([vectors[8], vectors[1]])[None],
        vectors[2:4][None],
        vectors[4:6][None],
    )


def solution(mesh):
    fine = Mesh(mesh.devices.reshape(NZ, 2, 2, NY, 2), ("z", "xl") + GROUP)
    tokens = P(("z", "xl", "y", "c"), "xh")
    tall = P(None, "xh", ("y", "c"))
    wide = P(None, ("y", "c"), "xh")
    head = P(None, ("y", "c"), "xh", None, None)
    unit = P(None, ("y", "c"), "xh", None)
    vector = P(None, None, "xh")
    return jax.shard_map(
        shards,
        mesh=fine,
        in_specs=(
            tokens,
            tall,
            head,
            wide,
            tall,
            unit,
            wide,
            vector,
            vector,
            vector,
            vector,
            tokens,
        ),
        out_specs=(
            tokens,
            tokens,
            tall,
            head,
            wide,
            tall,
            unit,
            wide,
            vector,
            vector,
            vector,
            vector,
        ),
        check_vma=False,
    )
```

profile of v0, /device:TPU:4, one launch (start us, length us, event | category | flops | bytes accessed | tf_op | source)
XLA Modules:
  0.0 355.3 jit_solution(16792660485977275345)
XLA Ops:
  4.8 7.6 %collective-permute-start.1 = (bf16[136,1024]{1,0:T(8,128)(2,1)S(1)}, bf16[136,1024]{1,0:T(8,128)(2,1)S(1)}, u32[]{:S(2)}, u32[]{:S(2)}) collective-permute-start(bf16[136,1024]{1,0:T(8,128)(2,1)S(1)} %get-tuple-element.126), channel_id=1, source_target_pairs={{4,8},{5,9},{6,10},{7,11},{8,4},{9,5},{10,6},{11,7},{20,24},{21,25... | collective-permute-start | bytes 835592 | tf_op jit(solution)/shard_map/ppermute | solution.py:69
  14.3 8.6 %collective-permute-done.1 = bf16[136,1024]{1,0:T(8,128)(2,1)S(1)} collective-permute-done((bf16[136,1024]{1,0:T(8,128)(2,1)S(1)}, bf16[136,1024]{1,0:T(8,128)(2,1)S(1)}, u32[]{:S(2)}, u32[]{:S(2)}) %collective-permute-start.1) | collective-permute-done | bytes 278560 | tf_op jit(solution)/shard_map/ppermute | solution.py:69
  26.7 2.7 collective-permute-start.3
  32.9 7.8 %collective-permute-done.4 = bf16[136,1024]{1,0:T(8,128)(2,1)S(1)} collective-permute-done((bf16[136,1024]{1,0:T(8,128)(2,1)S(1)}, bf16[136,1024]{1,0:T(8,128)(2,1)S(1)}, u32[]{:S(2)}, u32[]{:S(2)}) %collective-permute-start.4) | collective-permute-done | bytes 278560 | tf_op jit(solution)/shard_map/ppermute | solution.py:58
  43.7 2.7 collective-permute-start.8
  50.7 3.3 collective-permute-start.7
  56.9 2.4 collective-permute-done.8
  66.8 4.7 %shard_map.211 = bf16[1088,128]{1,0:T(8,128)(2,1)S(1)} custom-call(f32[1,1088]{1,0:T(1,128)S(1)} %compare_convert_fusion.mask_ref, bf16[1088,384]{1,0:T(8,128)(2,1)S(1)} %pad_maximum_fusion.6.packed_ref), custom_call_target="tpu_custom_call" | custom-call | flops 8000000000 | bytes 24000000 | tf_op jit(solution)/shard_map/pallas_call | solution.py:200
  72.0 2.7 collective-permute-done.11
  75.3 2.3 collective-permute-start.14
  79.2 3.2 collective-permute-start.15
  82.4 7.5 %collective-permute-done.14 = bf16[136,1024]{1,0:T(8,128)(2,1)S(1)} collective-permute-done((bf16[136,1024]{1,0:T(8,128)(2,1)S(1)}, bf16[136,1024]{1,0:T(8,128)(2,1)S(1)}, u32[]{:S(2)}, u32[]{:S(2)}) %collective-permute-start.14) | collective-permute-done | bytes 278560 | tf_op jit(solution)/shard_map/ppermute | solution.py:58
  89.9 3.7 %collective-permute-done.12 = bf16[136,1024]{1,0:T(8,128)(2,1)S(1)} collective-permute-done((bf16[136,1024]{1,0:T(8,128)(2,1)S(1)}, bf16[136,1024]{1,0:T(8,128)(2,1)S(1)}, u32[]{:S(2)}, u32[]{:S(2)}) %collective-permute-start.12) | collective-permute-done | bytes 278560 | tf_op jit(solution)/shard_map/ppermute | solution.py:58
  96.2 2.8 collective-permute-start.17
  103.2 7.9 %collective-permute-done.17 = bf16[136,1024]{1,0:T(8,128)(2,1)} collective-permute-done((bf16[136,1024]{1,0:T(8,128)(2,1)}, bf16[136,1024]{1,0:T(8,128)(2,1)}, u32[]{:S(2)}, u32[]{:S(2)}) %collective-permute-start.17) | collective-permute-done | bytes 278560 | tf_op jit(solution)/shard_map/ppermute | solution.py:58
  132.8 2.2 collective-permute-start.24
  136.0 2.3 fusion.89
  138.3 3.1 collective-permute-start.25
  141.5 5.7 %collective-permute-done.24 = bf16[136,1024]{1,0:T(8,128)(2,1)S(1)} collective-permute-done((bf16[136,1024]{1,0:T(8,128)(2,1)S(1)}, bf16[136,1024]{1,0:T(8,128)(2,1)S(1)}, u32[]{:S(2)}, u32[]{:S(2)}) %collective-permute-start.24) | collective-permute-done | bytes 278560 | tf_op jit(solution)/shard_map/ppermute | solution.py:58
  147.2 3.4 collective-permute-done.22
  161.7 3.0 convolution_add_fusion
  164.8 3.2 collective-permute-start.30
  168.1 5.2 %collective-permute-done.28 = bf16[136,1024]{1,0:T(8,128)(2,1)S(1)} collective-permute-done((bf16[136,1024]{1,0:T(8,128)(2,1)S(1)}, bf16[136,1024]{1,0:T(8,128)(2,1)S(1)}, u32[]{:S(2)}, u32[]{:S(2)}) %collective-permute-start.28) | collective-permute-done | bytes 278560 | tf_op jit(solution)/shard_map/ppermute | solution.py:58
  174.9 3.9 %collective-permute-done.30 = bf16[512,512]{1,0:T(8,128)(2,1)S(1)} collective-permute-done((bf16[512,512]{1,0:T(8,128)(2,1)S(1)}, bf16[512,512]{1,0:T(8,128)(2,1)S(1)}, u32[]{:S(2)}, u32[]{:S(2)}) %collective-permute-start.30) | collective-permute-done | bytes 524320 | tf_op jit(solution)/shard_map/ppermute | solution.py:54
  181.0 12.2 %shard_map.212 = bf16[1088,384]{1,0:T(8,128)(2,1)S(1)} custom-call(f32[1,1088]{1,0:T(1,128)S(1)} %compare_convert_fusion.mask_ref, bf16[1088,384]{1,0:T(8,128)(2,1)S(1)} %pad_maximum_fusion.6.packed_ref, bf16[1088,128]{1,0:T(8,128)(2,1)S(1)} %pad_maximum_fusion.14.grad_ref), custom_call_target="tpu_custom_call" | custom-call | flops 12000000000 | bytes 36000000 | tf_op jit(solution)/shard_map/pallas_call | solution.py:200
  199.8 3.4 fusion.86
  217.5 4.1 %collective-permute-done.33 = bf16[136,1024]{1,0:T(8,128)(2,1)} collective-permute-done((bf16[136,1024]{1,0:T(8,128)(2,1)}, bf16[136,1024]{1,0:T(8,128)(2,1)}, u32[]{:S(2)}, u32[]{:S(2)}) %collective-permute-start.33) | collective-permute-done | bytes 278560 | tf_op jit(solution)/shard_map/ppermute | solution.py:58
  223.1 4.1 %collective-permute-start.58 = (bf16[256,512]{1,0:T(8,128)(2,1)S(1)}, bf16[256,512]{1,0:T(8,128)(2,1)S(1)}, u32[]{:S(2)}, u32[]{:S(2)}) collective-permute-start(bf16[256,512]{1,0:T(8,128)(2,1)S(1)} %get-tuple-element.128), channel_id=1, source_target_pairs={{32,0},{64,32},{96,64},{0,96},{33,1},{65,33},{97,65},{1,97},{34,2}... | collective-permute-start | bytes 786440 | tf_op jit(solution)/shard_map/ppermute | solution.py:58
  229.8 8.8 %collective-permute-done.58 = bf16[256,512]{1,0:T(8,128)(2,1)S(1)} collective-permute-done((bf16[256,512]{1,0:T(8,128)(2,1)S(1)}, bf16[256,512]{1,0:T(8,128)(2,1)S(1)}, u32[]{:S(2)}, u32[]{:S(2)}) %collective-permute-start.58) | collective-permute-done | bytes 262176 | tf_op jit(solution)/shard_map/ppermute | solution.py:58
  238.6 3.1 collective-permute-start.43
  245.7 2.2 slice_add_fusion.2
  248.0 7.5 %collective-permute-done.43 = bf16[519,512]{1,0:T(8,128)(2,1)} collective-permute-done((bf16[519,512]{1,0:T(8,128)(2,1)}, bf16[519,512]{1,0:T(8,128)(2,1)}, u32[]{:S(2)}, u32[]{:S(2)}) %collective-permute-start.43) | collective-permute-done | bytes 531488 | tf_op jit(solution)/shard_map/ppermute | solution.py:54
  256.8 3.1 collective-permute-done.59
  261.1 4.7 %collective-permute-start.62 = (bf16[256,512]{1,0:T(8,128)(2,1)S(1)}, bf16[256,512]{1,0:T(8,128)(2,1)S(1)}, u32[]{:S(2)}, u32[]{:S(2)}) collective-permute-start(bf16[256,512]{1,0:T(8,128)(2,1)S(1)} %add_convert_fusion.2), channel_id=1, source_target_pairs={{96,0},{0,32},{32,64},{64,96},{97,1},{1,33},{33,65},{65,97},{98,2}... | collective-permute-start | bytes 786440 | tf_op jit(solution)/shard_map/ppermute | solution.py:58
  266.0 2.4 fusion.4
  268.4 3.3 collective-permute-done.61
  271.7 2.8 collective-permute-done.62
  278.7 3.4 fusion.87
  286.1 3.7 %collective-permute-start.46 = (f32[2,1024]{1,0:T(2,128)S(1)}, f32[2,1024]{1,0:T(2,128)S(1)}, u32[]{:S(2)}, u32[]{:S(2)}) collective-permute-start(f32[2,1024]{1,0:T(2,128)S(1)} %add.477), channel_id=1, source_target_pairs={{2,0},{4,2},{6,4},{0,6},{3,1},{5,3},{7,5},{1,7},{10,8},{12,10},{14... | collective-permute-start | bytes 24584 | tf_op jit(solution)/shard_map/ppermute | solution.py:58
  291.6 5.9 %collective-permute-done.46 = f32[2,1024]{1,0:T(2,128)S(1)} collective-permute-done((f32[2,1024]{1,0:T(2,128)S(1)}, f32[2,1024]{1,0:T(2,128)S(1)}, u32[]{:S(2)}, u32[]{:S(2)}) %collective-permute-start.46) | collective-permute-done | bytes 8224 | tf_op jit(solution)/shard_map/ppermute | solution.py:58
  298.4 4.4 %collective-permute-done.48 = f32[2,512]{1,0:T(2,128)S(1)} collective-permute-done((f32[2,512]{1,0:T(2,128)S(1)}, f32[2,512]{1,0:T(2,128)S(1)}, u32[]{:S(2)}, u32[]{:S(2)}) %collective-permute-start.48) | collective-permute-done | bytes 4128 | tf_op jit(solution)/shard_map/ppermute | solution.py:54
  302.8 3.4 collective-permute-start.42
  309.2 3.8 %collective-permute-start.51 = (bf16[136,512]{0,1:T(8,128)(2,1)S(1)}, bf16[136,512]{0,1:T(8,128)(2,1)S(1)}, u32[]{:S(2)}, u32[]{:S(2)}) collective-permute-start(bf16[136,512]{0,1:T(8,128)(2,1)S(1)} %get-tuple-element.131), channel_id=1, source_target_pairs={{32,0},{64,32},{96,64},{0,96},{33,1},{65,33},{97,65},{1,97},{34,2}... | collective-permute-start | bytes 417800 | tf_op jit(solution)/shard_map/ppermute | solution.py:58
  315.7 6.2 %collective-permute-done.51 = bf16[136,512]{0,1:T(8,128)(2,1)S(1)} collective-permute-done((bf16[136,512]{0,1:T(8,128)(2,1)S(1)}, bf16[136,512]{0,1:T(8,128)(2,1)S(1)}, u32[]{:S(2)}, u32[]{:S(2)}) %collective-permute-start.51) | collective-permute-done | bytes 139296 | tf_op jit(solution)/shard_map/ppermute | solution.py:58
  322.9 2.4 collective-permute-done.49
  326.6 6.1 %collective-permute-start.40 = (bf16[129,512]{1,0:T(8,128)(2,1)S(1)}, bf16[129,512]{1,0:T(8,128)(2,1)S(1)}, u32[]{:S(2)}, u32[]{:S(2)}) collective-permute-start(bf16[129,512]{1,0:T(8,128)(2,1)S(1)} %get-tuple-element.117), channel_id=1, source_target_pairs={{8,4},{9,5},{10,6},{11,7},{4,8},{5,9},{6,10},{7,11},{24,20},{25,21... | collective-permute-start | bytes 396296 | tf_op jit(solution)/shard_map/ppermute | solution.py:76
  338.6 5.5 %collective-permute-done.54 = bf16[136,512]{0,1:T(8,128)(2,1)S(1)} collective-permute-done((bf16[136,512]{0,1:T(8,128)(2,1)S(1)}, bf16[136,512]{0,1:T(8,128)(2,1)S(1)}, u32[]{:S(2)}, u32[]{:S(2)}) %collective-permute-start.54) | collective-permute-done | bytes 139296 | tf_op jit(solution)/shard_map/ppermute | solution.py:58
  344.0 2.7 collective-permute-done.55
  (477 shorter events, 140.8 us)
Async XLA Ops:
  4.8 18.1 %collective-permute-start.1 = (bf16[136,1024]{1,0:T(8,128)(2,1)S(1)}, bf16[136,1024]{1,0:T(8,128)(2,1)S(1)}, u32[]{:S(2)}, u32[]{:S(2)}) collective-permute-start(bf16[136,1024]{1,0:T(8,128)(2,1)S(1)} %get-tuple-element.126), channel_id=1, source_target_pairs={{4,8},{5,9},{6,10},{7,11},{8,4},{9,5},{10,6},{11,7},{20,24},{21,25... | collective-permute-start | bytes 835592 | tf_op jit(solution)/shard_map/ppermute | solution.py:69
  25.6 22.8 %collective-permute-start.5 = (bf16[528,512]{1,0:T(8,128)(2,1)S(1)}, bf16[528,512]{1,0:T(8,128)(2,1)S(1)}, u32[]{:S(2)}, u32[]{:S(2)}) collective-permute-start(bf16[528,512]{1,0:T(8,128)(2,1)S(1)} %fusion.33), channel_id=1, source_target_pairs={{0,8},{8,0},{1,9},{9,1},{2,10},{10,2},{3,11},{11,3},{4,12},{12,4},... | collective-permute-start | bytes 1622024 | tf_op jit(solution)/shard_map/ppermute | solution.py:54
  26.0 14.8 %collective-permute-start.4 = (bf16[136,1024]{1,0:T(8,128)(2,1)S(1)}, bf16[136,1024]{1,0:T(8,128)(2,1)S(1)}, u32[]{:S(2)}, u32[]{:S(2)}) collective-permute-start(bf16[136,1024]{1,0:T(8,128)(2,1)S(1)} %add_convert_fusion.1), channel_id=1, source_target_pairs={{6,0},{0,2},{2,4},{4,6},{7,1},{1,3},{3,5},{5,7},{14,8},{8,10},{10,... | collective-permute-start | bytes 835592 | tf_op jit(solution)/shard_map/ppermute | solution.py:58
  26.7 14.0 %collective-permute-start.3 = (bf16[136,1024]{1,0:T(8,128)(2,1)S(1)}, bf16[136,1024]{1,0:T(8,128)(2,1)}, u32[]{:S(2)}, u32[]{:S(2)}) collective-permute-start(bf16[136,1024]{1,0:T(8,128)(2,1)S(1)} %add_convert_fusion.1), channel_id=1, source_target_pairs={{4,0},{6,2},{0,4},{2,6},{5,1},{7,3},{1,5},{3,7},{12,8},{14,10},{8,... | collective-permute-start | bytes 835592 | tf_op jit(solution)/shard_map/ppermute | solution.py:58
  29.4 12.0 %collective-permute-start.2 = (bf16[136,1024]{1,0:T(8,128)(2,1)S(1)}, bf16[136,1024]{1,0:T(8,128)(2,1)}, u32[]{:S(2)}, u32[]{:S(2)}) collective-permute-start(bf16[136,1024]{1,0:T(8,128)(2,1)S(1)} %add_convert_fusion.1), channel_id=1, source_target_pairs={{2,0},{4,2},{6,4},{0,6},{3,1},{5,3},{7,5},{1,7},{10,8},{12,10},{14... | collective-permute-start | bytes 835592 | tf_op jit(solution)/shard_map/ppermute | solution.py:58
  43.7 19.9 %collective-permute-start.6 = (bf16[544,1024]{1,0:T(8,128)(2,1)}, bf16[544,1024]{1,0:T(8,128)(2,1)}, u32[]{:S(2)}, u32[]{:S(2)}) collective-permute-start(bf16[544,1024]{1,0:T(8,128)(2,1)} %pad_maximum_fusion.2), channel_id=1, source_target_pairs={{0,1},{1,0},{2,3},{3,2},{4,5},{5,4},{6,7},{7,6},{8,9},{9,8},{10,11... | collective-permute-start | bytes 3342344 | tf_op jit(solution)/shard_map/ppermute | solution.py:54
  43.7 15.5 %collective-permute-start.8 = (bf16[136,1024]{1,0:T(8,128)(2,1)}, bf16[136,1024]{1,0:T(8,128)(2,1)}, u32[]{:S(2)}, u32[]{:S(2)}) collective-permute-start(bf16[136,1024]{1,0:T(8,128)(2,1)} %get-tuple-element.34), channel_id=1, source_target_pairs={{2,0},{4,2},{6,4},{0,6},{3,1},{5,3},{7,5},{1,7},{10,8},{12,10},{14... | collective-permute-start | bytes 835592 | tf_op jit(solution)/shard_map/ppermute | solution.py:58
  46.4 13.8 %collective-permute-start.9 = (bf16[136,1024]{1,0:T(8,128)(2,1)}, bf16[136,1024]{1,0:T(8,128)(2,1)}, u32[]{:S(2)}, u32[]{:S(2)}) collective-permute-start(bf16[136,1024]{1,0:T(8,128)(2,1)} %get-tuple-element.34), channel_id=1, source_target_pairs={{4,0},{6,2},{0,4},{2,6},{5,1},{7,3},{1,5},{3,7},{12,8},{14,10},{8,... | collective-permute-start | bytes 835592 | tf_op jit(solution)/shard_map/ppermute | solution.py:58
  46.7 15.9 %collective-permute-start.10 = (bf16[136,1024]{1,0:T(8,128)(2,1)}, bf16[136,1024]{1,0:T(8,128)(2,1)}, u32[]{:S(2)}, u32[]{:S(2)}) collective-permute-start(bf16[136,1024]{1,0:T(8,128)(2,1)} %get-tuple-element.34), channel_id=1, source_target_pairs={{6,0},{0,2},{2,4},{4,6},{7,1},{1,3},{3,5},{5,7},{14,8},{8,10},{10,... | collective-permute-start | bytes 835592 | tf_op jit(solution)/shard_map/ppermute | solution.py:58
  50.7 16.1 %collective-permute-start.7 = (bf16[512,512]{1,0:T(8,128)(2,1)S(1)}, bf16[512,512]{1,0:T(8,128)(2,1)}, u32[]{:S(2)}, u32[]{:S(2)}) collective-permute-start(bf16[512,512]{1,0:T(8,128)(2,1)S(1)} %bitcast.124), channel_id=1, source_target_pairs={{0,8},{8,0},{1,9},{9,1},{2,10},{10,2},{3,11},{11,3},{4,12},{12,4},... | collective-permute-start | bytes 1572872 | tf_op jit(solution)/shard_map/ppermute | solution.py:54
  75.3 14.5 %collective-permute-start.14 = (bf16[136,1024]{1,0:T(8,128)(2,1)S(1)}, bf16[136,1024]{1,0:T(8,128)(2,1)S(1)}, u32[]{:S(2)}, u32[]{:S(2)}) collective-permute-start(bf16[136,1024]{1,0:T(8,128)(2,1)S(1)} %get-tuple-element.143), channel_id=1, source_target_pairs={{2,0},{4,2},{6,4},{0,6},{3,1},{5,3},{7,5},{1,7},{10,8},{12,10},{14... | collective-permute-start | bytes 835592 | tf_op jit(solution)/shard_map/ppermute | solution.py:58
  77.7 12.2 %collective-permute-start.13 = (bf16[136,1024]{1,0:T(8,128)(2,1)S(1)}, bf16[136,1024]{1,0:T(8,128)(2,1)S(1)}, u32[]{:S(2)}, u32[]{:S(2)}) collective-permute-start(bf16[136,1024]{1,0:T(8,128)(2,1)S(1)} %get-tuple-element.144), channel_id=1, source_target_pairs={{4,0},{6,2},{0,4},{2,6},{5,1},{7,3},{1,5},{3,7},{12,8},{14,10},{8,... | collective-permute-start | bytes 835592 | tf_op jit(solution)/shard_map/ppermute | solution.py:58
  79.2 14.4 %collective-permute-start.12 = (bf16[136,1024]{1,0:T(8,128)(2,1)S(1)}, bf16[136,1024]{1,0:T(8,128)(2,1)S(1)}, u32[]{:S(2)}, u32[]{:S(2)}) collective-permute-start(bf16[136,1024]{1,0:T(8,128)(2,1)S(1)} %get-tuple-element.142), channel_id=1, source_target_pairs={{6,0},{0,2},{2,4},{4,6},{7,1},{1,3},{3,5},{5,7},{14,8},{8,10},{10,... | collective-permute-start | bytes 835592 | tf_op jit(solution)/shard_map/ppermute | solution.py:58
  79.2 16.3 %collective-permute-start.16 = (bf16[544,1024]{1,0:T(8,128)(2,1)S(1)}, bf16[544,1024]{1,0:T(8,128)(2,1)S(1)}, u32[]{:S(2)}, u32[]{:S(2)}) collective-permute-start(bf16[544,1024]{1,0:T(8,128)(2,1)S(1)} %copy-done.5), channel_id=1, source_target_pairs={{0,1},{1,0},{2,3},{3,2},{4,5},{5,4},{6,7},{7,6},{8,9},{9,8},{10,11... | collective-permute-start | bytes 3342344 | tf_op jit(solution)/shard_map/ppermute | solution.py:54
  79.2 16.2 %collective-permute-start.15 = (bf16[512,512]{1,0:T(8,128)(2,1)S(1)}, bf16[512,512]{1,0:T(8,128)(2,1)S(1)}, u32[]{:S(2)}, u32[]{:S(2)}) collective-permute-start(bf16[512,512]{1,0:T(8,128)(2,1)S(1)} %bitcast.106), channel_id=1, source_target_pairs={{0,8},{8,0},{1,9},{9,1},{2,10},{10,2},{3,11},{11,3},{4,12},{12,4},... | collective-permute-start | bytes 1572872 | tf_op jit(solution)/shard_map/ppermute | solution.py:54
  96.2 14.9 %collective-permute-start.17 = (bf16[136,1024]{1,0:T(8,128)(2,1)}, bf16[136,1024]{1,0:T(8,128)(2,1)}, u32[]{:S(2)}, u32[]{:S(2)}) collective-permute-start(bf16[136,1024]{1,0:T(8,128)(2,1)} %add_convert_fusion), channel_id=1, source_target_pairs={{2,0},{4,2},{6,4},{0,6},{3,1},{5,3},{7,5},{1,7},{10,8},{12,10},{14... | collective-permute-start | bytes 835592 | tf_op jit(solution)/shard_map/ppermute | solution.py:58
  99.1 13.0 %collective-permute-start.18 = (bf16[136,1024]{1,0:T(8,128)(2,1)}, bf16[136,1024]{1,0:T(8,128)(2,1)}, u32[]{:S(2)}, u32[]{:S(2)}) collective-permute-start(bf16[136,1024]{1,0:T(8,128)(2,1)} %add_convert_fusion), channel_id=1, source_target_pairs={{4,0},{6,2},{0,4},{2,6},{5,1},{7,3},{1,5},{3,7},{12,8},{14,10},{8,... | collective-permute-start | bytes 835592 | tf_op jit(solution)/shard_map/ppermute | solution.py:58
  101.1 13.5 %collective-permute-start.19 = (bf16[136,1024]{1,0:T(8,128)(2,1)}, bf16[136,1024]{1,0:T(8,128)(2,1)S(1)}, u32[]{:S(2)}, u32[]{:S(2)}) collective-permute-start(bf16[136,1024]{1,0:T(8,128)(2,1)} %add_convert_fusion), channel_id=1, source_target_pairs={{6,0},{0,2},{2,4},{4,6},{7,1},{1,3},{3,5},{5,7},{14,8},{8,10},{10,... | collective-permute-start | bytes 835592 | tf_op jit(solution)/shard_map/ppermute | solution.py:58
  132.8 14.3 %collective-permute-start.24 = (bf16[136,1024]{1,0:T(8,128)(2,1)S(1)}, bf16[136,1024]{1,0:T(8,128)(2,1)S(1)}, u32[]{:S(2)}, u32[]{:S(2)}) collective-permute-start(bf16[136,1024]{1,0:T(8,128)(2,1)S(1)} %get-tuple-element.140), channel_id=1, source_target_pairs={{2,0},{4,2},{6,4},{0,6},{3,1},{5,3},{7,5},{1,7},{10,8},{12,10},{14... | collective-permute-start | bytes 835592 | tf_op jit(solution)/shard_map/ppermute | solution.py:58
  135.1 12.1 %collective-permute-start.23 = (bf16[136,1024]{1,0:T(8,128)(2,1)S(1)}, bf16[136,1024]{1,0:T(8,128)(2,1)S(1)}, u32[]{:S(2)}, u32[]{:S(2)}) collective-permute-start(bf16[136,1024]{1,0:T(8,128)(2,1)S(1)} %get-tuple-element.141), channel_id=1, source_target_pairs={{4,0},{6,2},{0,4},{2,6},{5,1},{7,3},{1,5},{3,7},{12,8},{14,10},{8,... | collective-permute-start | bytes 835592 | tf_op jit(solution)/shard_map/ppermute | solution.py:58
  135.1 15.5 %collective-permute-start.22 = (bf16[136,1024]{1,0:T(8,128)(2,1)S(1)}, bf16[136,1024]{1,0:T(8,128)(2,1)S(1)}, u32[]{:S(2)}, u32[]{:S(2)}) collective-permute-start(bf16[136,1024]{1,0:T(8,128)(2,1)S(1)} %get-tuple-element.139), channel_id=1, source_target_pairs={{6,0},{0,2},{2,4},{4,6},{7,1},{1,3},{3,5},{5,7},{14,8},{8,10},{10,... | collective-permute-start | bytes 835592 | tf_op jit(solution)/shard_map/ppermute | solution.py:58
  138.3 16.3 %collective-permute-start.25 = (bf16[512,512]{1,0:T(8,128)(2,1)S(1)}, bf16[512,512]{1,0:T(8,128)(2,1)S(1)}, u32[]{:S(2)}, u32[]{:S(2)}) collective-permute-start(bf16[512,512]{1,0:T(8,128)(2,1)S(1)} %slice.551), channel_id=1, source_target_pairs={{0,8},{8,0},{1,9},{9,1},{2,10},{10,2},{3,11},{11,3},{4,12},{12,4},... | collective-permute-start | bytes 1572872 | tf_op jit(solution)/shard_map/ppermute | solution.py:54
  157.8 15.5 %collective-permute-start.28 = (bf16[136,1024]{1,0:T(8,128)(2,1)S(1)}, bf16[136,1024]{1,0:T(8,128)(2,1)S(1)}, u32[]{:S(2)}, u32[]{:S(2)}) collective-permute-start(bf16[136,1024]{1,0:T(8,128)(2,1)S(1)} %pad.14), channel_id=1, source_target_pairs={{6,0},{0,2},{2,4},{4,6},{7,1},{1,3},{3,5},{5,7},{14,8},{8,10},{10,... | collective-permute-start | bytes 835592 | tf_op jit(solution)/shard_map/ppermute | solution.py:58
  158.6 14.7 %collective-permute-start.27 = (bf16[136,1024]{1,0:T(8,128)(2,1)S(1)}, bf16[136,1024]{1,0:T(8,128)(2,1)S(1)}, u32[]{:S(2)}, u32[]{:S(2)}) collective-permute-start(bf16[136,1024]{1,0:T(8,128)(2,1)S(1)} %pad.14), channel_id=1, source_target_pairs={{4,0},{6,2},{0,4},{2,6},{5,1},{7,3},{1,5},{3,7},{12,8},{14,10},{8,... | collective-permute-start | bytes 835592 | tf_op jit(solution)/shard_map/ppermute | solution.py:58
  160.2 13.7 %collective-permute-start.26 = (bf16[136,1024]{1,0:T(8,128)(2,1)S(1)}, bf16[136,1024]{1,0:T(8,128)(2,1)S(1)}, u32[]{:S(2)}, u32[]{:S(2)}) collective-permute-start(bf16[136,1024]{1,0:T(8,128)(2,1)S(1)} %pad.14), channel_id=1, source_target_pairs={{2,0},{4,2},{6,4},{0,6},{3,1},{5,3},{7,5},{1,7},{10,8},{12,10},{14... | collective-permute-start | bytes 835592 | tf_op jit(solution)/shard_map/ppermute | solution.py:58
  164.8 13.9 %collective-permute-start.30 = (bf16[512,512]{1,0:T(8,128)(2,1)S(1)}, bf16[512,512]{1,0:T(8,128)(2,1)S(1)}, u32[]{:S(2)}, u32[]{:S(2)}) collective-permute-start(bf16[512,512]{1,0:T(8,128)(2,1)S(1)} %slice.550), channel_id=1, source_target_pairs={{0,8},{8,0},{1,9},{9,1},{2,10},{10,2},{3,11},{11,3},{4,12},{12,4},... | collective-permute-start | bytes 1572872 | tf_op jit(solution)/shard_map/ppermute | solution.py:54
  204.1 41.6 %collective-permute-start.35 = (bf16[136,1024]{1,0:T(8,128)(2,1)}, bf16[136,1024]{1,0:T(8,128)(2,1)}, u32[]{:S(2)}, u32[]{:S(2)}) collective-permute-start(bf16[136,1024]{1,0:T(8,128)(2,1)} %get-tuple-element.136), channel_id=1, source_target_pairs={{2,0},{4,2},{6,4},{0,6},{3,1},{5,3},{7,5},{1,7},{10,8},{12,10},{14... | collective-permute-start | bytes 835592 | tf_op jit(solution)/shard_map/ppermute | solution.py:58
  205.1 40.6 %collective-permute-start.34 = (bf16[136,1024]{1,0:T(8,128)(2,1)}, bf16[136,1024]{1,0:T(8,128)(2,1)}, u32[]{:S(2)}, u32[]{:S(2)}) collective-permute-start(bf16[136,1024]{1,0:T(8,128)(2,1)} %get-tuple-element.137), channel_id=1, source_target_pairs={{4,0},{6,2},{0,4},{2,6},{5,1},{7,3},{1,5},{3,7},{12,8},{14,10},{8,... | collective-permute-start | bytes 835592 | tf_op jit(solution)/shard_map/ppermute | solution.py:58
  207.1 14.6 %collective-permute-start.33 = (bf16[136,1024]{1,0:T(8,128)(2,1)}, bf16[136,1024]{1,0:T(8,128)(2,1)}, u32[]{:S(2)}, u32[]{:S(2)}) collective-permute-start(bf16[136,1024]{1,0:T(8,128)(2,1)} %get-tuple-element.138), channel_id=1, source_target_pairs={{6,0},{0,2},{2,4},{4,6},{7,1},{1,3},{3,5},{5,7},{14,8},{8,10},{10,... | collective-permute-start | bytes 835592 | tf_op jit(solution)/shard_map/ppermute | solution.py:58
  223.1 15.5 %collective-permute-start.58 = (bf16[256,512]{1,0:T(8,128)(2,1)S(1)}, bf16[256,512]{1,0:T(8,128)(2,1)S(1)}, u32[]{:S(2)}, u32[]{:S(2)}) collective-permute-start(bf16[256,512]{1,0:T(8,128)(2,1)S(1)} %get-tuple-element.128), channel_id=1, source_target_pairs={{32,0},{64,32},{96,64},{0,96},{33,1},{65,33},{97,65},{1,97},{34,2}... | collective-permute-start | bytes 786440 | tf_op jit(solution)/shard_map/ppermute | solution.py:58
  227.3 15.3 %collective-permute-start.57 = (bf16[256,512]{1,0:T(8,128)(2,1)S(1)}, bf16[256,512]{1,0:T(8,128)(2,1)S(1)}, u32[]{:S(2)}, u32[]{:S(2)}) collective-permute-start(bf16[256,512]{1,0:T(8,128)(2,1)S(1)} %get-tuple-element.129), channel_id=1, source_target_pairs={{64,0},{96,32},{0,64},{32,96},{65,1},{97,33},{1,65},{33,97},{66,2}... | collective-permute-start | bytes 786440 | tf_op jit(solution)/shard_map/ppermute | solution.py:58
  227.4 15.3 %collective-permute-start.56 = (bf16[256,512]{1,0:T(8,128)(2,1)S(1)}, bf16[256,512]{1,0:T(8,128)(2,1)S(1)}, u32[]{:S(2)}, u32[]{:S(2)}) collective-permute-start(bf16[256,512]{1,0:T(8,128)(2,1)S(1)} %get-tuple-element.127), channel_id=1, source_target_pairs={{96,0},{0,32},{32,64},{64,96},{97,1},{1,33},{33,65},{65,97},{98,2}... | collective-permute-start | bytes 786440 | tf_op jit(solution)/shard_map/ppermute | solution.py:58
  238.6 16.9 %collective-permute-start.43 = (bf16[519,512]{1,0:T(8,128)(2,1)}, bf16[519,512]{1,0:T(8,128)(2,1)}, u32[]{:S(2)}, u32[]{:S(2)}) collective-permute-start(bf16[519,512]{1,0:T(8,128)(2,1)} %copy.77), channel_id=1, source_target_pairs={{0,8},{8,0},{1,9},{9,1},{2,10},{10,2},{3,11},{11,3},{4,12},{12,4},... | collective-permute-start | bytes 1594376 | tf_op jit(solution)/shard_map/ppermute | solution.py:54
  242.6 35.6 %collective-permute-start.32 = (bf16[544,1024]{1,0:T(8,128)(2,1)}, bf16[544,1024]{1,0:T(8,128)(2,1)}, u32[]{:S(2)}, u32[]{:S(2)}) collective-permute-start(bf16[544,1024]{1,0:T(8,128)(2,1)} %convolution_convert_fusion), channel_id=1, source_target_pairs={{0,1},{1,0},{2,3},{3,2},{4,5},{5,4},{6,7},{7,6},{8,9},{9,8},{10,11... | collective-permute-start | bytes 3342344 | tf_op jit(solution)/shard_map/ppermute | solution.py:54
  244.5 15.4 %collective-permute-start.59 = (bf16[256,512]{1,0:T(8,128)(2,1)}, bf16[256,512]{1,0:T(8,128)(2,1)}, u32[]{:S(2)}, u32[]{:S(2)}) collective-permute-start(bf16[256,512]{1,0:T(8,128)(2,1)} %add_convert_fusion.3), channel_id=1, source_target_pairs={{0,16},{16,0},{1,17},{17,1},{2,18},{18,2},{3,19},{19,3},{4,20},{20... | collective-permute-start | bytes 786440 | tf_op jit(solution)/shard_map/ppermute | solution.py:54
  261.0 10.8 %collective-permute-start.61 = (bf16[256,512]{1,0:T(8,128)(2,1)S(1)}, bf16[256,512]{1,0:T(8,128)(2,1)S(1)}, u32[]{:S(2)}, u32[]{:S(2)}) collective-permute-start(bf16[256,512]{1,0:T(8,128)(2,1)S(1)} %add_convert_fusion.2), channel_id=1, source_target_pairs={{64,0},{96,32},{0,64},{32,96},{65,1},{97,33},{1,65},{33,97},{66,2}... | collective-permute-start | bytes 786440 | tf_op jit(solution)/shard_map/ppermute | solution.py:58
  261.1 13.4 %collective-permute-start.62 = (bf16[256,512]{1,0:T(8,128)(2,1)S(1)}, bf16[256,512]{1,0:T(8,128)(2,1)S(1)}, u32[]{:S(2)}, u32[]{:S(2)}) collective-permute-start(bf16[256,512]{1,0:T(8,128)(2,1)S(1)} %add_convert_fusion.2), channel_id=1, source_target_pairs={{96,0},{0,32},{32,64},{64,96},{97,1},{1,33},{33,65},{65,97},{98,2}... | collective-permute-start | bytes 786440 | tf_op jit(solution)/shard_map/ppermute | solution.py:58
  283.8 22.8 %collective-permute-start.38 = (bf16[136,1024]{1,0:T(8,128)(2,1)}, bf16[136,1024]{1,0:T(8,128)(2,1)}, u32[]{:S(2)}, u32[]{:S(2)}) collective-permute-start(bf16[136,1024]{1,0:T(8,128)(2,1)} %get-tuple-element.48), channel_id=1, source_target_pairs={{2,0},{4,2},{6,4},{0,6},{3,1},{5,3},{7,5},{1,7},{10,8},{12,10},{14... | collective-permute-start | bytes 835592 | tf_op jit(solution)/shard_map/ppermute | solution.py:58
  283.9 22.7 %collective-permute-start.37 = (bf16[136,1024]{1,0:T(8,128)(2,1)}, bf16[136,1024]{1,0:T(8,128)(2,1)}, u32[]{:S(2)}, u32[]{:S(2)}) collective-permute-start(bf16[136,1024]{1,0:T(8,128)(2,1)} %get-tuple-element.47), channel_id=1, source_target_pairs={{4,0},{6,2},{0,4},{2,6},{5,1},{7,3},{1,5},{3,7},{12,8},{14,10},{8,... | collective-permute-start | bytes 835592 | tf_op jit(solution)/shard_map/ppermute | solution.py:58
  286.1 11.5 %collective-permute-start.46 = (f32[2,1024]{1,0:T(2,128)S(1)}, f32[2,1024]{1,0:T(2,128)S(1)}, u32[]{:S(2)}, u32[]{:S(2)}) collective-permute-start(f32[2,1024]{1,0:T(2,128)S(1)} %add.477), channel_id=1, source_target_pairs={{2,0},{4,2},{6,4},{0,6},{3,1},{5,3},{7,5},{1,7},{10,8},{12,10},{14... | collective-permute-start | bytes 24584 | tf_op jit(solution)/shard_map/ppermute | solution.py:58
  297.7 16.2 %collective-permute-start.41 = (bf16[129,512]{1,0:T(8,128)(2,1)S(1)}, bf16[129,512]{1,0:T(8,128)(2,1)S(1)}, u32[]{:S(2)}, u32[]{:S(2)}) collective-permute-start(bf16[129,512]{1,0:T(8,128)(2,1)S(1)} %get-tuple-element.112), channel_id=1, source_target_pairs={{4,0},{5,1},{6,2},{7,3},{12,4},{13,5},{14,6},{15,7},{0,8},{1,9},{2... | collective-permute-start | bytes 396296 | tf_op jit(solution)/shard_map/ppermute | solution.py:75
  302.8 11.1 %collective-permute-start.42 = (bf16[129,512]{1,0:T(8,128)(2,1)S(1)}, bf16[129,512]{1,0:T(8,128)(2,1)}, u32[]{:S(2)}, u32[]{:S(2)}) collective-permute-start(bf16[129,512]{1,0:T(8,128)(2,1)S(1)} %get-tuple-element.113), channel_id=1, source_target_pairs={{8,4},{9,5},{10,6},{11,7},{4,8},{5,9},{6,10},{7,11},{24,20},{25,21... | collective-permute-start | bytes 396296 | tf_op jit(solution)/shard_map/ppermute | solution.py:76
  309.2 12.8 %collective-permute-start.51 = (bf16[136,512]{0,1:T(8,128)(2,1)S(1)}, bf16[136,512]{0,1:T(8,128)(2,1)S(1)}, u32[]{:S(2)}, u32[]{:S(2)}) collective-permute-start(bf16[136,512]{0,1:T(8,128)(2,1)S(1)} %get-tuple-element.131), channel_id=1, source_target_pairs={{32,0},{64,32},{96,64},{0,96},{33,1},{65,33},{97,65},{1,97},{34,2}... | collective-permute-start | bytes 417800 | tf_op jit(solution)/shard_map/ppermute | solution.py:58
  312.9 12.4 %collective-permute-start.49 = (bf16[136,512]{0,1:T(8,128)(2,1)S(1)}, bf16[136,512]{0,1:T(8,128)(2,1)S(1)}, u32[]{:S(2)}, u32[]{:S(2)}) collective-permute-start(bf16[136,512]{0,1:T(8,128)(2,1)S(1)} %get-tuple-element.130), channel_id=1, source_target_pairs={{96,0},{0,32},{32,64},{64,96},{97,1},{1,33},{33,65},{65,97},{98,2}... | collective-permute-start | bytes 417800 | tf_op jit(solution)/shard_map/ppermute | solution.py:58
  326.6 11.0 %collective-permute-start.40 = (bf16[129,512]{1,0:T(8,128)(2,1)S(1)}, bf16[129,512]{1,0:T(8,128)(2,1)S(1)}, u32[]{:S(2)}, u32[]{:S(2)}) collective-permute-start(bf16[129,512]{1,0:T(8,128)(2,1)S(1)} %get-tuple-element.117), channel_id=1, source_target_pairs={{8,4},{9,5},{10,6},{11,7},{4,8},{5,9},{6,10},{7,11},{24,20},{25,21... | collective-permute-start | bytes 396296 | tf_op jit(solution)/shard_map/ppermute | solution.py:76
  333.2 10.8 %collective-permute-start.54 = (bf16[136,512]{0,1:T(8,128)(2,1)S(1)}, bf16[136,512]{0,1:T(8,128)(2,1)S(1)}, u32[]{:S(2)}, u32[]{:S(2)}) collective-permute-start(bf16[136,512]{0,1:T(8,128)(2,1)S(1)} %add_convert_fusion.4), channel_id=1, source_target_pairs={{64,0},{96,32},{0,64},{32,96},{65,1},{97,33},{1,65},{33,97},{66,2}... | collective-permute-start | bytes 417800 | tf_op jit(solution)/shard_map/ppermute | solution.py:58
  333.5 13.3 %collective-permute-start.55 = (bf16[136,512]{0,1:T(8,128)(2,1)S(1)}, bf16[136,512]{0,1:T(8,128)(2,1)S(1)}, u32[]{:S(2)}, u32[]{:S(2)}) collective-permute-start(bf16[136,512]{0,1:T(8,128)(2,1)S(1)} %add_convert_fusion.4), channel_id=1, source_target_pairs={{96,0},{0,32},{32,64},{64,96},{97,1},{1,33},{33,65},{65,97},{98,2}... | collective-permute-start | bytes 417800 | tf_op jit(solution)/shard_map/ppermute | solution.py:58
  334.7 12.1 %collective-permute-start.53 = (bf16[136,512]{0,1:T(8,128)(2,1)S(1)}, bf16[136,512]{0,1:T(8,128)(2,1)S(1)}, u32[]{:S(2)}, u32[]{:S(2)}) collective-permute-start(bf16[136,512]{0,1:T(8,128)(2,1)S(1)} %add_convert_fusion.4), channel_id=1, source_target_pairs={{32,0},{64,32},{96,64},{0,96},{33,1},{65,33},{97,65},{1,97},{34,2}... | collective-permute-start | bytes 417800 | tf_op jit(solution)/shard_map/ppermute | solution.py:58
  (116 other events, 794.7 us)
where the time goes:
time: 361 us; the launch traced here: 355 us
  waiting for transfers between devices  126 us (35%)
  starting transfers between devices  91.3 us (25%)
  matrix products  41.5 us (11%)
  local copies, waits for them, and re-layouts  41 us (11%)
  other arithmetic  35.6 us (10%)
  Pallas kernels  16.9 us (5%)
    ppermute x39, waiting for transfers between devices, pull(): lax.ppermute(value, axis, [((i + distance) % 4, i) for i in range(4)])  92.1 us
    ppermute x39, starting transfers between devices, pull(): lax.ppermute(value, axis, [((i + distance) % 4, i) for i in range(4)])  53.2 us
    dot_general x24, matrix products, dot(): lax.dot_general(first, second, (((contract[0],), (contract[1],)), ((), ()...  41.5 us
    ppermute x18, waiting for transfers between devices, swap(): return lax.ppermute(value, axis, [(0, 1), (1, 0)])  23.2 us
    ppermute x18, starting transfers between devices, swap(): return lax.ppermute(value, axis, [(0, 1), (1, 0)])  19.7 us
    unnamed x216, local copies, waits for them, and re-layouts  18.2 us
    pallas_call x2, Pallas kernels, local_kernel(): pl.pallas_call(kernel, out_shape=jax.ShapeDtypeStruct((SLOTS * ROWS, widt...  16.9 us
    ppermute x2, starting transfers between devices, place_out(): crossed = lax.ppermute(other, GROUP, EXIT_SECOND)  9.5 us
  transfers between devices with their start and end apart: 63, of which 33 were waited for; matrix products, arithmetic and copies ran while one was open for 21% of the time, Pallas kernels for 0%

commit v1 on v0

--- a/solution.py
+++ b/solution.py
@@ -100,12 +100,16 @@
     return own + swap(other.astype(BF), "xh").astype(F32)
 
 
-def replica_scatter(values):
-    rows = values.shape[0] // NZ
+def replica_scatter(arrays):
     z = lax.axis_index("z")
 
     def chunk(d):
-        return lax.dynamic_slice_in_dim(values, ((z + d) % NZ) * rows, rows, 0)
+        sizes = [values.shape[0] // NZ for values in arrays]
+        cuts = [
+            lax.dynamic_slice_in_dim(values, ((z + d) % NZ) * rows, rows, 0)
+            for values, rows in zip(arrays, sizes)
+        ]
+        return jnp.concatenate(cuts, axis=0)
 
     total = chunk(0)
     for d in (1, 2, 3):
@@ -113,17 +117,21 @@
     return total.astype(BF)
 
 
-def replica_gather(total):
+def replica_gather(total, split):
     z = lax.axis_index("z")
     total = (total.astype(F32) + swap(total, "xl").astype(F32)).astype(BF)
     pieces = [total] + [pull(total, "z", d) for d in (1, 2, 3)]
 
-    def slot(k):
-        d = (k - z) % NZ
-        low = jnp.where(d == 0, pieces[0], pieces[1])
-        return jnp.where(d < 2, low, jnp.where(d == 2, pieces[2], pieces[3])).astype(F32)
-
-    return jnp.concatenate([slot(k) for k in range(NZ)], axis=0)
+    def whole(parts):
+        slots = []
+        for k in range(NZ):
+            d = (k - z) % NZ
+            low = jnp.where(d == 0, parts[0], parts[1])
+            high = jnp.where(d == 2, parts[2], parts[3])
+            slots.append(jnp.where(d < 2, low, high).astype(F32))
+        return jnp.concatenate(slots, axis=0)
+
+    return whole([piece[:split] for piece in pieces]), whole([piece[split:] for piece in pieces])
 
 
 def column_sum(values):
@@ -244,25 +252,24 @@
     own_rows = jnp.concatenate(own_rows, axis=0)
     small = jnp.concatenate([qv_bias.reshape(-1), fc1_bias.reshape(-1)])
     spare = ROWS - HALF
+    real = jnp.arange(ROWS)[:, None] < HALF
+    mine, theirs = place_in(inputs, own_rows[:spare], home)
+    x = jnp.where(real, jnp.concatenate([mine, theirs], axis=1).astype(F32), 0.0)
+    rows = jnp.concatenate([own_rows[:spare], theirs[HALF:]], axis=1).astype(F32)
+    gains, shifts, scales, first_bias = rows[0:2], rows[2:4], rows[4:6], rows[6:7]
+    normed, scaled_first, inverse_first = norm(x, gains[0], shifts[0])
+    normed_first = gather(normed)
     spare_rows = jnp.pad(own_rows[spare:], ((0, spare - 1), (0, 0)))
-    spare_rows = jnp.concatenate([own_rows[:spare], spare_rows], axis=1)
-    block = jnp.concatenate([inputs, cotangent], axis=1)
-    mine, theirs = place_in(block, spare_rows, home)
-    real = jnp.arange(ROWS)[:, None] < HALF
-    x = jnp.concatenate([mine[:, : D // 2], theirs[:, : D // 2]], axis=1)
-    x = jnp.where(real, x.astype(F32), 0.0)
-    upstream = jnp.concatenate([mine[:, D // 2 :], theirs[:, D // 2 :]], axis=1)
-    upstream = jnp.where(real, upstream.astype(F32), 0.0)
-    rows = jnp.concatenate([own_rows[:spare], theirs[HALF:, : D // 2]], axis=1).astype(F32)
-    gains, shifts, scales, first_bias = rows[0:2], rows[2:4], rows[4:6], rows[6:7]
-    second_bias = theirs[HALF : HALF + 1, D // 2 :]
+    mine, theirs = place_in(after(cotangent, normed), spare_rows, home)
+    upstream = jnp.where(real, jnp.concatenate([mine, theirs], axis=1).astype(F32), 0.0)
+    second_bias = theirs[HALF : HALF + 1]
     second_bias = jnp.concatenate([own_rows[spare:], second_bias], axis=1).astype(F32)
 
     out_columns = w_out[0].reshape(128, 4, 128).transpose(1, 0, 2).reshape(D // 2, 128)
     first_weights = jnp.concatenate([w_qkv[0], out_columns], axis=1)
     small_row = jnp.pad(small[None], ((0, 15), (0, 128)))
     first_weights = jnp.concatenate([first_weights, small_row], axis=0)
-    first_weights = swap(after(first_weights, theirs), "xh")
+    first_weights = swap(after(first_weights, normed), "xh")
     small_other = first_weights[D // 2, :384]
     qkv_weight = jnp.concatenate([w_qkv[0], first_weights[: D // 2, :384]], axis=0)
     qkv_weight = qkv_weight.reshape(D, 2, 3, HD).transpose(0, 2, 1, 3).reshape(D, 6 * HD)
@@ -272,8 +279,6 @@
     fc2_other = swap(after(w_fc2[0], fc1_other), "xh")
     fc1_weight = jnp.concatenate([w_fc1[0], fc1_other], axis=0)
     fc2_weight = jnp.concatenate([w_fc2[0], fc2_other], axis=1)
-    normed, scaled_first, inverse_first = norm(x, gains[0], shifts[0])
-    normed_first = gather(normed)
     head_bias = in_order(small[:128], small_other[:128]).astype(F32).reshape(2, 2, HD)
     zeros = jnp.zeros((128,), F32)
     full_bias = jnp.concatenate([head_bias[:, 0].reshape(-1), zeros, head_bias[:, 1].reshape(-1)])
@@ -363,18 +368,19 @@
     late_other = jnp.concatenate([late[D // 2 :], vectors[:, D // 2 :], other], axis=0)
     late_other = late_other.astype(BF)
     late = image_sum(late_own, late_other)
-    fc_sum = replica_gather(replica_scatter(after(fc_sum, arrived[0])))
     active = [after(half, late_other) for half in active]
     branch_second, pieces = scatter_begin(active, fc2_weight, (1, 0))
     normed_grad = after(normed_grad, *pieces)
     branch_second = scatter_end(branch_second, after(pieces, normed_grad)) + second_bias
     output = place_out(x + scales[1] * branch_second, home)
-    final = column_sum(after(jnp.stack([gain_part, shift_part]), normed_grad))
+    final = column_sum(after(jnp.stack([gain_part, shift_part]), late_other, arrived[1]))
     final = final[:, : D // 2] + swap(final[:, D // 2 :], "xh")
     late = jnp.concatenate([late, final, jnp.zeros((32 - 9, D // 2), F32)], axis=0)
     first_pull = norm_pull(normed_grad, scaled_first, inverse_first, gains[0])
     input_grad = place_out(upstream + first_pull, home)
-    late = replica_gather(replica_scatter(after(late, fc_sum, branch_second, first_pull)))
+    quarter = replica_scatter([fc_sum, after(late, normed_grad)])
+    quarter = after(quarter, branch_second, first_pull)
+    fc_sum, late = replica_gather(quarter, fc_sum.shape[0] // NZ)
 
     qkv_grad = late[: D // 2, :384].reshape(D // 2, 3, 2, HD).transpose(0, 2, 1, 3)
     out_grad = late[: D // 2, 384:].T

time: 361 us -> 330 us (0.914)
  waiting for transfers between devices: 126 us -> 117 us
  matrix products: 41.5 us -> 35.3 us
  local copies, waits for them, and re-layouts: 41 us -> 35.1 us
  starting transfers between devices: 91.3 us -> 85.6 us
  other arithmetic: 35.6 us -> 30.8 us
    ppermute x39 -> x33, waiting for transfers between devices: 92.1 us -> 80.4 us  [pull(): lax.ppermute(value, axis, [((i + distance) % 4, i) for i in range(4)])]
    ppermute x18 -> x17, waiting for transfers between devices: 23.2 us -> 32.7 us  [swap(): return lax.ppermute(value, axis, [(0, 1), (1, 0)])]
    ppermute x18 -> x17, starting transfers between devices: 19.7 us -> 10.6 us  [swap(): return lax.ppermute(value, axis, [(0, 1), (1, 0)])]
    ppermute x1 -> x2, starting transfers between devices: 7.63 us -> 14.1 us  [place_in(): crossed = lax.ppermute(second, GROUP, ENTRY_SECOND)]
    dot_general x24, matrix products: 41.5 us -> 35.3 us  [dot(): lax.dot_general(first, second, (((contract[0],), (contract[1],)), ((), ()...]
    ppermute x1 -> x2, waiting for transfers between devices: 8.6 us -> 3.71 us  [place_in(): crossed = lax.ppermute(second, GROUP, ENTRY_SECOND)]
    ppermute x39 -> x33, starting transfers between devices: 53.2 us -> 49 us  [pull(): lax.ppermute(value, axis, [((i + distance) % 4, i) for i in range(4)])]
    unnamed x216 -> x210, local copies, waits for them, and re-layouts: 18.2 us -> 19.4 us
  transfers between devices with their start and end apart: 63 -> 58, of which waited for: 33 -> 28; matrix products, arithmetic and copies ran while one was open for 21% -> 20% of each run, Pallas kernels for 0% -> 0%
where the time goes in v1:
time: 330 us; the launch traced here: 323 us
  waiting for transfers between devices  117 us (35%)
  starting transfers between devices  85.6 us (26%)
  matrix products  35.3 us (11%)
  local copies, waits for them, and re-layouts  35.1 us (11%)
  other arithmetic  30.8 us (9%)
  Pallas kernels  16.9 us (5%)
    ppermute x33, waiting for transfers between devices, pull(): lax.ppermute(value, axis, [((i + distance) % 4, i) for i in range(4)])  80.4 us
    ppermute x33, starting transfers between devices, pull(): lax.ppermute(value, axis, [((i + distance) % 4, i) for i in range(4)])  49 us
    dot_general x24, matrix products, dot(): lax.dot_general(first, second, (((contract[0],), (contract[1],)), ((), ()...  35.3 us
    ppermute x17, waiting for transfers between devices, swap(): return lax.ppermute(value, axis, [(0, 1), (1, 0)])  32.7 us
    unnamed x210, local copies, waits for them, and re-layouts  19.4 us
    pallas_call x2, Pallas kernels, local_kernel(): pl.pallas_call(kernel, out_shape=jax.ShapeDtypeStruct((SLOTS * ROWS, widt...  16.9 us
    ppermute x2, starting transfers between devices, place_in(): crossed = lax.ppermute(second, GROUP, ENTRY_SECOND)  14.1 us
    ppermute x17, starting transfers between devices, swap(): return lax.ppermute(value, axis, [(0, 1), (1, 0)])  10.6 us
  transfers between devices with their start and end apart: 58, of which 28 were waited for; matrix products, arithmetic and copies ran while one was open for 20% of the time, Pallas kernels for 0%

profile of v1, /device:TPU:4, one launch (start us, length us, event | category | flops | bytes accessed | tf_op | source)
XLA Modules:
  0.0 323.4 jit_solution(1274895236908354590)
XLA Ops:
  3.0 7.6 %collective-permute-start.1 = (bf16[136,512]{1,0:T(8,128)(2,1)S(1)}, bf16[136,512]{1,0:T(8,128)(2,1)S(1)}, u32[]{:S(2)}, u32[]{:S(2)}) collective-permute-start(bf16[136,512]{1,0:T(8,128)(2,1)S(1)} %get-tuple-element.163), channel_id=1, source_target_pairs={{4,8},{5,9},{6,10},{7,11},{8,4},{9,5},{10,6},{11,7},{20,24},{21,25... | collective-permute-start | bytes 417800 | tf_op jit(solution)/shard_map/ppermute | solution.py:69
  11.4 3.7 %collective-permute-done.1 = bf16[136,512]{1,0:T(8,128)(2,1)S(1)} collective-permute-done((bf16[136,512]{1,0:T(8,128)(2,1)S(1)}, bf16[136,512]{1,0:T(8,128)(2,1)S(1)}, u32[]{:S(2)}, u32[]{:S(2)}) %collective-permute-start.1) | collective-permute-done | bytes 139296 | tf_op jit(solution)/shard_map/ppermute | solution.py:69
  17.4 6.5 %collective-permute-start.9 = (bf16[136,512]{1,0:T(8,128)(2,1)S(1)}, bf16[136,512]{1,0:T(8,128)(2,1)S(1)}, u32[]{:S(2)}, u32[]{:S(2)}) collective-permute-start(bf16[136,512]{1,0:T(8,128)(2,1)S(1)} %get-tuple-element.165), channel_id=1, source_target_pairs={{4,8},{5,9},{6,10},{7,11},{8,4},{9,5},{10,6},{11,7},{20,24},{21,25... | collective-permute-start | bytes 417800 | tf_op jit(solution)/shard_map/ppermute | solution.py:69
  26.8 2.8 collective-permute-start.2
  32.3 8.0 %collective-permute-done.4 = bf16[136,1024]{1,0:T(8,128)(2,1)S(1)} collective-permute-done((bf16[136,1024]{1,0:T(8,128)(2,1)S(1)}, bf16[136,1024]{1,0:T(8,128)(2,1)S(1)}, u32[]{:S(2)}, u32[]{:S(2)}) %collective-permute-start.4) | collective-permute-done | bytes 278560 | tf_op jit(solution)/shard_map/ppermute | solution.py:58
  42.0 2.6 collective-permute-start.10
  54.3 3.2 collective-permute-done.10
  62.8 2.0 fusion.3
  65.2 4.7 %shard_map.211 = bf16[1088,128]{1,0:T(8,128)(2,1)S(1)} custom-call(f32[1,1088]{1,0:T(1,128)S(1)} %compare_convert_fusion.mask_ref, bf16[1088,384]{1,0:T(8,128)(2,1)S(1)} %pad_maximum_fusion.6.packed_ref), custom_call_target="tpu_custom_call" | custom-call | flops 8000000000 | bytes 24000000 | tf_op jit(solution)/shard_map/pallas_call | solution.py:208
  70.4 2.7 collective-permute-done.13
  73.8 2.4 collective-permute-start.16
  76.1 2.0 collective-permute-start.15
  79.1 9.2 %collective-permute-done.16 = bf16[136,1024]{1,0:T(8,128)(2,1)S(1)} collective-permute-done((bf16[136,1024]{1,0:T(8,128)(2,1)S(1)}, bf16[136,1024]{1,0:T(8,128)(2,1)S(1)}, u32[]{:S(2)}, u32[]{:S(2)}) %collective-permute-start.16) | collective-permute-done | bytes 278560 | tf_op jit(solution)/shard_map/ppermute | solution.py:58
  88.3 3.7 %collective-permute-done.14 = bf16[136,1024]{1,0:T(8,128)(2,1)S(1)} collective-permute-done((bf16[136,1024]{1,0:T(8,128)(2,1)S(1)}, bf16[136,1024]{1,0:T(8,128)(2,1)S(1)}, u32[]{:S(2)}, u32[]{:S(2)}) %collective-permute-start.14) | collective-permute-done | bytes 278560 | tf_op jit(solution)/shard_map/ppermute | solution.py:58
  94.8 3.2 collective-permute-start.19
  102.9 7.2 %collective-permute-done.19 = bf16[136,1024]{1,0:T(8,128)(2,1)} collective-permute-done((bf16[136,1024]{1,0:T(8,128)(2,1)}, bf16[136,1024]{1,0:T(8,128)(2,1)}, u32[]{:S(2)}, u32[]{:S(2)}) %collective-permute-start.19) | collective-permute-done | bytes 278560 | tf_op jit(solution)/shard_map/ppermute | solution.py:58
  119.7 2.2 multiply_convert_fusion.1
  122.0 2.4 multiply_convert_fusion
  125.5 1.9 convolution_convert_fusion.1
  134.4 3.5 %collective-permute-start.26 = (bf16[136,1024]{1,0:T(8,128)(2,1)S(1)}, bf16[136,1024]{1,0:T(8,128)(2,1)S(1)}, u32[]{:S(2)}, u32[]{:S(2)}) collective-permute-start(bf16[136,1024]{1,0:T(8,128)(2,1)S(1)} %get-tuple-element.146), channel_id=1, source_target_pairs={{2,0},{4,2},{6,4},{0,6},{3,1},{5,3},{7,5},{1,7},{10,8},{12,10},{14... | collective-permute-start | bytes 835592 | tf_op jit(solution)/shard_map/ppermute | solution.py:58
  138.9 3.6 %fusion.97 = f32[1024,512]{1,0:T(8,128)} fusion(bf16[544,1024]{1,0:T(8,128)(2,1)} %collective-permute-done.22, bf16[544,512]{1,0:T(8,128)(2,1)S(1)} %get-tuple-element.203), kind=kOutput, calls=%fused_computation.301 | convolution fusion | flops 570425344 | bytes 3768320 | tf_op jit(solution)/shard_map/dot_general | solution.py:144
  143.4 6.6 %collective-permute-done.26 = bf16[136,1024]{1,0:T(8,128)(2,1)S(1)} collective-permute-done((bf16[136,1024]{1,0:T(8,128)(2,1)S(1)}, bf16[136,1024]{1,0:T(8,128)(2,1)S(1)}, u32[]{:S(2)}, u32[]{:S(2)}) %collective-permute-start.26) | collective-permute-done | bytes 278560 | tf_op jit(solution)/shard_map/ppermute | solution.py:58
  150.0 3.4 %collective-permute-done.24 = bf16[136,1024]{1,0:T(8,128)(2,1)S(1)} collective-permute-done((bf16[136,1024]{1,0:T(8,128)(2,1)S(1)}, bf16[136,1024]{1,0:T(8,128)(2,1)S(1)}, u32[]{:S(2)}, u32[]{:S(2)}) %collective-permute-start.24) | collective-permute-done | bytes 278560 | tf_op jit(solution)/shard_map/ppermute | solution.py:58
  160.6 2.1 collective-permute-start.30
  165.7 2.9 convolution_add_fusion
  168.7 7.5 %collective-permute-done.30 = bf16[136,1024]{1,0:T(8,128)(2,1)S(1)} collective-permute-done((bf16[136,1024]{1,0:T(8,128)(2,1)S(1)}, bf16[136,1024]{1,0:T(8,128)(2,1)S(1)}, u32[]{:S(2)}, u32[]{:S(2)}) %collective-permute-start.30) | collective-permute-done | bytes 278560 | tf_op jit(solution)/shard_map/ppermute | solution.py:58
  178.8 14.3 %collective-permute-done.32 = bf16[512,512]{1,0:T(8,128)(2,1)S(1)} collective-permute-done((bf16[512,512]{1,0:T(8,128)(2,1)S(1)}, bf16[512,512]{1,0:T(8,128)(2,1)S(1)}, u32[]{:S(2)}, u32[]{:S(2)}) %collective-permute-start.32) | collective-permute-done | bytes 524320 | tf_op jit(solution)/shard_map/ppermute | solution.py:54
  195.2 12.2 %shard_map.212 = bf16[1088,384]{1,0:T(8,128)(2,1)S(1)} custom-call(f32[1,1088]{1,0:T(1,128)S(1)} %compare_convert_fusion.mask_ref, bf16[1088,384]{1,0:T(8,128)(2,1)S(1)} %pad_maximum_fusion.6.packed_ref, bf16[1088,128]{1,0:T(8,128)(2,1)S(1)} %pad_maximum_fusion.15.grad_ref), custom_call_target="tpu_custom_call" | custom-call | flops 12000000000 | bytes 36000000 | tf_op jit(solution)/shard_map/pallas_call | solution.py:208
  211.4 2.1 fusion.94
  214.4 2.6 collective-permute-start.37
  218.8 2.3 fusion.48
  226.2 2.2 collective-permute-done.36
  229.6 4.1 %collective-permute-start.48 = (f32[2,1024]{1,0:T(2,128)S(1)}, f32[2,1024]{1,0:T(2,128)S(1)}, u32[]{:S(2)}, u32[]{:S(2)}) collective-permute-start(f32[2,1024]{1,0:T(2,128)S(1)} %add.467), channel_id=1, source_target_pairs={{2,0},{4,2},{6,4},{0,6},{3,1},{5,3},{7,5},{1,7},{10,8},{12,10},{14... | collective-permute-start | bytes 24584 | tf_op jit(solution)/shard_map/ppermute | solution.py:58
  236.3 2.3 collective-permute-done.49
  241.6 9.2 %collective-permute-done.50 = f32[2,512]{1,0:T(2,128)S(1)} collective-permute-done((f32[2,512]{1,0:T(2,128)S(1)}, f32[2,512]{1,0:T(2,128)S(1)}, u32[]{:S(2)}, u32[]{:S(2)}) %collective-permute-start.50) | collective-permute-done | bytes 4128 | tf_op jit(solution)/shard_map/ppermute | solution.py:54
  255.3 2.7 collective-permute-start.40
  261.0 4.1 %collective-permute-start.53 = (bf16[392,512]{1,0:T(8,128)(2,1)S(1)}, bf16[392,512]{1,0:T(8,128)(2,1)S(1)}, u32[]{:S(2)}, u32[]{:S(2)}) collective-permute-start(bf16[392,512]{1,0:T(8,128)(2,1)S(1)} %pad_maximum_fusion.12), channel_id=1, source_target_pairs={{32,0},{64,32},{96,64},{0,96},{33,1},{65,33},{97,65},{1,97},{34,2}... | collective-permute-start | bytes 1204232 | tf_op jit(solution)/shard_map/ppermute | solution.py:58
  265.3 2.9 collective-permute-done.40
  268.2 1.9 collective-permute-start.51
  270.1 2.1 collective-permute-start.43
  272.2 3.7 %collective-permute-start.44 = (bf16[129,512]{1,0:T(8,128)(2,1)S(1)}, bf16[129,512]{1,0:T(8,128)(2,1)S(1)}, u32[]{:S(2)}, u32[]{:S(2)}) collective-permute-start(bf16[129,512]{1,0:T(8,128)(2,1)S(1)} %get-tuple-element.113), channel_id=1, source_target_pairs={{8,4},{9,5},{10,6},{11,7},{4,8},{5,9},{6,10},{7,11},{24,20},{25,21... | collective-permute-start | bytes 396296 | tf_op jit(solution)/shard_map/ppermute | solution.py:76
  276.2 4.1 %collective-permute-done.53 = bf16[392,512]{1,0:T(8,128)(2,1)S(1)} collective-permute-done((bf16[392,512]{1,0:T(8,128)(2,1)S(1)}, bf16[392,512]{1,0:T(8,128)(2,1)S(1)}, u32[]{:S(2)}, u32[]{:S(2)}) %collective-permute-start.53) | collective-permute-done | bytes 401440 | tf_op jit(solution)/shard_map/ppermute | solution.py:58
  280.3 3.7 %collective-permute-done.51 = bf16[392,512]{1,0:T(8,128)(2,1)S(1)} collective-permute-done((bf16[392,512]{1,0:T(8,128)(2,1)S(1)}, bf16[392,512]{1,0:T(8,128)(2,1)S(1)}, u32[]{:S(2)}, u32[]{:S(2)}) %collective-permute-start.51) | collective-permute-done | bytes 401440 | tf_op jit(solution)/shard_map/ppermute | solution.py:58
  285.5 2.2 collective-permute-start.41
  287.7 3.3 %collective-permute-start.42 = (bf16[129,512]{1,0:T(8,128)(2,1)S(1)}, bf16[129,512]{1,0:T(8,128)(2,1)S(1)}, u32[]{:S(2)}, u32[]{:S(2)}) collective-permute-start(bf16[129,512]{1,0:T(8,128)(2,1)S(1)} %get-tuple-element.117), channel_id=1, source_target_pairs={{8,4},{9,5},{10,6},{11,7},{4,8},{5,9},{6,10},{7,11},{24,20},{25,21... | collective-permute-start | bytes 396296 | tf_op jit(solution)/shard_map/ppermute | solution.py:76
  291.0 4.9 %collective-permute-done.54 = bf16[392,512]{1,0:T(8,128)(2,1)S(1)} collective-permute-done((bf16[392,512]{1,0:T(8,128)(2,1)S(1)}, bf16[392,512]{1,0:T(8,128)(2,1)S(1)}, u32[]{:S(2)}, u32[]{:S(2)}) %collective-permute-start.54) | collective-permute-done | bytes 401440 | tf_op jit(solution)/shard_map/ppermute | solution.py:54
  297.1 2.2 collective-permute-start.55
  301.1 12.6 %collective-permute-done.57 = bf16[392,512]{1,0:T(8,128)(2,1)S(1)} collective-permute-done((bf16[392,512]{1,0:T(8,128)(2,1)S(1)}, bf16[392,512]{1,0:T(8,128)(2,1)S(1)}, u32[]{:S(2)}, u32[]{:S(2)}) %collective-permute-start.57) | collective-permute-done | bytes 401440 | tf_op jit(solution)/shard_map/ppermute | solution.py:58
  (459 shorter events, 110.7 us)
Async XLA Ops:
  3.0 12.1 %collective-permute-start.1 = (bf16[136,512]{1,0:T(8,128)(2,1)S(1)}, bf16[136,512]{1,0:T(8,128)(2,1)S(1)}, u32[]{:S(2)}, u32[]{:S(2)}) collective-permute-start(bf16[136,512]{1,0:T(8,128)(2,1)S(1)} %get-tuple-element.163), channel_id=1, source_target_pairs={{4,8},{5,9},{6,10},{7,11},{8,4},{9,5},{10,6},{11,7},{20,24},{21,25... | collective-permute-start | bytes 417800 | tf_op jit(solution)/shard_map/ppermute | solution.py:69
  17.3 12.3 %collective-permute-start.8 = (bf16[136,512]{1,0:T(8,128)(2,1)S(1)}, bf16[136,512]{1,0:T(8,128)(2,1)S(1)}, u32[]{:S(2)}, u32[]{:S(2)}) collective-permute-start(bf16[136,512]{1,0:T(8,128)(2,1)S(1)} %get-tuple-element.166), channel_id=1, source_target_pairs={{0,4},{1,5},{2,6},{3,7},{4,12},{5,13},{6,14},{7,15},{8,0},{9,1},{1... | collective-permute-start | bytes 417800 | tf_op jit(solution)/shard_map/ppermute | solution.py:68
  17.4 13.3 %collective-permute-start.9 = (bf16[136,512]{1,0:T(8,128)(2,1)S(1)}, bf16[136,512]{1,0:T(8,128)(2,1)S(1)}, u32[]{:S(2)}, u32[]{:S(2)}) collective-permute-start(bf16[136,512]{1,0:T(8,128)(2,1)S(1)} %get-tuple-element.165), channel_id=1, source_target_pairs={{4,8},{5,9},{6,10},{7,11},{8,4},{9,5},{10,6},{11,7},{20,24},{21,25... | collective-permute-start | bytes 417800 | tf_op jit(solution)/shard_map/ppermute | solution.py:69
  26.1 14.2 %collective-permute-start.4 = (bf16[136,1024]{1,0:T(8,128)(2,1)S(1)}, bf16[136,1024]{1,0:T(8,128)(2,1)S(1)}, u32[]{:S(2)}, u32[]{:S(2)}) collective-permute-start(bf16[136,1024]{1,0:T(8,128)(2,1)S(1)} %add_convert_fusion.2), channel_id=1, source_target_pairs={{6,0},{0,2},{2,4},{4,6},{7,1},{1,3},{3,5},{5,7},{14,8},{8,10},{10,... | collective-permute-start | bytes 835592 | tf_op jit(solution)/shard_map/ppermute | solution.py:58
  26.8 13.4 %collective-permute-start.3 = (bf16[136,1024]{1,0:T(8,128)(2,1)S(1)}, bf16[136,1024]{1,0:T(8,128)(2,1)S(1)}, u32[]{:S(2)}, u32[]{:S(2)}) collective-permute-start(bf16[136,1024]{1,0:T(8,128)(2,1)S(1)} %add_convert_fusion.2), channel_id=1, source_target_pairs={{4,0},{6,2},{0,4},{2,6},{5,1},{7,3},{1,5},{3,7},{12,8},{14,10},{8,... | collective-permute-start | bytes 835592 | tf_op jit(solution)/shard_map/ppermute | solution.py:58
  26.8 14.0 %collective-permute-start.2 = (bf16[136,1024]{1,0:T(8,128)(2,1)S(1)}, bf16[136,1024]{1,0:T(8,128)(2,1)S(1)}, u32[]{:S(2)}, u32[]{:S(2)}) collective-permute-start(bf16[136,1024]{1,0:T(8,128)(2,1)S(1)} %add_convert_fusion.2), channel_id=1, source_target_pairs={{2,0},{4,2},{6,4},{0,6},{3,1},{5,3},{7,5},{1,7},{10,8},{12,10},{14... | collective-permute-start | bytes 835592 | tf_op jit(solution)/shard_map/ppermute | solution.py:58
  29.6 17.0 %collective-permute-start.5 = (bf16[528,512]{1,0:T(8,128)(2,1)S(1)}, bf16[528,512]{1,0:T(8,128)(2,1)S(1)}, u32[]{:S(2)}, u32[]{:S(2)}) collective-permute-start(bf16[528,512]{1,0:T(8,128)(2,1)S(1)} %fusion.33), channel_id=1, source_target_pairs={{0,8},{8,0},{1,9},{9,1},{2,10},{10,2},{3,11},{11,3},{4,12},{12,4},... | collective-permute-start | bytes 1622024 | tf_op jit(solution)/shard_map/ppermute | solution.py:54
  42.0 19.9 %collective-permute-start.6 = (bf16[544,1024]{1,0:T(8,128)(2,1)}, bf16[544,1024]{1,0:T(8,128)(2,1)}, u32[]{:S(2)}, u32[]{:S(2)}) collective-permute-start(bf16[544,1024]{1,0:T(8,128)(2,1)} %pad_maximum_fusion.1), channel_id=1, source_target_pairs={{0,1},{1,0},{2,3},{3,2},{4,5},{5,4},{6,7},{7,6},{8,9},{9,8},{10,11... | collective-permute-start | bytes 3342344 | tf_op jit(solution)/shard_map/ppermute | solution.py:54
  42.0 15.5 %collective-permute-start.10 = (bf16[136,1024]{1,0:T(8,128)(2,1)}, bf16[136,1024]{1,0:T(8,128)(2,1)}, u32[]{:S(2)}, u32[]{:S(2)}) collective-permute-start(bf16[136,1024]{1,0:T(8,128)(2,1)} %get-tuple-element.36), channel_id=1, source_target_pairs={{2,0},{4,2},{6,4},{0,6},{3,1},{5,3},{7,5},{1,7},{10,8},{12,10},{14... | collective-permute-start | bytes 835592 | tf_op jit(solution)/shard_map/ppermute | solution.py:58
  44.6 13.9 %collective-permute-start.11 = (bf16[136,1024]{1,0:T(8,128)(2,1)}, bf16[136,1024]{1,0:T(8,128)(2,1)}, u32[]{:S(2)}, u32[]{:S(2)}) collective-permute-start(bf16[136,1024]{1,0:T(8,128)(2,1)} %get-tuple-element.36), channel_id=1, source_target_pairs={{4,0},{6,2},{0,4},{2,6},{5,1},{7,3},{1,5},{3,7},{12,8},{14,10},{8,... | collective-permute-start | bytes 835592 | tf_op jit(solution)/shard_map/ppermute | solution.py:58
  44.6 16.3 %collective-permute-start.12 = (bf16[136,1024]{1,0:T(8,128)(2,1)}, bf16[136,1024]{1,0:T(8,128)(2,1)}, u32[]{:S(2)}, u32[]{:S(2)}) collective-permute-start(bf16[136,1024]{1,0:T(8,128)(2,1)} %get-tuple-element.36), channel_id=1, source_target_pairs={{6,0},{0,2},{2,4},{4,6},{7,1},{1,3},{3,5},{5,7},{14,8},{8,10},{10,... | collective-permute-start | bytes 835592 | tf_op jit(solution)/shard_map/ppermute | solution.py:58
  49.6 15.6 %collective-permute-start.7 = (bf16[512,512]{1,0:T(8,128)(2,1)S(1)}, bf16[512,512]{1,0:T(8,128)(2,1)}, u32[]{:S(2)}, u32[]{:S(2)}) collective-permute-start(bf16[512,512]{1,0:T(8,128)(2,1)S(1)} %bitcast.126), channel_id=1, source_target_pairs={{0,8},{8,0},{1,9},{9,1},{2,10},{10,2},{3,11},{11,3},{4,12},{12,4},... | collective-permute-start | bytes 1572872 | tf_op jit(solution)/shard_map/ppermute | solution.py:54
  73.8 14.6 %collective-permute-start.16 = (bf16[136,1024]{1,0:T(8,128)(2,1)S(1)}, bf16[136,1024]{1,0:T(8,128)(2,1)S(1)}, u32[]{:S(2)}, u32[]{:S(2)}) collective-permute-start(bf16[136,1024]{1,0:T(8,128)(2,1)S(1)} %get-tuple-element.149), channel_id=1, source_target_pairs={{2,0},{4,2},{6,4},{0,6},{3,1},{5,3},{7,5},{1,7},{10,8},{12,10},{14... | collective-permute-start | bytes 835592 | tf_op jit(solution)/shard_map/ppermute | solution.py:58
  76.1 12.2 %collective-permute-start.15 = (bf16[136,1024]{1,0:T(8,128)(2,1)S(1)}, bf16[136,1024]{1,0:T(8,128)(2,1)S(1)}, u32[]{:S(2)}, u32[]{:S(2)}) collective-permute-start(bf16[136,1024]{1,0:T(8,128)(2,1)S(1)} %get-tuple-element.150), channel_id=1, source_target_pairs={{4,0},{6,2},{0,4},{2,6},{5,1},{7,3},{1,5},{3,7},{12,8},{14,10},{8,... | collective-permute-start | bytes 835592 | tf_op jit(solution)/shard_map/ppermute | solution.py:58
  78.2 13.9 %collective-permute-start.14 = (bf16[136,1024]{1,0:T(8,128)(2,1)S(1)}, bf16[136,1024]{1,0:T(8,128)(2,1)S(1)}, u32[]{:S(2)}, u32[]{:S(2)}) collective-permute-start(bf16[136,1024]{1,0:T(8,128)(2,1)S(1)} %get-tuple-element.148), channel_id=1, source_target_pairs={{6,0},{0,2},{2,4},{4,6},{7,1},{1,3},{3,5},{5,7},{14,8},{8,10},{10,... | collective-permute-start | bytes 835592 | tf_op jit(solution)/shard_map/ppermute | solution.py:58
  78.2 15.9 %collective-permute-start.18 = (bf16[544,1024]{1,0:T(8,128)(2,1)S(1)}, bf16[544,1024]{1,0:T(8,128)(2,1)S(1)}, u32[]{:S(2)}, u32[]{:S(2)}) collective-permute-start(bf16[544,1024]{1,0:T(8,128)(2,1)S(1)} %copy-done.6), channel_id=1, source_target_pairs={{0,1},{1,0},{2,3},{3,2},{4,5},{5,4},{6,7},{7,6},{8,9},{9,8},{10,11... | collective-permute-start | bytes 3342344 | tf_op jit(solution)/shard_map/ppermute | solution.py:54
  78.2 15.8 %collective-permute-start.17 = (bf16[512,512]{1,0:T(8,128)(2,1)S(1)}, bf16[512,512]{1,0:T(8,128)(2,1)S(1)}, u32[]{:S(2)}, u32[]{:S(2)}) collective-permute-start(bf16[512,512]{1,0:T(8,128)(2,1)S(1)} %bitcast.108), channel_id=1, source_target_pairs={{0,8},{8,0},{1,9},{9,1},{2,10},{10,2},{3,11},{11,3},{4,12},{12,4},... | collective-permute-start | bytes 1572872 | tf_op jit(solution)/shard_map/ppermute | solution.py:54
  94.8 15.2 %collective-permute-start.19 = (bf16[136,1024]{1,0:T(8,128)(2,1)}, bf16[136,1024]{1,0:T(8,128)(2,1)}, u32[]{:S(2)}, u32[]{:S(2)}) collective-permute-start(bf16[136,1024]{1,0:T(8,128)(2,1)} %add_convert_fusion.1), channel_id=1, source_target_pairs={{2,0},{4,2},{6,4},{0,6},{3,1},{5,3},{7,5},{1,7},{10,8},{12,10},{14... | collective-permute-start | bytes 835592 | tf_op jit(solution)/shard_map/ppermute | solution.py:58
  98.0 13.7 %collective-permute-start.20 = (bf16[136,1024]{1,0:T(8,128)(2,1)}, bf16[136,1024]{1,0:T(8,128)(2,1)}, u32[]{:S(2)}, u32[]{:S(2)}) collective-permute-start(bf16[136,1024]{1,0:T(8,128)(2,1)} %add_convert_fusion.1), channel_id=1, source_target_pairs={{4,0},{6,2},{0,4},{2,6},{5,1},{7,3},{1,5},{3,7},{12,8},{14,10},{8,... | collective-permute-start | bytes 835592 | tf_op jit(solution)/shard_map/ppermute | solution.py:58
  99.6 14.1 %collective-permute-start.21 = (bf16[136,1024]{1,0:T(8,128)(2,1)}, bf16[136,1024]{1,0:T(8,128)(2,1)S(1)}, u32[]{:S(2)}, u32[]{:S(2)}) collective-permute-start(bf16[136,1024]{1,0:T(8,128)(2,1)} %add_convert_fusion.1), channel_id=1, source_target_pairs={{6,0},{0,2},{2,4},{4,6},{7,1},{1,3},{3,5},{5,7},{14,8},{8,10},{10,... | collective-permute-start | bytes 835592 | tf_op jit(solution)/shard_map/ppermute | solution.py:58
  134.4 15.6 %collective-permute-start.26 = (bf16[136,1024]{1,0:T(8,128)(2,1)S(1)}, bf16[136,1024]{1,0:T(8,128)(2,1)S(1)}, u32[]{:S(2)}, u32[]{:S(2)}) collective-permute-start(bf16[136,1024]{1,0:T(8,128)(2,1)S(1)} %get-tuple-element.146), channel_id=1, source_target_pairs={{2,0},{4,2},{6,4},{0,6},{3,1},{5,3},{7,5},{1,7},{10,8},{12,10},{14... | collective-permute-start | bytes 835592 | tf_op jit(solution)/shard_map/ppermute | solution.py:58
  137.9 12.1 %collective-permute-start.25 = (bf16[136,1024]{1,0:T(8,128)(2,1)S(1)}, bf16[136,1024]{1,0:T(8,128)(2,1)S(1)}, u32[]{:S(2)}, u32[]{:S(2)}) collective-permute-start(bf16[136,1024]{1,0:T(8,128)(2,1)S(1)} %get-tuple-element.147), channel_id=1, source_target_pairs={{4,0},{6,2},{0,4},{2,6},{5,1},{7,3},{1,5},{3,7},{12,8},{14,10},{8,... | collective-permute-start | bytes 835592 | tf_op jit(solution)/shard_map/ppermute | solution.py:58
  137.9 15.5 %collective-permute-start.24 = (bf16[136,1024]{1,0:T(8,128)(2,1)S(1)}, bf16[136,1024]{1,0:T(8,128)(2,1)S(1)}, u32[]{:S(2)}, u32[]{:S(2)}) collective-permute-start(bf16[136,1024]{1,0:T(8,128)(2,1)S(1)} %get-tuple-element.145), channel_id=1, source_target_pairs={{6,0},{0,2},{2,4},{4,6},{7,1},{1,3},{3,5},{5,7},{14,8},{8,10},{10,... | collective-permute-start | bytes 835592 | tf_op jit(solution)/shard_map/ppermute | solution.py:58
  142.5 15.0 %collective-permute-start.27 = (bf16[512,512]{1,0:T(8,128)(2,1)S(1)}, bf16[512,512]{1,0:T(8,128)(2,1)S(1)}, u32[]{:S(2)}, u32[]{:S(2)}) collective-permute-start(bf16[512,512]{1,0:T(8,128)(2,1)S(1)} %slice.609), channel_id=1, source_target_pairs={{0,8},{8,0},{1,9},{9,1},{2,10},{10,2},{3,11},{11,3},{4,12},{12,4},... | collective-permute-start | bytes 1572872 | tf_op jit(solution)/shard_map/ppermute | solution.py:54
  160.6 15.5 %collective-permute-start.30 = (bf16[136,1024]{1,0:T(8,128)(2,1)S(1)}, bf16[136,1024]{1,0:T(8,128)(2,1)S(1)}, u32[]{:S(2)}, u32[]{:S(2)}) collective-permute-start(bf16[136,1024]{1,0:T(8,128)(2,1)S(1)} %pad.14), channel_id=1, source_target_pairs={{6,0},{0,2},{2,4},{4,6},{7,1},{1,3},{3,5},{5,7},{14,8},{8,10},{10,... | collective-permute-start | bytes 835592 | tf_op jit(solution)/shard_map/ppermute | solution.py:58
  162.7 13.4 %collective-permute-start.29 = (bf16[136,1024]{1,0:T(8,128)(2,1)S(1)}, bf16[136,1024]{1,0:T(8,128)(2,1)S(1)}, u32[]{:S(2)}, u32[]{:S(2)}) collective-permute-start(bf16[136,1024]{1,0:T(8,128)(2,1)S(1)} %pad.14), channel_id=1, source_target_pairs={{4,0},{6,2},{0,4},{2,6},{5,1},{7,3},{1,5},{3,7},{12,8},{14,10},{8,... | collective-permute-start | bytes 835592 | tf_op jit(solution)/shard_map/ppermute | solution.py:58
  164.2 12.5 %collective-permute-start.28 = (bf16[136,1024]{1,0:T(8,128)(2,1)S(1)}, bf16[136,1024]{1,0:T(8,128)(2,1)S(1)}, u32[]{:S(2)}, u32[]{:S(2)}) collective-permute-start(bf16[136,1024]{1,0:T(8,128)(2,1)S(1)} %pad.14), channel_id=1, source_target_pairs={{2,0},{4,2},{6,4},{0,6},{3,1},{5,3},{7,5},{1,7},{10,8},{12,10},{14... | collective-permute-start | bytes 835592 | tf_op jit(solution)/shard_map/ppermute | solution.py:58
  176.8 17.8 %collective-permute-start.31 = (bf16[544,1024]{1,0:T(8,128)(2,1)S(1)}, bf16[544,1024]{1,0:T(8,128)(2,1)S(1)}, u32[]{:S(2)}, u32[]{:S(2)}) collective-permute-start(bf16[544,1024]{1,0:T(8,128)(2,1)S(1)} %pad_maximum_fusion.2), channel_id=1, source_target_pairs={{0,1},{1,0},{2,3},{3,2},{4,5},{5,4},{6,7},{7,6},{8,9},{9,8},{10,11... | collective-permute-start | bytes 3342344 | tf_op jit(solution)/shard_map/ppermute | solution.py:54
  177.2 15.9 %collective-permute-start.32 = (bf16[512,512]{1,0:T(8,128)(2,1)S(1)}, bf16[512,512]{1,0:T(8,128)(2,1)S(1)}, u32[]{:S(2)}, u32[]{:S(2)}) collective-permute-start(bf16[512,512]{1,0:T(8,128)(2,1)S(1)} %slice.608), channel_id=1, source_target_pairs={{0,8},{8,0},{1,9},{9,1},{2,10},{10,2},{3,11},{11,3},{4,12},{12,4},... | collective-permute-start | bytes 1572872 | tf_op jit(solution)/shard_map/ppermute | solution.py:54
  214.4 25.7 %collective-permute-start.37 = (bf16[136,1024]{1,0:T(8,128)(2,1)}, bf16[136,1024]{1,0:T(8,128)(2,1)}, u32[]{:S(2)}, u32[]{:S(2)}) collective-permute-start(bf16[136,1024]{1,0:T(8,128)(2,1)} %get-tuple-element.142), channel_id=1, source_target_pairs={{2,0},{4,2},{6,4},{0,6},{3,1},{5,3},{7,5},{1,7},{10,8},{12,10},{14... | collective-permute-start | bytes 835592 | tf_op jit(solution)/shard_map/ppermute | solution.py:58
  217.1 23.1 %collective-permute-start.35 = (bf16[136,1024]{1,0:T(8,128)(2,1)}, bf16[136,1024]{1,0:T(8,128)(2,1)}, u32[]{:S(2)}, u32[]{:S(2)}) collective-permute-start(bf16[136,1024]{1,0:T(8,128)(2,1)} %get-tuple-element.144), channel_id=1, source_target_pairs={{6,0},{0,2},{2,4},{4,6},{7,1},{1,3},{3,5},{5,7},{14,8},{8,10},{10,... | collective-permute-start | bytes 835592 | tf_op jit(solution)/shard_map/ppermute | solution.py:58
  235.3 15.5 %collective-permute-start.45 = (bf16[519,512]{1,0:T(8,128)(2,1)}, bf16[519,512]{1,0:T(8,128)(2,1)S(1)}, u32[]{:S(2)}, u32[]{:S(2)}) collective-permute-start(bf16[519,512]{1,0:T(8,128)(2,1)} %pad_maximum_fusion.9), channel_id=1, source_target_pairs={{0,8},{8,0},{1,9},{9,1},{2,10},{10,2},{3,11},{11,3},{4,12},{12,4},... | collective-permute-start | bytes 1594376 | tf_op jit(solution)/shard_map/ppermute | solution.py:54
  238.6 13.5 %collective-permute-start.34 = (bf16[544,1024]{1,0:T(8,128)(2,1)}, bf16[544,1024]{1,0:T(8,128)(2,1)S(1)}, u32[]{:S(2)}, u32[]{:S(2)}) collective-permute-start(bf16[544,1024]{1,0:T(8,128)(2,1)} %convolution_convert_fusion), channel_id=1, source_target_pairs={{0,1},{1,0},{2,3},{3,2},{4,5},{5,4},{6,7},{7,6},{8,9},{9,8},{10,11... | collective-permute-start | bytes 3342344 | tf_op jit(solution)/shard_map/ppermute | solution.py:54
  238.9 11.9 %collective-permute-start.50 = (f32[2,512]{1,0:T(2,128)S(1)}, f32[2,512]{1,0:T(2,128)S(1)}, u32[]{:S(2)}, u32[]{:S(2)}) collective-permute-start(f32[2,512]{1,0:T(2,128)S(1)} %slice.469), channel_id=1, source_target_pairs={{0,8},{8,0},{1,9},{9,1},{2,10},{10,2},{3,11},{11,3},{4,12},{12,4},... | collective-permute-start | bytes 12296 | tf_op jit(solution)/shard_map/ppermute | solution.py:54
  255.3 12.9 %collective-permute-start.40 = (bf16[136,1024]{1,0:T(8,128)(2,1)S(1)}, bf16[136,1024]{1,0:T(8,128)(2,1)S(1)}, u32[]{:S(2)}, u32[]{:S(2)}) collective-permute-start(bf16[136,1024]{1,0:T(8,128)(2,1)S(1)} %get-tuple-element.50), channel_id=1, source_target_pairs={{2,0},{4,2},{6,4},{0,6},{3,1},{5,3},{7,5},{1,7},{10,8},{12,10},{14... | collective-permute-start | bytes 835592 | tf_op jit(solution)/shard_map/ppermute | solution.py:58
  258.0 12.1 %collective-permute-start.39 = (bf16[136,1024]{1,0:T(8,128)(2,1)S(1)}, bf16[136,1024]{1,0:T(8,128)(2,1)S(1)}, u32[]{:S(2)}, u32[]{:S(2)}) collective-permute-start(bf16[136,1024]{1,0:T(8,128)(2,1)S(1)} %get-tuple-element.49), channel_id=1, source_target_pairs={{4,0},{6,2},{0,4},{2,6},{5,1},{7,3},{1,5},{3,7},{12,8},{14,10},{8,... | collective-permute-start | bytes 835592 | tf_op jit(solution)/shard_map/ppermute | solution.py:58
  259.7 12.5 %collective-permute-start.38 = (bf16[136,1024]{1,0:T(8,128)(2,1)S(1)}, bf16[136,1024]{1,0:T(8,128)(2,1)S(1)}, u32[]{:S(2)}, u32[]{:S(2)}) collective-permute-start(bf16[136,1024]{1,0:T(8,128)(2,1)S(1)} %get-tuple-element.48), channel_id=1, source_target_pairs={{6,0},{0,2},{2,4},{4,6},{7,1},{1,3},{3,5},{5,7},{14,8},{8,10},{10,... | collective-permute-start | bytes 835592 | tf_op jit(solution)/shard_map/ppermute | solution.py:58
  261.0 19.3 %collective-permute-start.53 = (bf16[392,512]{1,0:T(8,128)(2,1)S(1)}, bf16[392,512]{1,0:T(8,128)(2,1)S(1)}, u32[]{:S(2)}, u32[]{:S(2)}) collective-permute-start(bf16[392,512]{1,0:T(8,128)(2,1)S(1)} %pad_maximum_fusion.12), channel_id=1, source_target_pairs={{32,0},{64,32},{96,64},{0,96},{33,1},{65,33},{97,65},{1,97},{34,2}... | collective-permute-start | bytes 1204232 | tf_op jit(solution)/shard_map/ppermute | solution.py:58
  265.1 15.1 %collective-permute-start.52 = (bf16[392,512]{1,0:T(8,128)(2,1)S(1)}, bf16[392,512]{1,0:T(8,128)(2,1)S(1)}, u32[]{:S(2)}, u32[]{:S(2)}) collective-permute-start(bf16[392,512]{1,0:T(8,128)(2,1)S(1)} %pad_maximum_fusion.11), channel_id=1, source_target_pairs={{64,0},{96,32},{0,64},{32,96},{65,1},{97,33},{1,65},{33,97},{66,2}... | collective-permute-start | bytes 1204232 | tf_op jit(solution)/shard_map/ppermute | solution.py:58
  268.2 15.8 %collective-permute-start.51 = (bf16[392,512]{1,0:T(8,128)(2,1)S(1)}, bf16[392,512]{1,0:T(8,128)(2,1)S(1)}, u32[]{:S(2)}, u32[]{:S(2)}) collective-permute-start(bf16[392,512]{1,0:T(8,128)(2,1)S(1)} %pad_maximum_fusion.10), channel_id=1, source_target_pairs={{96,0},{0,32},{32,64},{64,96},{97,1},{1,33},{33,65},{65,97},{98,2}... | collective-permute-start | bytes 1204232 | tf_op jit(solution)/shard_map/ppermute | solution.py:58
  270.1 15.3 %collective-permute-start.43 = (bf16[129,512]{1,0:T(8,128)(2,1)S(1)}, bf16[129,512]{1,0:T(8,128)(2,1)S(1)}, u32[]{:S(2)}, u32[]{:S(2)}) collective-permute-start(bf16[129,512]{1,0:T(8,128)(2,1)S(1)} %get-tuple-element.112), channel_id=1, source_target_pairs={{4,0},{5,1},{6,2},{7,3},{12,4},{13,5},{14,6},{15,7},{0,8},{1,9},{2... | collective-permute-start | bytes 396296 | tf_op jit(solution)/shard_map/ppermute | solution.py:75
  272.2 13.2 %collective-permute-start.44 = (bf16[129,512]{1,0:T(8,128)(2,1)S(1)}, bf16[129,512]{1,0:T(8,128)(2,1)S(1)}, u32[]{:S(2)}, u32[]{:S(2)}) collective-permute-start(bf16[129,512]{1,0:T(8,128)(2,1)S(1)} %get-tuple-element.113), channel_id=1, source_target_pairs={{8,4},{9,5},{10,6},{11,7},{4,8},{5,9},{6,10},{7,11},{24,20},{25,21... | collective-permute-start | bytes 396296 | tf_op jit(solution)/shard_map/ppermute | solution.py:76
  284.1 11.8 %collective-permute-start.54 = (bf16[392,512]{1,0:T(8,128)(2,1)S(1)}, bf16[392,512]{1,0:T(8,128)(2,1)S(1)}, u32[]{:S(2)}, u32[]{:S(2)}) collective-permute-start(bf16[392,512]{1,0:T(8,128)(2,1)S(1)} %fusion.20), channel_id=1, source_target_pairs={{0,16},{16,0},{1,17},{17,1},{2,18},{18,2},{3,19},{19,3},{4,20},{20... | collective-permute-start | bytes 1204232 | tf_op jit(solution)/shard_map/ppermute | solution.py:54
  285.5 14.7 %collective-permute-start.41 = (bf16[129,512]{1,0:T(8,128)(2,1)S(1)}, bf16[129,512]{1,0:T(8,128)(2,1)S(1)}, u32[]{:S(2)}, u32[]{:S(2)}) collective-permute-start(bf16[129,512]{1,0:T(8,128)(2,1)S(1)} %get-tuple-element.116), channel_id=1, source_target_pairs={{4,0},{5,1},{6,2},{7,3},{12,4},{13,5},{14,6},{15,7},{0,8},{1,9},{2... | collective-permute-start | bytes 396296 | tf_op jit(solution)/shard_map/ppermute | solution.py:75
  287.7 12.5 %collective-permute-start.42 = (bf16[129,512]{1,0:T(8,128)(2,1)S(1)}, bf16[129,512]{1,0:T(8,128)(2,1)S(1)}, u32[]{:S(2)}, u32[]{:S(2)}) collective-permute-start(bf16[129,512]{1,0:T(8,128)(2,1)S(1)} %get-tuple-element.117), channel_id=1, source_target_pairs={{8,4},{9,5},{10,6},{11,7},{4,8},{5,9},{6,10},{7,11},{24,20},{25,21... | collective-permute-start | bytes 396296 | tf_op jit(solution)/shard_map/ppermute | solution.py:76
  296.1 17.7 %collective-permute-start.57 = (bf16[392,512]{1,0:T(8,128)(2,1)S(1)}, bf16[392,512]{1,0:T(8,128)(2,1)S(1)}, u32[]{:S(2)}, u32[]{:S(2)}) collective-permute-start(bf16[392,512]{1,0:T(8,128)(2,1)S(1)} %add_convert_fusion), channel_id=1, source_target_pairs={{96,0},{0,32},{32,64},{64,96},{97,1},{1,33},{33,65},{65,97},{98,2}... | collective-permute-start | bytes 1204232 | tf_op jit(solution)/shard_map/ppermute | solution.py:58
  296.1 17.6 %collective-permute-start.56 = (bf16[392,512]{1,0:T(8,128)(2,1)S(1)}, bf16[392,512]{1,0:T(8,128)(2,1)S(1)}, u32[]{:S(2)}, u32[]{:S(2)}) collective-permute-start(bf16[392,512]{1,0:T(8,128)(2,1)S(1)} %add_convert_fusion), channel_id=1, source_target_pairs={{64,0},{96,32},{0,64},{32,96},{65,1},{97,33},{1,65},{33,97},{66,2}... | collective-permute-start | bytes 1204232 | tf_op jit(solution)/shard_map/ppermute | solution.py:58
  297.1 17.2 %collective-permute-start.55 = (bf16[392,512]{1,0:T(8,128)(2,1)S(1)}, bf16[392,512]{1,0:T(8,128)(2,1)S(1)}, u32[]{:S(2)}, u32[]{:S(2)}) collective-permute-start(bf16[392,512]{1,0:T(8,128)(2,1)S(1)} %add_convert_fusion), channel_id=1, source_target_pairs={{32,0},{64,32},{96,64},{0,96},{33,1},{65,33},{97,65},{1,97},{34,2}... | collective-permute-start | bytes 1204232 | tf_op jit(solution)/shard_map/ppermute | solution.py:58
  (110 other events, 720.3 us)

commit v2 on v1

--- a/solution.py
+++ b/solution.py
@@ -78,15 +78,24 @@
     return jnp.concatenate([jnp.where(home, own, moved), jnp.where(home, moved, crossed)], axis=0)
 
 
-def gather(piece):
+def gather(piece, *beside):
     near = jnp.concatenate([piece] + [pull(piece, "y", d) for d in (1, 2, 3)], axis=0)
+    near = after(near, *beside)
     return near, swap(near, "c")
 
 
-def scatter_begin(halves, weight, contract):
+def scatter_begin(halves, weight, contract, extra=None):
+    def product(half):
+        result = dot(half, weight, contract)
+        if extra is not None:
+            row = jnp.arange(NY * ROWS)[:, None] % ROWS - HALF
+            for i in range(extra.shape[0]):
+                result = jnp.where(row == i, extra[i], result)
+        return result
+
     near, far = halves
-    far = swap(dot(far, weight, contract).astype(BF), "c")
-    summed = dot(near, weight, contract) + far.astype(F32)
+    far = swap(product(far).astype(BF), "c")
+    summed = product(near) + far.astype(F32)
     return summed[:ROWS], [summed[d * ROWS : (d + 1) * ROWS].astype(BF) for d in (1, 2, 3)]
 
 
@@ -132,12 +141,6 @@
         return jnp.concatenate(slots, axis=0)
 
     return whole([piece[:split] for piece in pieces]), whole([piece[split:] for piece in pieces])
-
-
-def column_sum(values):
-    values = values + swap(values, "c")
-    opposite, later, earlier = (pull(values, "y", d) for d in (2, 1, 3))
-    return (values + opposite) + (later + earlier)
 
 
 def dot(first, second, contract):
@@ -260,7 +263,7 @@
     normed, scaled_first, inverse_first = norm(x, gains[0], shifts[0])
     normed_first = gather(normed)
     spare_rows = jnp.pad(own_rows[spare:], ((0, spare - 1), (0, 0)))
-    mine, theirs = place_in(after(cotangent, normed), spare_rows, home)
+    mine, theirs = place_in(after(cotangent, normed_first[0]), spare_rows, home)
     upstream = jnp.where(real, jnp.concatenate([mine, theirs], axis=1).astype(F32), 0.0)
     second_bias = theirs[HALF : HALF + 1]
     second_bias = jnp.concatenate([own_rows[spare:], second_bias], axis=1).astype(F32)
@@ -330,7 +333,7 @@
         scale_second,
     ]
     carried = jnp.concatenate([first_grad[:HALF], jnp.stack(vectors).astype(BF)], axis=0)
-    carried = gather(jnp.pad(carried, ((0, spare - 4), (0, 0))))
+    carried = gather(jnp.pad(carried, ((0, spare - 4), (0, 0))), fc1_sum)
     real = jnp.arange(NY * ROWS)[:, None] % ROWS < HALF
     first_full = [jnp.where(real, half, jnp.zeros((), BF)) for half in carried]
     spares = [half.reshape(NY, ROWS, D)[:, HALF : HALF + 4].astype(F32) for half in carried]
@@ -341,14 +344,9 @@
 
     mixture_grad = [dot(half, out_block, (1, 1)).astype(BF) for half in first_full]
     fc_sum = jnp.concatenate([fc1_sum, fc2_sum], axis=0)
-    mixture_grad = after(jnp.concatenate(mixture_grad, axis=0), fc_sum)
+    mixture_grad = jnp.concatenate(mixture_grad, axis=0)
     out_grad = sum(dot(one, two, (0, 0)) for one, two in zip(first_full, mixture_halves))
     packed_grad = attend_pull(packed, mask, mixture_grad)
-    packed_halves = packed_grad[:half_rows], packed_grad[half_rows:]
-    begun, sent = scatter_begin(packed_halves, qkv_weight, (1, 1))
-    arrived = [pull(piece, "y", -d) for d, piece in zip((1, 2, 3), sent)]
-    normed_grad = begun + sum(piece.astype(F32) for piece in arrived)
-    packed_grad = after(packed_grad, *sent)
     packed_halves = packed_grad[:half_rows], packed_grad[half_rows:]
     qkv_grad = sum(dot(one, two, (0, 0)) for one, two in zip(normed_first, packed_halves))
     totals = jnp.sum(packed_grad.astype(F32), axis=0)
@@ -368,23 +366,27 @@
     late_other = jnp.concatenate([late[D // 2 :], vectors[:, D // 2 :], other], axis=0)
     late_other = late_other.astype(BF)
     late = image_sum(late_own, late_other)
-    active = [after(half, late_other) for half in active]
-    branch_second, pieces = scatter_begin(active, fc2_weight, (1, 0))
-    normed_grad = after(normed_grad, *pieces)
-    branch_second = scatter_end(branch_second, after(pieces, normed_grad)) + second_bias
-    output = place_out(x + scales[1] * branch_second, home)
-    final = column_sum(after(jnp.stack([gain_part, shift_part]), late_other, arrived[1]))
+
+    final = jnp.stack([gain_part, shift_part])
+    packed_halves = after(packed_halves, late_other)
+    begun, sent = scatter_begin(packed_halves, qkv_weight, (1, 1), final)
+    normed_grad = scatter_end(begun, sent)
+    final = normed_grad[HALF : HALF + 2]
     final = final[:, : D // 2] + swap(final[:, D // 2 :], "xh")
     late = jnp.concatenate([late, final, jnp.zeros((32 - 9, D // 2), F32)], axis=0)
+    active = [after(half, normed_grad) for half in active]
+    begun, sent = scatter_begin(active, fc2_weight, (1, 0))
+    branch_second = scatter_end(begun, after(sent, late)) + second_bias
+    output = place_out(x + scales[1] * branch_second, home)
     first_pull = norm_pull(normed_grad, scaled_first, inverse_first, gains[0])
     input_grad = place_out(upstream + first_pull, home)
-    quarter = replica_scatter([fc_sum, after(late, normed_grad)])
+    quarter = replica_scatter([fc_sum, late])
     quarter = after(quarter, branch_second, first_pull)
     fc_sum, late = replica_gather(quarter, fc_sum.shape[0] // NZ)
 
     qkv_grad = late[: D // 2, :384].reshape(D // 2, 3, 2, HD).transpose(0, 2, 1, 3)
     out_grad = late[: D // 2, 384:].T
-    vectors = late[D // 2 : D // 2 + 9]
+    vectors, final = late[D // 2 : D // 2 + 7], late[D // 2 + 7 : D // 2 + 9]
     small = vectors[6]
     return (
         output,
@@ -395,8 +397,8 @@
         fc_sum[None, : D // 2],
         small[:256].reshape(1, 1, 1, -1),
         fc_sum[None, D // 2 :],
-        jnp.stack([vectors[7], vectors[0]])[None],
-        jnp.stack([vectors[8], vectors[1]])[None],
+        jnp.stack([final[0], vectors[0]])[None],
+        jnp.stack([final[1], vectors[1]])[None],
         vectors[2:4][None],
         vectors[4:6][None],
     )

time: 330 us -> 307 us (0.930)
  local copies, waits for them, and re-layouts: 35.1 us -> 19.7 us
  matrix products: 35.3 us -> 25.9 us
  waiting for transfers between devices: 117 us -> 123 us
  other arithmetic: 30.8 us -> 27.5 us
    unnamed x210 -> x108, local copies, waits for them, and re-layouts: 19.4 us -> 8.38 us
    ppermute x17 -> x16, starting transfers between devices: 10.6 us -> 20.4 us  [swap(): return lax.ppermute(value, axis, [(0, 1), (1, 0)])]
    dot_general x24, matrix products: 35.3 us -> 25.9 us  [dot(): lax.dot_general(first, second, (((contract[0],), (contract[1],)), ((), ()...]
    ppermute x33 -> x30, starting transfers between devices: 49 us -> 40.1 us  [pull(): lax.ppermute(value, axis, [((i + distance) % 4, i) for i in range(4)])]
    ppermute x17 -> x16, waiting for transfers between devices: 32.7 us -> 23.9 us  [swap(): return lax.ppermute(value, axis, [(0, 1), (1, 0)])]
    ppermute x2, waiting for transfers between devices: 3.71 us -> 9.83 us  [place_in(): crossed = lax.ppermute(second, GROUP, ENTRY_SECOND)]
    ppermute x2, waiting for transfers between devices: 0.01 us -> 4.54 us  [place_out(): crossed = lax.ppermute(other, GROUP, EXIT_SECOND)]
    ppermute x33 -> x30, waiting for transfers between devices: 80.4 us -> 84.6 us  [pull(): lax.ppermute(value, axis, [((i + distance) % 4, i) for i in range(4)])]
  transfers between devices with their start and end apart: 58 -> 54, of which waited for: 28 -> 29; matrix products, arithmetic and copies ran while one was open for 20% -> 12% of each run, Pallas kernels for 0% -> 0%
where the time goes in v2:
time: 307 us; the launch traced here: 302 us
  waiting for transfers between devices  123 us (40%)
  starting transfers between devices  86.5 us (28%)
  other arithmetic  27.5 us (9%)
  matrix products  25.9 us (8%)
  local copies, waits for them, and re-layouts  19.7 us (6%)
  Pallas kernels  17 us (6%)
    ppermute x30, waiting for transfers between devices, pull(): lax.ppermute(value, axis, [((i + distance) % 4, i) for i in range(4)])  84.6 us
    ppermute x30, starting transfers between devices, pull(): lax.ppermute(value, axis, [((i + distance) % 4, i) for i in range(4)])  40.1 us
    dot_general x24, matrix products, dot(): lax.dot_general(first, second, (((contract[0],), (contract[1],)), ((), ()...  25.9 us
    ppermute x16, waiting for transfers between devices, swap(): return lax.ppermute(value, axis, [(0, 1), (1, 0)])  23.9 us
    ppermute x16, starting transfers between devices, swap(): return lax.ppermute(value, axis, [(0, 1), (1, 0)])  20.4 us
    pallas_call x2, Pallas kernels, local_kernel(): pl.pallas_call(kernel, out_shape=jax.ShapeDtypeStruct((SLOTS * ROWS, widt...  17 us
    ppermute x2, starting transfers between devices, place_in(): crossed = lax.ppermute(second, GROUP, ENTRY_SECOND)  11.6 us
    ppermute x2, waiting for transfers between devices, place_in(): crossed = lax.ppermute(second, GROUP, ENTRY_SECOND)  9.83 us
  transfers between devices with their start and end apart: 54, of which 29 were waited for; matrix products, arithmetic and copies ran while one was open for 12% of the time, Pallas kernels for 0%

profile of v2, /device:TPU:4, one launch (start us, length us, event | category | flops | bytes accessed | tf_op | source)
XLA Modules:
  0.0 301.9 jit_solution(12536859488377934366)
XLA Ops:
  3.0 7.6 %collective-permute-start.1 = (bf16[136,512]{1,0:T(8,128)(2,1)S(1)}, bf16[136,512]{1,0:T(8,128)(2,1)S(1)}, u32[]{:S(2)}, u32[]{:S(2)}) collective-permute-start(bf16[136,512]{1,0:T(8,128)(2,1)S(1)} %get-tuple-element.162), channel_id=1, source_target_pairs={{4,8},{5,9},{6,10},{7,11},{8,4},{9,5},{10,6},{11,7},{20,24},{21,25... | collective-permute-start | bytes 417800 | tf_op jit(solution)/shard_map/ppermute | solution.py:69
  10.7 4.5 %collective-permute-done.1 = bf16[136,512]{1,0:T(8,128)(2,1)S(1)} collective-permute-done((bf16[136,512]{1,0:T(8,128)(2,1)S(1)}, bf16[136,512]{1,0:T(8,128)(2,1)S(1)}, u32[]{:S(2)}, u32[]{:S(2)}) %collective-permute-start.1) | collective-permute-done | bytes 139296 | tf_op jit(solution)/shard_map/ppermute | solution.py:69
  16.8 2.8 collective-permute-start.2
  20.6 4.4 %collective-permute-start.5 = (bf16[528,512]{1,0:T(8,128)(2,1)}, bf16[528,512]{1,0:T(8,128)(2,1)}, u32[]{:S(2)}, u32[]{:S(2)}) collective-permute-start(bf16[528,512]{1,0:T(8,128)(2,1)} %fusion.35), channel_id=1, source_target_pairs={{0,8},{8,0},{1,9},{9,1},{2,10},{10,2},{3,11},{11,3},{4,12},{12,4},... | collective-permute-start | bytes 1622024 | tf_op jit(solution)/shard_map/ppermute | solution.py:54
  25.0 5.9 %collective-permute-done.4 = bf16[136,1024]{1,0:T(8,128)(2,1)S(1)} collective-permute-done((bf16[136,1024]{1,0:T(8,128)(2,1)S(1)}, bf16[136,1024]{1,0:T(8,128)(2,1)S(1)}, u32[]{:S(2)}, u32[]{:S(2)}) %collective-permute-start.4) | collective-permute-done | bytes 278560 | tf_op jit(solution)/shard_map/ppermute | solution.py:58
  31.7 2.3 collective-permute-start.8
  33.9 3.9 %collective-permute-start.9 = (bf16[136,512]{1,0:T(8,128)(2,1)S(1)}, bf16[136,512]{1,0:T(8,128)(2,1)S(1)}, u32[]{:S(2)}, u32[]{:S(2)}) collective-permute-start(bf16[136,512]{1,0:T(8,128)(2,1)S(1)} %get-tuple-element.164), channel_id=1, source_target_pairs={{4,8},{5,9},{6,10},{7,11},{8,4},{9,5},{10,6},{11,7},{20,24},{21,25... | collective-permute-start | bytes 417800 | tf_op jit(solution)/shard_map/ppermute | solution.py:69
  39.5 5.4 %collective-permute-done.9 = bf16[136,512]{1,0:T(8,128)(2,1)S(1)} collective-permute-done((bf16[136,512]{1,0:T(8,128)(2,1)S(1)}, bf16[136,512]{1,0:T(8,128)(2,1)S(1)}, u32[]{:S(2)}, u32[]{:S(2)}) %collective-permute-start.9) | collective-permute-done | bytes 139296 | tf_op jit(solution)/shard_map/ppermute | solution.py:69
  47.0 2.7 collective-permute-start.10
  56.4 3.1 %collective-permute-done.12 = bf16[136,1024]{1,0:T(8,128)(2,1)} collective-permute-done((bf16[136,1024]{1,0:T(8,128)(2,1)}, bf16[136,1024]{1,0:T(8,128)(2,1)}, u32[]{:S(2)}, u32[]{:S(2)}) %collective-permute-start.12) | collective-permute-done | bytes 278560 | tf_op jit(solution)/shard_map/ppermute | solution.py:58
  60.8 2.4 fusion.3
  63.3 2.5 collective-permute-done.7
  65.8 4.8 %shard_map.211 = bf16[1088,128]{1,0:T(8,128)(2,1)S(1)} custom-call(f32[1,1088]{1,0:T(1,128)S(1)} %compare_convert_fusion.mask_ref, bf16[1088,384]{1,0:T(8,128)(2,1)S(1)} %pad_maximum_fusion.7.packed_ref), custom_call_target="tpu_custom_call" | custom-call | flops 8000000000 | bytes 24000000 | tf_op jit(solution)/shard_map/pallas_call | solution.py:211
  71.1 2.7 collective-permute-done.13
  76.7 3.3 %collective-permute-start.17 = (bf16[512,512]{1,0:T(8,128)(2,1)S(1)}, bf16[512,512]{1,0:T(8,128)(2,1)S(1)}, u32[]{:S(2)}, u32[]{:S(2)}) collective-permute-start(bf16[512,512]{1,0:T(8,128)(2,1)S(1)} %bitcast.111), channel_id=1, source_target_pairs={{0,8},{8,0},{1,9},{9,1},{2,10},{10,2},{3,11},{11,3},{4,12},{12,4},... | collective-permute-start | bytes 1572872 | tf_op jit(solution)/shard_map/ppermute | solution.py:54
  80.0 3.9 %collective-permute-done.16 = bf16[136,1024]{1,0:T(8,128)(2,1)S(1)} collective-permute-done((bf16[136,1024]{1,0:T(8,128)(2,1)S(1)}, bf16[136,1024]{1,0:T(8,128)(2,1)S(1)}, u32[]{:S(2)}, u32[]{:S(2)}) %collective-permute-start.16) | collective-permute-done | bytes 278560 | tf_op jit(solution)/shard_map/ppermute | solution.py:58
  83.9 2.7 collective-permute-done.15
  86.6 4.8 %collective-permute-done.14 = bf16[136,1024]{1,0:T(8,128)(2,1)S(1)} collective-permute-done((bf16[136,1024]{1,0:T(8,128)(2,1)S(1)}, bf16[136,1024]{1,0:T(8,128)(2,1)S(1)}, u32[]{:S(2)}, u32[]{:S(2)}) %collective-permute-start.14) | collective-permute-done | bytes 278560 | tf_op jit(solution)/shard_map/ppermute | solution.py:58
  92.6 2.4 collective-permute-start.21
  94.9 2.4 collective-permute-start.20
  99.1 3.4 %collective-permute-done.21 = bf16[136,1024]{1,0:T(8,128)(2,1)S(1)} collective-permute-done((bf16[136,1024]{1,0:T(8,128)(2,1)S(1)}, bf16[136,1024]{1,0:T(8,128)(2,1)S(1)}, u32[]{:S(2)}, u32[]{:S(2)}) %collective-permute-start.21) | collective-permute-done | bytes 278560 | tf_op jit(solution)/shard_map/ppermute | solution.py:58
  102.5 7.1 %collective-permute-done.20 = bf16[136,1024]{1,0:T(8,128)(2,1)S(1)} collective-permute-done((bf16[136,1024]{1,0:T(8,128)(2,1)S(1)}, bf16[136,1024]{1,0:T(8,128)(2,1)S(1)}, u32[]{:S(2)}, u32[]{:S(2)}) %collective-permute-start.20) | collective-permute-done | bytes 278560 | tf_op jit(solution)/shard_map/ppermute | solution.py:58
  120.8 2.2 collective-permute-start.26
  129.4 6.1 %collective-permute-done.26 = bf16[136,1024]{1,0:T(8,128)(2,1)S(1)} collective-permute-done((bf16[136,1024]{1,0:T(8,128)(2,1)S(1)}, bf16[136,1024]{1,0:T(8,128)(2,1)S(1)}, u32[]{:S(2)}, u32[]{:S(2)}) %collective-permute-start.26) | collective-permute-done | bytes 278560 | tf_op jit(solution)/shard_map/ppermute | solution.py:58
  135.5 3.7 %collective-permute-done.24 = bf16[136,1024]{1,0:T(8,128)(2,1)S(1)} collective-permute-done((bf16[136,1024]{1,0:T(8,128)(2,1)S(1)}, bf16[136,1024]{1,0:T(8,128)(2,1)S(1)}, u32[]{:S(2)}, u32[]{:S(2)}) %collective-permute-start.24) | collective-permute-done | bytes 278560 | tf_op jit(solution)/shard_map/ppermute | solution.py:58
  140.1 2.2 collective-permute-done.27
  143.5 2.2 collective-permute-start.31
  146.1 2.3 collective-permute-start.30
  152.7 3.7 %collective-permute-done.30 = bf16[136,1024]{1,0:T(8,128)(2,1)S(1)} collective-permute-done((bf16[136,1024]{1,0:T(8,128)(2,1)S(1)}, bf16[136,1024]{1,0:T(8,128)(2,1)S(1)}, u32[]{:S(2)}, u32[]{:S(2)}) %collective-permute-start.30) | collective-permute-done | bytes 278560 | tf_op jit(solution)/shard_map/ppermute | solution.py:58
  156.5 5.1 %collective-permute-done.29 = bf16[136,1024]{1,0:T(8,128)(2,1)} collective-permute-done((bf16[136,1024]{1,0:T(8,128)(2,1)S(1)}, bf16[136,1024]{1,0:T(8,128)(2,1)}, u32[]{:S(2)}, u32[]{:S(2)}) %collective-permute-start.29) | collective-permute-done | bytes 278560 | tf_op jit(solution)/shard_map/ppermute | solution.py:58
  162.7 2.6 slice_add_fusion
  169.9 12.3 %shard_map.212 = bf16[1088,384]{1,0:T(8,128)(2,1)S(1)} custom-call(f32[1,1088]{1,0:T(1,128)S(1)} %compare_convert_fusion.mask_ref, bf16[1088,384]{1,0:T(8,128)(2,1)S(1)} %pad_maximum_fusion.7.packed_ref, bf16[1088,128]{1,0:T(8,128)(2,1)S(1)} %pad_maximum_fusion.16.grad_ref), custom_call_target="tpu_custom_call" | custom-call | flops 12000000000 | bytes 36000000 | tf_op jit(solution)/shard_map/pallas_call | solution.py:211
  186.8 2.3 fusion.76
  198.8 2.3 fusion.96
  201.2 2.7 collective-permute-start.36
  204.8 9.3 %collective-permute-done.38 = bf16[519,512]{1,0:T(8,128)(2,1)S(1)} collective-permute-done((bf16[519,512]{1,0:T(8,128)(2,1)}, bf16[519,512]{1,0:T(8,128)(2,1)S(1)}, u32[]{:S(2)}, u32[]{:S(2)}) %collective-permute-start.38) | collective-permute-done | bytes 531488 | tf_op jit(solution)/shard_map/ppermute | solution.py:54
  216.2 3.7 %collective-permute-done.34 = bf16[136,1024]{1,0:T(8,128)(2,1)S(1)} collective-permute-done((bf16[136,1024]{1,0:T(8,128)(2,1)S(1)}, bf16[136,1024]{1,0:T(8,128)(2,1)S(1)}, u32[]{:S(2)}, u32[]{:S(2)}) %collective-permute-start.34) | collective-permute-done | bytes 278560 | tf_op jit(solution)/shard_map/ppermute | solution.py:58
  222.1 2.6 collective-permute-start.39
  225.0 2.2 collective-permute-done.39
  228.3 4.3 %collective-permute-start.49 = (bf16[392,512]{1,0:T(8,128)(2,1)S(1)}, bf16[392,512]{1,0:T(8,128)(2,1)S(1)}, u32[]{:S(2)}, u32[]{:S(2)}) collective-permute-start(bf16[392,512]{1,0:T(8,128)(2,1)S(1)} %pad_maximum_fusion.13), channel_id=1, source_target_pairs={{32,0},{64,32},{96,64},{0,96},{33,1},{65,33},{97,65},{1,97},{34,2}... | collective-permute-start | bytes 1204232 | tf_op jit(solution)/shard_map/ppermute | solution.py:58
  236.3 13.0 %collective-permute-done.49 = bf16[392,512]{1,0:T(8,128)(2,1)S(1)} collective-permute-done((bf16[392,512]{1,0:T(8,128)(2,1)S(1)}, bf16[392,512]{1,0:T(8,128)(2,1)S(1)}, u32[]{:S(2)}, u32[]{:S(2)}) %collective-permute-start.49) | collective-permute-done | bytes 401440 | tf_op jit(solution)/shard_map/ppermute | solution.py:58
  252.9 5.0 %collective-permute-start.46 = (bf16[129,512]{1,0:T(8,128)(2,1)S(1)}, bf16[129,512]{1,0:T(8,128)(2,1)S(1)}, u32[]{:S(2)}, u32[]{:S(2)}) collective-permute-start(bf16[129,512]{1,0:T(8,128)(2,1)S(1)} %get-tuple-element.109), channel_id=1, source_target_pairs={{8,4},{9,5},{10,6},{11,7},{4,8},{5,9},{6,10},{7,11},{24,20},{25,21... | collective-permute-start | bytes 396296 | tf_op jit(solution)/shard_map/ppermute | solution.py:76
  258.4 2.3 collective-permute-start.50
  260.7 4.5 %collective-permute-done.46 = bf16[129,512]{1,0:T(8,128)(2,1)S(1)} collective-permute-done((bf16[129,512]{1,0:T(8,128)(2,1)S(1)}, bf16[129,512]{1,0:T(8,128)(2,1)S(1)}, u32[]{:S(2)}, u32[]{:S(2)}) %collective-permute-start.46) | collective-permute-done | bytes 132128 | tf_op jit(solution)/shard_map/ppermute | solution.py:76
  265.4 4.3 %collective-permute-start.44 = (bf16[129,512]{1,0:T(8,128)(2,1)S(1)}, bf16[129,512]{1,0:T(8,128)(2,1)S(1)}, u32[]{:S(2)}, u32[]{:S(2)}) collective-permute-start(bf16[129,512]{1,0:T(8,128)(2,1)S(1)} %get-tuple-element.114), channel_id=1, source_target_pairs={{8,4},{9,5},{10,6},{11,7},{4,8},{5,9},{6,10},{7,11},{24,20},{25,21... | collective-permute-start | bytes 396296 | tf_op jit(solution)/shard_map/ppermute | solution.py:76
  269.7 3.3 %collective-permute-done.50 = bf16[392,512]{1,0:T(8,128)(2,1)S(1)} collective-permute-done((bf16[392,512]{1,0:T(8,128)(2,1)S(1)}, bf16[392,512]{1,0:T(8,128)(2,1)S(1)}, u32[]{:S(2)}, u32[]{:S(2)}) %collective-permute-start.50) | collective-permute-done | bytes 401440 | tf_op jit(solution)/shard_map/ppermute | solution.py:54
  273.3 2.7 collective-permute-start.52
  278.2 14.0 %collective-permute-done.53 = bf16[392,512]{1,0:T(8,128)(2,1)S(1)} collective-permute-done((bf16[392,512]{1,0:T(8,128)(2,1)S(1)}, bf16[392,512]{1,0:T(8,128)(2,1)S(1)}, u32[]{:S(2)}, u32[]{:S(2)}) %collective-permute-start.53) | collective-permute-done | bytes 401440 | tf_op jit(solution)/shard_map/ppermute | solution.py:58
  (346 shorter events, 93.6 us)
Async XLA Ops:
  2.5 8.2 %collective-permute-start = (bf16[136,512]{1,0:T(8,128)(2,1)S(1)}, bf16[136,512]{1,0:T(8,128)(2,1)S(1)}, u32[]{:S(2)}, u32[]{:S(2)}) collective-permute-start(bf16[136,512]{1,0:T(8,128)(2,1)S(1)} %get-tuple-element.163), channel_id=1, source_target_pairs={{0,4},{1,5},{2,6},{3,7},{4,12},{5,13},{6,14},{7,15},{8,0},{9,1},{1... | collective-permute-start | bytes 417800 | tf_op jit(solution)/shard_map/ppermute | solution.py:68
  3.0 12.2 %collective-permute-start.1 = (bf16[136,512]{1,0:T(8,128)(2,1)S(1)}, bf16[136,512]{1,0:T(8,128)(2,1)S(1)}, u32[]{:S(2)}, u32[]{:S(2)}) collective-permute-start(bf16[136,512]{1,0:T(8,128)(2,1)S(1)} %get-tuple-element.162), channel_id=1, source_target_pairs={{4,8},{5,9},{6,10},{7,11},{8,4},{9,5},{10,6},{11,7},{20,24},{21,25... | collective-permute-start | bytes 417800 | tf_op jit(solution)/shard_map/ppermute | solution.py:69
  16.1 14.7 %collective-permute-start.4 = (bf16[136,1024]{1,0:T(8,128)(2,1)S(1)}, bf16[136,1024]{1,0:T(8,128)(2,1)S(1)}, u32[]{:S(2)}, u32[]{:S(2)}) collective-permute-start(bf16[136,1024]{1,0:T(8,128)(2,1)S(1)} %add_convert_fusion.2), channel_id=1, source_target_pairs={{6,0},{0,2},{2,4},{4,6},{7,1},{1,3},{3,5},{5,7},{14,8},{8,10},{10,... | collective-permute-start | bytes 835592 | tf_op jit(solution)/shard_map/ppermute | solution.py:58
  16.8 14.1 %collective-permute-start.3 = (bf16[136,1024]{1,0:T(8,128)(2,1)S(1)}, bf16[136,1024]{1,0:T(8,128)(2,1)S(1)}, u32[]{:S(2)}, u32[]{:S(2)}) collective-permute-start(bf16[136,1024]{1,0:T(8,128)(2,1)S(1)} %add_convert_fusion.2), channel_id=1, source_target_pairs={{4,0},{6,2},{0,4},{2,6},{5,1},{7,3},{1,5},{3,7},{12,8},{14,10},{8,... | collective-permute-start | bytes 835592 | tf_op jit(solution)/shard_map/ppermute | solution.py:58
  16.8 14.7 %collective-permute-start.2 = (bf16[136,1024]{1,0:T(8,128)(2,1)S(1)}, bf16[136,1024]{1,0:T(8,128)(2,1)S(1)}, u32[]{:S(2)}, u32[]{:S(2)}) collective-permute-start(bf16[136,1024]{1,0:T(8,128)(2,1)S(1)} %add_convert_fusion.2), channel_id=1, source_target_pairs={{2,0},{4,2},{6,4},{0,6},{3,1},{5,3},{7,5},{1,7},{10,8},{12,10},{14... | collective-permute-start | bytes 835592 | tf_op jit(solution)/shard_map/ppermute | solution.py:58
  20.6 29.1 %collective-permute-start.5 = (bf16[528,512]{1,0:T(8,128)(2,1)}, bf16[528,512]{1,0:T(8,128)(2,1)}, u32[]{:S(2)}, u32[]{:S(2)}) collective-permute-start(bf16[528,512]{1,0:T(8,128)(2,1)} %fusion.35), channel_id=1, source_target_pairs={{0,8},{8,0},{1,9},{9,1},{2,10},{10,2},{3,11},{11,3},{4,12},{12,4},... | collective-permute-start | bytes 1622024 | tf_op jit(solution)/shard_map/ppermute | solution.py:54
  31.7 7.8 %collective-permute-start.8 = (bf16[136,512]{1,0:T(8,128)(2,1)S(1)}, bf16[136,512]{1,0:T(8,128)(2,1)S(1)}, u32[]{:S(2)}, u32[]{:S(2)}) collective-permute-start(bf16[136,512]{1,0:T(8,128)(2,1)S(1)} %get-tuple-element.165), channel_id=1, source_target_pairs={{0,4},{1,5},{2,6},{3,7},{4,12},{5,13},{6,14},{7,15},{8,0},{9,1},{1... | collective-permute-start | bytes 417800 | tf_op jit(solution)/shard_map/ppermute | solution.py:68
  33.9 11.0 %collective-permute-start.9 = (bf16[136,512]{1,0:T(8,128)(2,1)S(1)}, bf16[136,512]{1,0:T(8,128)(2,1)S(1)}, u32[]{:S(2)}, u32[]{:S(2)}) collective-permute-start(bf16[136,512]{1,0:T(8,128)(2,1)S(1)} %get-tuple-element.164), channel_id=1, source_target_pairs={{4,8},{5,9},{6,10},{7,11},{8,4},{9,5},{10,6},{11,7},{20,24},{21,25... | collective-permute-start | bytes 417800 | tf_op jit(solution)/shard_map/ppermute | solution.py:69
  39.5 21.3 %collective-permute-start.6 = (bf16[544,1024]{1,0:T(8,128)(2,1)S(1)}, bf16[544,1024]{1,0:T(8,128)(2,1)}, u32[]{:S(2)}, u32[]{:S(2)}) collective-permute-start(bf16[544,1024]{1,0:T(8,128)(2,1)S(1)} %pad_maximum_fusion), channel_id=1, source_target_pairs={{0,1},{1,0},{2,3},{3,2},{4,5},{5,4},{6,7},{7,6},{8,9},{9,8},{10,11... | collective-permute-start | bytes 3342344 | tf_op jit(solution)/shard_map/ppermute | solution.py:54
  45.8 13.6 %collective-permute-start.12 = (bf16[136,1024]{1,0:T(8,128)(2,1)}, bf16[136,1024]{1,0:T(8,128)(2,1)}, u32[]{:S(2)}, u32[]{:S(2)}) collective-permute-start(bf16[136,1024]{1,0:T(8,128)(2,1)} %get-tuple-element.34), channel_id=1, source_target_pairs={{6,0},{0,2},{2,4},{4,6},{7,1},{1,3},{3,5},{5,7},{14,8},{8,10},{10,... | collective-permute-start | bytes 835592 | tf_op jit(solution)/shard_map/ppermute | solution.py:58
  47.0 12.5 %collective-permute-start.11 = (bf16[136,1024]{1,0:T(8,128)(2,1)}, bf16[136,1024]{1,0:T(8,128)(2,1)}, u32[]{:S(2)}, u32[]{:S(2)}) collective-permute-start(bf16[136,1024]{1,0:T(8,128)(2,1)} %get-tuple-element.34), channel_id=1, source_target_pairs={{4,0},{6,2},{0,4},{2,6},{5,1},{7,3},{1,5},{3,7},{12,8},{14,10},{8,... | collective-permute-start | bytes 835592 | tf_op jit(solution)/shard_map/ppermute | solution.py:58
  47.0 12.5 %collective-permute-start.10 = (bf16[136,1024]{1,0:T(8,128)(2,1)}, bf16[136,1024]{1,0:T(8,128)(2,1)}, u32[]{:S(2)}, u32[]{:S(2)}) collective-permute-start(bf16[136,1024]{1,0:T(8,128)(2,1)} %get-tuple-element.34), channel_id=1, source_target_pairs={{2,0},{4,2},{6,4},{0,6},{3,1},{5,3},{7,5},{1,7},{10,8},{12,10},{14... | collective-permute-start | bytes 835592 | tf_op jit(solution)/shard_map/ppermute | solution.py:58
  52.8 12.9 %collective-permute-start.7 = (bf16[512,512]{1,0:T(8,128)(2,1)S(1)}, bf16[512,512]{1,0:T(8,128)(2,1)S(1)}, u32[]{:S(2)}, u32[]{:S(2)}) collective-permute-start(bf16[512,512]{1,0:T(8,128)(2,1)S(1)} %bitcast.128), channel_id=1, source_target_pairs={{0,8},{8,0},{1,9},{9,1},{2,10},{10,2},{3,11},{11,3},{4,12},{12,4},... | collective-permute-start | bytes 1572872 | tf_op jit(solution)/shard_map/ppermute | solution.py:54
  74.3 9.6 %collective-permute-start.16 = (bf16[136,1024]{1,0:T(8,128)(2,1)S(1)}, bf16[136,1024]{1,0:T(8,128)(2,1)S(1)}, u32[]{:S(2)}, u32[]{:S(2)}) collective-permute-start(bf16[136,1024]{1,0:T(8,128)(2,1)S(1)} %get-tuple-element.146), channel_id=1, source_target_pairs={{2,0},{4,2},{6,4},{0,6},{3,1},{5,3},{7,5},{1,7},{10,8},{12,10},{14... | collective-permute-start | bytes 835592 | tf_op jit(solution)/shard_map/ppermute | solution.py:58
  75.5 11.1 %collective-permute-start.15 = (bf16[136,1024]{1,0:T(8,128)(2,1)S(1)}, bf16[136,1024]{1,0:T(8,128)(2,1)S(1)}, u32[]{:S(2)}, u32[]{:S(2)}) collective-permute-start(bf16[136,1024]{1,0:T(8,128)(2,1)S(1)} %get-tuple-element.147), channel_id=1, source_target_pairs={{4,0},{6,2},{0,4},{2,6},{5,1},{7,3},{1,5},{3,7},{12,8},{14,10},{8,... | collective-permute-start | bytes 835592 | tf_op jit(solution)/shard_map/ppermute | solution.py:58
  76.7 14.7 %collective-permute-start.14 = (bf16[136,1024]{1,0:T(8,128)(2,1)S(1)}, bf16[136,1024]{1,0:T(8,128)(2,1)S(1)}, u32[]{:S(2)}, u32[]{:S(2)}) collective-permute-start(bf16[136,1024]{1,0:T(8,128)(2,1)S(1)} %get-tuple-element.145), channel_id=1, source_target_pairs={{6,0},{0,2},{2,4},{4,6},{7,1},{1,3},{3,5},{5,7},{14,8},{8,10},{10,... | collective-permute-start | bytes 835592 | tf_op jit(solution)/shard_map/ppermute | solution.py:58
  76.7 15.9 %collective-permute-start.18 = (bf16[544,1024]{1,0:T(8,128)(2,1)S(1)}, bf16[544,1024]{1,0:T(8,128)(2,1)S(1)}, u32[]{:S(2)}, u32[]{:S(2)}) collective-permute-start(bf16[544,1024]{1,0:T(8,128)(2,1)S(1)} %pad_maximum_fusion.1), channel_id=1, source_target_pairs={{0,1},{1,0},{2,3},{3,2},{4,5},{5,4},{6,7},{7,6},{8,9},{9,8},{10,11... | collective-permute-start | bytes 3342344 | tf_op jit(solution)/shard_map/ppermute | solution.py:54
  76.7 15.9 %collective-permute-start.17 = (bf16[512,512]{1,0:T(8,128)(2,1)S(1)}, bf16[512,512]{1,0:T(8,128)(2,1)S(1)}, u32[]{:S(2)}, u32[]{:S(2)}) collective-permute-start(bf16[512,512]{1,0:T(8,128)(2,1)S(1)} %bitcast.111), channel_id=1, source_target_pairs={{0,8},{8,0},{1,9},{9,1},{2,10},{10,2},{3,11},{11,3},{4,12},{12,4},... | collective-permute-start | bytes 1572872 | tf_op jit(solution)/shard_map/ppermute | solution.py:54
  92.6 9.9 %collective-permute-start.21 = (bf16[136,1024]{1,0:T(8,128)(2,1)S(1)}, bf16[136,1024]{1,0:T(8,128)(2,1)S(1)}, u32[]{:S(2)}, u32[]{:S(2)}) collective-permute-start(bf16[136,1024]{1,0:T(8,128)(2,1)S(1)} %add_convert_fusion.1), channel_id=1, source_target_pairs={{6,0},{0,2},{2,4},{4,6},{7,1},{1,3},{3,5},{5,7},{14,8},{8,10},{10,... | collective-permute-start | bytes 835592 | tf_op jit(solution)/shard_map/ppermute | solution.py:58
  94.9 14.6 %collective-permute-start.20 = (bf16[136,1024]{1,0:T(8,128)(2,1)S(1)}, bf16[136,1024]{1,0:T(8,128)(2,1)S(1)}, u32[]{:S(2)}, u32[]{:S(2)}) collective-permute-start(bf16[136,1024]{1,0:T(8,128)(2,1)S(1)} %add_convert_fusion.1), channel_id=1, source_target_pairs={{4,0},{6,2},{0,4},{2,6},{5,1},{7,3},{1,5},{3,7},{12,8},{14,10},{8,... | collective-permute-start | bytes 835592 | tf_op jit(solution)/shard_map/ppermute | solution.py:58
  97.3 12.2 %collective-permute-start.19 = (bf16[136,1024]{1,0:T(8,128)(2,1)S(1)}, bf16[136,1024]{1,0:T(8,128)(2,1)S(1)}, u32[]{:S(2)}, u32[]{:S(2)}) collective-permute-start(bf16[136,1024]{1,0:T(8,128)(2,1)S(1)} %add_convert_fusion.1), channel_id=1, source_target_pairs={{2,0},{4,2},{6,4},{0,6},{3,1},{5,3},{7,5},{1,7},{10,8},{12,10},{14... | collective-permute-start | bytes 835592 | tf_op jit(solution)/shard_map/ppermute | solution.py:58
  120.8 14.7 %collective-permute-start.26 = (bf16[136,1024]{1,0:T(8,128)(2,1)S(1)}, bf16[136,1024]{1,0:T(8,128)(2,1)S(1)}, u32[]{:S(2)}, u32[]{:S(2)}) collective-permute-start(bf16[136,1024]{1,0:T(8,128)(2,1)S(1)} %get-tuple-element.143), channel_id=1, source_target_pairs={{2,0},{4,2},{6,4},{0,6},{3,1},{5,3},{7,5},{1,7},{10,8},{12,10},{14... | collective-permute-start | bytes 835592 | tf_op jit(solution)/shard_map/ppermute | solution.py:58
  123.1 12.4 %collective-permute-start.25 = (bf16[136,1024]{1,0:T(8,128)(2,1)S(1)}, bf16[136,1024]{1,0:T(8,128)(2,1)S(1)}, u32[]{:S(2)}, u32[]{:S(2)}) collective-permute-start(bf16[136,1024]{1,0:T(8,128)(2,1)S(1)} %get-tuple-element.144), channel_id=1, source_target_pairs={{4,0},{6,2},{0,4},{2,6},{5,1},{7,3},{1,5},{3,7},{12,8},{14,10},{8,... | collective-permute-start | bytes 835592 | tf_op jit(solution)/shard_map/ppermute | solution.py:58
  124.2 15.0 %collective-permute-start.24 = (bf16[136,1024]{1,0:T(8,128)(2,1)S(1)}, bf16[136,1024]{1,0:T(8,128)(2,1)S(1)}, u32[]{:S(2)}, u32[]{:S(2)}) collective-permute-start(bf16[136,1024]{1,0:T(8,128)(2,1)S(1)} %get-tuple-element.142), channel_id=1, source_target_pairs={{6,0},{0,2},{2,4},{4,6},{7,1},{1,3},{3,5},{5,7},{14,8},{8,10},{10,... | collective-permute-start | bytes 835592 | tf_op jit(solution)/shard_map/ppermute | solution.py:58
  127.4 14.9 %collective-permute-start.27 = (bf16[512,512]{1,0:T(8,128)(2,1)S(1)}, bf16[512,512]{1,0:T(8,128)(2,1)S(1)}, u32[]{:S(2)}, u32[]{:S(2)}) collective-permute-start(bf16[512,512]{1,0:T(8,128)(2,1)S(1)} %slice.603), channel_id=1, source_target_pairs={{0,8},{8,0},{1,9},{9,1},{2,10},{10,2},{3,11},{11,3},{4,12},{12,4},... | collective-permute-start | bytes 1572872 | tf_op jit(solution)/shard_map/ppermute | solution.py:54
  143.5 19.2 %collective-permute-start.31 = (bf16[512,512]{1,0:T(8,128)(2,1)}, bf16[512,512]{1,0:T(8,128)(2,1)}, u32[]{:S(2)}, u32[]{:S(2)}) collective-permute-start(bf16[512,512]{1,0:T(8,128)(2,1)} %slice.602), channel_id=1, source_target_pairs={{0,8},{8,0},{1,9},{9,1},{2,10},{10,2},{3,11},{11,3},{4,12},{12,4},... | collective-permute-start | bytes 1572872 | tf_op jit(solution)/shard_map/ppermute | solution.py:54
  146.1 10.4 %collective-permute-start.30 = (bf16[136,1024]{1,0:T(8,128)(2,1)S(1)}, bf16[136,1024]{1,0:T(8,128)(2,1)S(1)}, u32[]{:S(2)}, u32[]{:S(2)}) collective-permute-start(bf16[136,1024]{1,0:T(8,128)(2,1)S(1)} %pad.14), channel_id=1, source_target_pairs={{6,0},{0,2},{2,4},{4,6},{7,1},{1,3},{3,5},{5,7},{14,8},{8,10},{10,... | collective-permute-start | bytes 835592 | tf_op jit(solution)/shard_map/ppermute | solution.py:58
  148.4 13.1 %collective-permute-start.29 = (bf16[136,1024]{1,0:T(8,128)(2,1)S(1)}, bf16[136,1024]{1,0:T(8,128)(2,1)}, u32[]{:S(2)}, u32[]{:S(2)}) collective-permute-start(bf16[136,1024]{1,0:T(8,128)(2,1)S(1)} %pad.14), channel_id=1, source_target_pairs={{4,0},{6,2},{0,4},{2,6},{5,1},{7,3},{1,5},{3,7},{12,8},{14,10},{8,... | collective-permute-start | bytes 835592 | tf_op jit(solution)/shard_map/ppermute | solution.py:58
  150.6 10.9 %collective-permute-start.28 = (bf16[136,1024]{1,0:T(8,128)(2,1)S(1)}, bf16[136,1024]{1,0:T(8,128)(2,1)}, u32[]{:S(2)}, u32[]{:S(2)}) collective-permute-start(bf16[136,1024]{1,0:T(8,128)(2,1)S(1)} %pad.14), channel_id=1, source_target_pairs={{2,0},{4,2},{6,4},{0,6},{3,1},{5,3},{7,5},{1,7},{10,8},{12,10},{14... | collective-permute-start | bytes 835592 | tf_op jit(solution)/shard_map/ppermute | solution.py:58
  197.9 16.2 %collective-permute-start.38 = (bf16[519,512]{1,0:T(8,128)(2,1)}, bf16[519,512]{1,0:T(8,128)(2,1)S(1)}, u32[]{:S(2)}, u32[]{:S(2)}) collective-permute-start(bf16[519,512]{1,0:T(8,128)(2,1)} %pad_maximum_fusion.10), channel_id=1, source_target_pairs={{0,8},{8,0},{1,9},{9,1},{2,10},{10,2},{3,11},{11,3},{4,12},{12,4},... | collective-permute-start | bytes 1594376 | tf_op jit(solution)/shard_map/ppermute | solution.py:54
  201.2 15.0 %collective-permute-start.36 = (bf16[136,1024]{1,0:T(8,128)(2,1)S(1)}, bf16[136,1024]{1,0:T(8,128)(2,1)S(1)}, u32[]{:S(2)}, u32[]{:S(2)}) collective-permute-start(bf16[136,1024]{1,0:T(8,128)(2,1)S(1)} %get-tuple-element.140), channel_id=1, source_target_pairs={{2,0},{4,2},{6,4},{0,6},{3,1},{5,3},{7,5},{1,7},{10,8},{12,10},{14... | collective-permute-start | bytes 835592 | tf_op jit(solution)/shard_map/ppermute | solution.py:58
  203.9 12.3 %collective-permute-start.35 = (bf16[136,1024]{1,0:T(8,128)(2,1)S(1)}, bf16[136,1024]{1,0:T(8,128)(2,1)S(1)}, u32[]{:S(2)}, u32[]{:S(2)}) collective-permute-start(bf16[136,1024]{1,0:T(8,128)(2,1)S(1)} %get-tuple-element.141), channel_id=1, source_target_pairs={{4,0},{6,2},{0,4},{2,6},{5,1},{7,3},{1,5},{3,7},{12,8},{14,10},{8,... | collective-permute-start | bytes 835592 | tf_op jit(solution)/shard_map/ppermute | solution.py:58
  204.6 15.2 %collective-permute-start.34 = (bf16[136,1024]{1,0:T(8,128)(2,1)S(1)}, bf16[136,1024]{1,0:T(8,128)(2,1)S(1)}, u32[]{:S(2)}, u32[]{:S(2)}) collective-permute-start(bf16[136,1024]{1,0:T(8,128)(2,1)S(1)} %get-tuple-element.139), channel_id=1, source_target_pairs={{6,0},{0,2},{2,4},{4,6},{7,1},{1,3},{3,5},{5,7},{14,8},{8,10},{10,... | collective-permute-start | bytes 835592 | tf_op jit(solution)/shard_map/ppermute | solution.py:58
  222.0 12.1 %collective-permute-start.37 = (bf16[544,1024]{1,0:T(8,128)(2,1)S(1)}, bf16[544,1024]{1,0:T(8,128)(2,1)S(1)}, u32[]{:S(2)}, u32[]{:S(2)}) collective-permute-start(bf16[544,1024]{1,0:T(8,128)(2,1)S(1)} %convolution_convert_fusion), channel_id=1, source_target_pairs={{0,1},{1,0},{2,3},{3,2},{4,5},{5,4},{6,7},{7,6},{8,9},{9,8},{10,11... | collective-permute-start | bytes 3342344 | tf_op jit(solution)/shard_map/ppermute | solution.py:54
  228.3 20.9 %collective-permute-start.49 = (bf16[392,512]{1,0:T(8,128)(2,1)S(1)}, bf16[392,512]{1,0:T(8,128)(2,1)S(1)}, u32[]{:S(2)}, u32[]{:S(2)}) collective-permute-start(bf16[392,512]{1,0:T(8,128)(2,1)S(1)} %pad_maximum_fusion.13), channel_id=1, source_target_pairs={{32,0},{64,32},{96,64},{0,96},{33,1},{65,33},{97,65},{1,97},{34,2}... | collective-permute-start | bytes 1204232 | tf_op jit(solution)/shard_map/ppermute | solution.py:58
  232.7 16.6 %collective-permute-start.48 = (bf16[392,512]{1,0:T(8,128)(2,1)S(1)}, bf16[392,512]{1,0:T(8,128)(2,1)S(1)}, u32[]{:S(2)}, u32[]{:S(2)}) collective-permute-start(bf16[392,512]{1,0:T(8,128)(2,1)S(1)} %pad_maximum_fusion.12), channel_id=1, source_target_pairs={{64,0},{96,32},{0,64},{32,96},{65,1},{97,33},{1,65},{33,97},{66,2}... | collective-permute-start | bytes 1204232 | tf_op jit(solution)/shard_map/ppermute | solution.py:58
  232.8 20.1 %collective-permute-start.47 = (bf16[392,512]{1,0:T(8,128)(2,1)S(1)}, bf16[392,512]{1,0:T(8,128)(2,1)S(1)}, u32[]{:S(2)}, u32[]{:S(2)}) collective-permute-start(bf16[392,512]{1,0:T(8,128)(2,1)S(1)} %pad_maximum_fusion.11), channel_id=1, source_target_pairs={{96,0},{0,32},{32,64},{64,96},{97,1},{1,33},{33,65},{65,97},{98,2}... | collective-permute-start | bytes 1204232 | tf_op jit(solution)/shard_map/ppermute | solution.py:58
  235.0 23.2 %collective-permute-start.42 = (bf16[136,1024]{1,0:T(8,128)(2,1)S(1)}, bf16[136,1024]{1,0:T(8,128)(2,1)S(1)}, u32[]{:S(2)}, u32[]{:S(2)}) collective-permute-start(bf16[136,1024]{1,0:T(8,128)(2,1)S(1)} %get-tuple-element.48), channel_id=1, source_target_pairs={{2,0},{4,2},{6,4},{0,6},{3,1},{5,3},{7,5},{1,7},{10,8},{12,10},{14... | collective-permute-start | bytes 835592 | tf_op jit(solution)/shard_map/ppermute | solution.py:58
  235.6 22.5 %collective-permute-start.41 = (bf16[136,1024]{1,0:T(8,128)(2,1)S(1)}, bf16[136,1024]{1,0:T(8,128)(2,1)S(1)}, u32[]{:S(2)}, u32[]{:S(2)}) collective-permute-start(bf16[136,1024]{1,0:T(8,128)(2,1)S(1)} %get-tuple-element.47), channel_id=1, source_target_pairs={{4,0},{6,2},{0,4},{2,6},{5,1},{7,3},{1,5},{3,7},{12,8},{14,10},{8,... | collective-permute-start | bytes 835592 | tf_op jit(solution)/shard_map/ppermute | solution.py:58
  249.2 8.9 %collective-permute-start.40 = (bf16[136,1024]{1,0:T(8,128)(2,1)S(1)}, bf16[136,1024]{1,0:T(8,128)(2,1)S(1)}, u32[]{:S(2)}, u32[]{:S(2)}) collective-permute-start(bf16[136,1024]{1,0:T(8,128)(2,1)S(1)} %get-tuple-element.46), channel_id=1, source_target_pairs={{6,0},{0,2},{2,4},{4,6},{7,1},{1,3},{3,5},{5,7},{14,8},{8,10},{10,... | collective-permute-start | bytes 835592 | tf_op jit(solution)/shard_map/ppermute | solution.py:58
  249.3 11.4 %collective-permute-start.45 = (bf16[129,512]{1,0:T(8,128)(2,1)S(1)}, bf16[129,512]{1,0:T(8,128)(2,1)S(1)}, u32[]{:S(2)}, u32[]{:S(2)}) collective-permute-start(bf16[129,512]{1,0:T(8,128)(2,1)S(1)} %get-tuple-element.108), channel_id=1, source_target_pairs={{4,0},{5,1},{6,2},{7,3},{12,4},{13,5},{14,6},{15,7},{0,8},{1,9},{2... | collective-permute-start | bytes 396296 | tf_op jit(solution)/shard_map/ppermute | solution.py:75
  252.9 12.3 %collective-permute-start.46 = (bf16[129,512]{1,0:T(8,128)(2,1)S(1)}, bf16[129,512]{1,0:T(8,128)(2,1)S(1)}, u32[]{:S(2)}, u32[]{:S(2)}) collective-permute-start(bf16[129,512]{1,0:T(8,128)(2,1)S(1)} %get-tuple-element.109), channel_id=1, source_target_pairs={{8,4},{9,5},{10,6},{11,7},{4,8},{5,9},{6,10},{7,11},{24,20},{25,21... | collective-permute-start | bytes 396296 | tf_op jit(solution)/shard_map/ppermute | solution.py:76
  258.4 14.7 %collective-permute-start.50 = (bf16[392,512]{1,0:T(8,128)(2,1)S(1)}, bf16[392,512]{1,0:T(8,128)(2,1)S(1)}, u32[]{:S(2)}, u32[]{:S(2)}) collective-permute-start(bf16[392,512]{1,0:T(8,128)(2,1)S(1)} %fusion.20), channel_id=1, source_target_pairs={{0,16},{16,0},{1,17},{17,1},{2,18},{18,2},{3,19},{19,3},{4,20},{20... | collective-permute-start | bytes 1204232 | tf_op jit(solution)/shard_map/ppermute | solution.py:54
  265.3 12.0 %collective-permute-start.43 = (bf16[129,512]{1,0:T(8,128)(2,1)S(1)}, bf16[129,512]{1,0:T(8,128)(2,1)S(1)}, u32[]{:S(2)}, u32[]{:S(2)}) collective-permute-start(bf16[129,512]{1,0:T(8,128)(2,1)S(1)} %get-tuple-element.113), channel_id=1, source_target_pairs={{4,0},{5,1},{6,2},{7,3},{12,4},{13,5},{14,6},{15,7},{0,8},{1,9},{2... | collective-permute-start | bytes 396296 | tf_op jit(solution)/shard_map/ppermute | solution.py:75
  265.4 11.9 %collective-permute-start.44 = (bf16[129,512]{1,0:T(8,128)(2,1)S(1)}, bf16[129,512]{1,0:T(8,128)(2,1)S(1)}, u32[]{:S(2)}, u32[]{:S(2)}) collective-permute-start(bf16[129,512]{1,0:T(8,128)(2,1)S(1)} %get-tuple-element.114), channel_id=1, source_target_pairs={{8,4},{9,5},{10,6},{11,7},{4,8},{5,9},{6,10},{7,11},{24,20},{25,21... | collective-permute-start | bytes 396296 | tf_op jit(solution)/shard_map/ppermute | solution.py:76
  273.2 19.1 %collective-permute-start.53 = (bf16[392,512]{1,0:T(8,128)(2,1)S(1)}, bf16[392,512]{1,0:T(8,128)(2,1)S(1)}, u32[]{:S(2)}, u32[]{:S(2)}) collective-permute-start(bf16[392,512]{1,0:T(8,128)(2,1)S(1)} %add_convert_fusion), channel_id=1, source_target_pairs={{96,0},{0,32},{32,64},{64,96},{97,1},{1,33},{33,65},{65,97},{98,2}... | collective-permute-start | bytes 1204232 | tf_op jit(solution)/shard_map/ppermute | solution.py:58
  273.3 19.0 %collective-permute-start.52 = (bf16[392,512]{1,0:T(8,128)(2,1)S(1)}, bf16[392,512]{1,0:T(8,128)(2,1)S(1)}, u32[]{:S(2)}, u32[]{:S(2)}) collective-permute-start(bf16[392,512]{1,0:T(8,128)(2,1)S(1)} %add_convert_fusion), channel_id=1, source_target_pairs={{64,0},{96,32},{0,64},{32,96},{65,1},{97,33},{1,65},{33,97},{66,2}... | collective-permute-start | bytes 1204232 | tf_op jit(solution)/shard_map/ppermute | solution.py:58
  276.0 16.9 %collective-permute-start.51 = (bf16[392,512]{1,0:T(8,128)(2,1)S(1)}, bf16[392,512]{1,0:T(8,128)(2,1)S(1)}, u32[]{:S(2)}, u32[]{:S(2)}) collective-permute-start(bf16[392,512]{1,0:T(8,128)(2,1)S(1)} %add_convert_fusion), channel_id=1, source_target_pairs={{32,0},{64,32},{96,64},{0,96},{33,1},{65,33},{97,65},{1,97},{34,2}... | collective-permute-start | bytes 1204232 | tf_op jit(solution)/shard_map/ppermute | solution.py:58
  (57 other events, 585.5 us)

commit v3 on v2

--- a/solution.py
+++ b/solution.py
@@ -126,9 +126,10 @@
     return total.astype(BF)
 
 
-def replica_gather(total, split):
+def replica_gather(total, split, *beside):
     z = lax.axis_index("z")
     total = (total.astype(F32) + swap(total, "xl").astype(F32)).astype(BF)
+    total = after(total, *beside)
     pieces = [total] + [pull(total, "z", d) for d in (1, 2, 3)]
 
     def whole(parts):
@@ -381,8 +382,7 @@
     first_pull = norm_pull(normed_grad, scaled_first, inverse_first, gains[0])
     input_grad = place_out(upstream + first_pull, home)
     quarter = replica_scatter([fc_sum, late])
-    quarter = after(quarter, branch_second, first_pull)
-    fc_sum, late = replica_gather(quarter, fc_sum.shape[0] // NZ)
+    fc_sum, late = replica_gather(quarter, fc_sum.shape[0] // NZ, branch_second, first_pull)
 
     qkv_grad = late[: D // 2, :384].reshape(D // 2, 3, 2, HD).transpose(0, 2, 1, 3)
     out_grad = late[: D // 2, 384:].T

time: 307 us -> 304 us (level)
    ppermute x30, waiting for transfers between devices: 84.6 us -> 89.2 us  [pull(): lax.ppermute(value, axis, [((i + distance) % 4, i) for i in range(4)])]
    ppermute x2, waiting for transfers between devices: 4.54 us -> 0.48 us  [place_out(): crossed = lax.ppermute(other, GROUP, EXIT_SECOND)]
    ppermute x16, waiting for transfers between devices: 23.9 us -> 20.6 us  [swap(): return lax.ppermute(value, axis, [(0, 1), (1, 0)])]
where the time goes in v3:
time: 304 us; the launch traced here: 298 us
  waiting for transfers between devices  120 us (39%)
  starting transfers between devices  85.5 us (28%)
  other arithmetic  27.5 us (9%)
  matrix products  25.9 us (9%)
  local copies, waits for them, and re-layouts  19.7 us (6%)
  Pallas kernels  17 us (6%)
    ppermute x30, waiting for transfers between devices, pull(): lax.ppermute(value, axis, [((i + distance) % 4, i) for i in range(4)])  89.2 us
    ppermute x30, starting transfers between devices, pull(): lax.ppermute(value, axis, [((i + distance) % 4, i) for i in range(4)])  39.9 us
    dot_general x24, matrix products, dot(): lax.dot_general(first, second, (((contract[0],), (contract[1],)), ((), ()...  25.9 us
    ppermute x16, waiting for transfers between devices, swap(): return lax.ppermute(value, axis, [(0, 1), (1, 0)])  20.6 us
    ppermute x16, starting transfers between devices, swap(): return lax.ppermute(value, axis, [(0, 1), (1, 0)])  20 us
    pallas_call x2, Pallas kernels, local_kernel(): pl.pallas_call(kernel, out_shape=jax.ShapeDtypeStruct((SLOTS * ROWS, widt...  17 us
    ppermute x2, starting transfers between devices, place_in(): crossed = lax.ppermute(second, GROUP, ENTRY_SECOND)  11.6 us
    ppermute x2, starting transfers between devices, place_out(): crossed = lax.ppermute(other, GROUP, EXIT_SECOND)  10 us
  transfers between devices with their start and end apart: 54, of which 29 were waited for; matrix products, arithmetic and copies ran while one was open for 12% of the time, Pallas kernels for 0%

profile of v3, /device:TPU:4, one launch (start us, length us, event | category | flops | bytes accessed | tf_op | source)
XLA Modules:
  0.0 298.2 jit_solution(5028006889776637434)
XLA Ops:
  3.0 7.6 %collective-permute-start.1 = (bf16[136,512]{1,0:T(8,128)(2,1)S(1)}, bf16[136,512]{1,0:T(8,128)(2,1)S(1)}, u32[]{:S(2)}, u32[]{:S(2)}) collective-permute-start(bf16[136,512]{1,0:T(8,128)(2,1)S(1)} %get-tuple-element.162), channel_id=1, source_target_pairs={{4,8},{5,9},{6,10},{7,11},{8,4},{9,5},{10,6},{11,7},{20,24},{21,25... | collective-permute-start | bytes 417800 | tf_op jit(solution)/shard_map/ppermute | solution.py:69
  10.7 4.5 %collective-permute-done.1 = bf16[136,512]{1,0:T(8,128)(2,1)S(1)} collective-permute-done((bf16[136,512]{1,0:T(8,128)(2,1)S(1)}, bf16[136,512]{1,0:T(8,128)(2,1)S(1)}, u32[]{:S(2)}, u32[]{:S(2)}) %collective-permute-start.1) | collective-permute-done | bytes 139296 | tf_op jit(solution)/shard_map/ppermute | solution.py:69
  16.8 2.8 collective-permute-start.2
  20.6 4.4 %collective-permute-start.5 = (bf16[528,512]{1,0:T(8,128)(2,1)}, bf16[528,512]{1,0:T(8,128)(2,1)}, u32[]{:S(2)}, u32[]{:S(2)}) collective-permute-start(bf16[528,512]{1,0:T(8,128)(2,1)} %fusion.35), channel_id=1, source_target_pairs={{0,8},{8,0},{1,9},{9,1},{2,10},{10,2},{3,11},{11,3},{4,12},{12,4},... | collective-permute-start | bytes 1622024 | tf_op jit(solution)/shard_map/ppermute | solution.py:54
  25.0 5.9 %collective-permute-done.4 = bf16[136,1024]{1,0:T(8,128)(2,1)S(1)} collective-permute-done((bf16[136,1024]{1,0:T(8,128)(2,1)S(1)}, bf16[136,1024]{1,0:T(8,128)(2,1)S(1)}, u32[]{:S(2)}, u32[]{:S(2)}) %collective-permute-start.4) | collective-permute-done | bytes 278560 | tf_op jit(solution)/shard_map/ppermute | solution.py:58
  31.7 2.3 collective-permute-start.8
  33.9 3.9 %collective-permute-start.9 = (bf16[136,512]{1,0:T(8,128)(2,1)S(1)}, bf16[136,512]{1,0:T(8,128)(2,1)S(1)}, u32[]{:S(2)}, u32[]{:S(2)}) collective-permute-start(bf16[136,512]{1,0:T(8,128)(2,1)S(1)} %get-tuple-element.164), channel_id=1, source_target_pairs={{4,8},{5,9},{6,10},{7,11},{8,4},{9,5},{10,6},{11,7},{20,24},{21,25... | collective-permute-start | bytes 417800 | tf_op jit(solution)/shard_map/ppermute | solution.py:69
  39.5 5.4 %collective-permute-done.9 = bf16[136,512]{1,0:T(8,128)(2,1)S(1)} collective-permute-done((bf16[136,512]{1,0:T(8,128)(2,1)S(1)}, bf16[136,512]{1,0:T(8,128)(2,1)S(1)}, u32[]{:S(2)}, u32[]{:S(2)}) %collective-permute-start.9) | collective-permute-done | bytes 139296 | tf_op jit(solution)/shard_map/ppermute | solution.py:69
  47.0 2.7 collective-permute-start.10
  56.4 3.1 %collective-permute-done.12 = bf16[136,1024]{1,0:T(8,128)(2,1)} collective-permute-done((bf16[136,1024]{1,0:T(8,128)(2,1)}, bf16[136,1024]{1,0:T(8,128)(2,1)}, u32[]{:S(2)}, u32[]{:S(2)}) %collective-permute-start.12) | collective-permute-done | bytes 278560 | tf_op jit(solution)/shard_map/ppermute | solution.py:58
  60.8 2.4 fusion.3
  63.3 2.5 collective-permute-done.7
  65.8 4.8 %shard_map.211 = bf16[1088,128]{1,0:T(8,128)(2,1)S(1)} custom-call(f32[1,1088]{1,0:T(1,128)S(1)} %compare_convert_fusion.mask_ref, bf16[1088,384]{1,0:T(8,128)(2,1)S(1)} %pad_maximum_fusion.7.packed_ref), custom_call_target="tpu_custom_call" | custom-call | flops 8000000000 | bytes 24000000 | tf_op jit(solution)/shard_map/pallas_call | solution.py:212
  71.1 2.7 collective-permute-done.13
  76.7 3.3 %collective-permute-start.17 = (bf16[512,512]{1,0:T(8,128)(2,1)S(1)}, bf16[512,512]{1,0:T(8,128)(2,1)S(1)}, u32[]{:S(2)}, u32[]{:S(2)}) collective-permute-start(bf16[512,512]{1,0:T(8,128)(2,1)S(1)} %bitcast.111), channel_id=1, source_target_pairs={{0,8},{8,0},{1,9},{9,1},{2,10},{10,2},{3,11},{11,3},{4,12},{12,4},... | collective-permute-start | bytes 1572872 | tf_op jit(solution)/shard_map/ppermute | solution.py:54
  80.0 3.9 %collective-permute-done.16 = bf16[136,1024]{1,0:T(8,128)(2,1)S(1)} collective-permute-done((bf16[136,1024]{1,0:T(8,128)(2,1)S(1)}, bf16[136,1024]{1,0:T(8,128)(2,1)S(1)}, u32[]{:S(2)}, u32[]{:S(2)}) %collective-permute-start.16) | collective-permute-done | bytes 278560 | tf_op jit(solution)/shard_map/ppermute | solution.py:58
  83.9 2.7 collective-permute-done.15
  86.6 4.8 %collective-permute-done.14 = bf16[136,1024]{1,0:T(8,128)(2,1)S(1)} collective-permute-done((bf16[136,1024]{1,0:T(8,128)(2,1)S(1)}, bf16[136,1024]{1,0:T(8,128)(2,1)S(1)}, u32[]{:S(2)}, u32[]{:S(2)}) %collective-permute-start.14) | collective-permute-done | bytes 278560 | tf_op jit(solution)/shard_map/ppermute | solution.py:58
  92.6 2.4 collective-permute-start.21
  94.9 2.4 collective-permute-start.20
  99.1 3.4 %collective-permute-done.21 = bf16[136,1024]{1,0:T(8,128)(2,1)S(1)} collective-permute-done((bf16[136,1024]{1,0:T(8,128)(2,1)S(1)}, bf16[136,1024]{1,0:T(8,128)(2,1)S(1)}, u32[]{:S(2)}, u32[]{:S(2)}) %collective-permute-start.21) | collective-permute-done | bytes 278560 | tf_op jit(solution)/shard_map/ppermute | solution.py:58
  102.5 7.1 %collective-permute-done.20 = bf16[136,1024]{1,0:T(8,128)(2,1)S(1)} collective-permute-done((bf16[136,1024]{1,0:T(8,128)(2,1)S(1)}, bf16[136,1024]{1,0:T(8,128)(2,1)S(1)}, u32[]{:S(2)}, u32[]{:S(2)}) %collective-permute-start.20) | collective-permute-done | bytes 278560 | tf_op jit(solution)/shard_map/ppermute | solution.py:58
  120.8 2.2 collective-permute-start.26
  129.4 6.1 %collective-permute-done.26 = bf16[136,1024]{1,0:T(8,128)(2,1)S(1)} collective-permute-done((bf16[136,1024]{1,0:T(8,128)(2,1)S(1)}, bf16[136,1024]{1,0:T(8,128)(2,1)S(1)}, u32[]{:S(2)}, u32[]{:S(2)}) %collective-permute-start.26) | collective-permute-done | bytes 278560 | tf_op jit(solution)/shard_map/ppermute | solution.py:58
  135.5 3.7 %collective-permute-done.24 = bf16[136,1024]{1,0:T(8,128)(2,1)S(1)} collective-permute-done((bf16[136,1024]{1,0:T(8,128)(2,1)S(1)}, bf16[136,1024]{1,0:T(8,128)(2,1)S(1)}, u32[]{:S(2)}, u32[]{:S(2)}) %collective-permute-start.24) | collective-permute-done | bytes 278560 | tf_op jit(solution)/shard_map/ppermute | solution.py:58
  140.1 2.2 collective-permute-done.27
  143.5 2.2 collective-permute-start.31
  146.1 2.3 collective-permute-start.30
  148.4 2.2 collective-permute-start.29
  152.7 3.7 %collective-permute-done.30 = bf16[136,1024]{1,0:T(8,128)(2,1)S(1)} collective-permute-done((bf16[136,1024]{1,0:T(8,128)(2,1)S(1)}, bf16[136,1024]{1,0:T(8,128)(2,1)S(1)}, u32[]{:S(2)}, u32[]{:S(2)}) %collective-permute-start.30) | collective-permute-done | bytes 278560 | tf_op jit(solution)/shard_map/ppermute | solution.py:58
  156.5 5.1 %collective-permute-done.29 = bf16[136,1024]{1,0:T(8,128)(2,1)} collective-permute-done((bf16[136,1024]{1,0:T(8,128)(2,1)S(1)}, bf16[136,1024]{1,0:T(8,128)(2,1)}, u32[]{:S(2)}, u32[]{:S(2)}) %collective-permute-start.29) | collective-permute-done | bytes 278560 | tf_op jit(solution)/shard_map/ppermute | solution.py:58
  162.7 2.6 slice_add_fusion
  169.9 12.3 %shard_map.212 = bf16[1088,384]{1,0:T(8,128)(2,1)S(1)} custom-call(f32[1,1088]{1,0:T(1,128)S(1)} %compare_convert_fusion.mask_ref, bf16[1088,384]{1,0:T(8,128)(2,1)S(1)} %pad_maximum_fusion.7.packed_ref, bf16[1088,128]{1,0:T(8,128)(2,1)S(1)} %pad_maximum_fusion.16.grad_ref), custom_call_target="tpu_custom_call" | custom-call | flops 12000000000 | bytes 36000000 | tf_op jit(solution)/shard_map/pallas_call | solution.py:212
  186.8 2.3 fusion.76
  198.8 2.3 fusion.96
  201.2 2.7 collective-permute-start.36
  204.8 9.3 %collective-permute-done.38 = bf16[519,512]{1,0:T(8,128)(2,1)S(1)} collective-permute-done((bf16[519,512]{1,0:T(8,128)(2,1)}, bf16[519,512]{1,0:T(8,128)(2,1)S(1)}, u32[]{:S(2)}, u32[]{:S(2)}) %collective-permute-start.38) | collective-permute-done | bytes 531488 | tf_op jit(solution)/shard_map/ppermute | solution.py:54
  216.2 3.7 %collective-permute-done.34 = bf16[136,1024]{1,0:T(8,128)(2,1)S(1)} collective-permute-done((bf16[136,1024]{1,0:T(8,128)(2,1)S(1)}, bf16[136,1024]{1,0:T(8,128)(2,1)S(1)}, u32[]{:S(2)}, u32[]{:S(2)}) %collective-permute-start.34) | collective-permute-done | bytes 278560 | tf_op jit(solution)/shard_map/ppermute | solution.py:58
  222.1 2.6 collective-permute-start.39
  226.3 5.0 %collective-permute-start.46 = (bf16[129,512]{1,0:T(8,128)(2,1)S(1)}, bf16[129,512]{1,0:T(8,128)(2,1)S(1)}, u32[]{:S(2)}, u32[]{:S(2)}) collective-permute-start(bf16[129,512]{1,0:T(8,128)(2,1)S(1)} %get-tuple-element.109), channel_id=1, source_target_pairs={{8,4},{9,5},{10,6},{11,7},{4,8},{5,9},{6,10},{7,11},{24,20},{25,21... | collective-permute-start | bytes 396296 | tf_op jit(solution)/shard_map/ppermute | solution.py:76
  232.2 4.1 %collective-permute-start.49 = (bf16[392,512]{1,0:T(8,128)(2,1)S(1)}, bf16[392,512]{1,0:T(8,128)(2,1)S(1)}, u32[]{:S(2)}, u32[]{:S(2)}) collective-permute-start(bf16[392,512]{1,0:T(8,128)(2,1)S(1)} %pad_maximum_fusion.13), channel_id=1, source_target_pairs={{32,0},{64,32},{96,64},{0,96},{33,1},{65,33},{97,65},{1,97},{34,2}... | collective-permute-start | bytes 1204232 | tf_op jit(solution)/shard_map/ppermute | solution.py:58
  240.0 13.2 %collective-permute-done.49 = bf16[392,512]{1,0:T(8,128)(2,1)S(1)} collective-permute-done((bf16[392,512]{1,0:T(8,128)(2,1)S(1)}, bf16[392,512]{1,0:T(8,128)(2,1)S(1)}, u32[]{:S(2)}, u32[]{:S(2)}) %collective-permute-start.49) | collective-permute-done | bytes 401440 | tf_op jit(solution)/shard_map/ppermute | solution.py:58
  253.3 3.6 %collective-permute-done.47 = bf16[392,512]{1,0:T(8,128)(2,1)S(1)} collective-permute-done((bf16[392,512]{1,0:T(8,128)(2,1)S(1)}, bf16[392,512]{1,0:T(8,128)(2,1)S(1)}, u32[]{:S(2)}, u32[]{:S(2)}) %collective-permute-start.47) | collective-permute-done | bytes 401440 | tf_op jit(solution)/shard_map/ppermute | solution.py:58
  259.0 2.6 collective-permute-done.40
  261.9 5.1 %collective-permute-start.44 = (bf16[129,512]{1,0:T(8,128)(2,1)S(1)}, bf16[129,512]{1,0:T(8,128)(2,1)S(1)}, u32[]{:S(2)}, u32[]{:S(2)}) collective-permute-start(bf16[129,512]{1,0:T(8,128)(2,1)S(1)} %get-tuple-element.114), channel_id=1, source_target_pairs={{8,4},{9,5},{10,6},{11,7},{4,8},{5,9},{6,10},{7,11},{24,20},{25,21... | collective-permute-start | bytes 396296 | tf_op jit(solution)/shard_map/ppermute | solution.py:76
  267.0 2.3 collective-permute-done.50
  269.5 3.0 collective-permute-start.52
  274.9 13.6 %collective-permute-done.53 = bf16[392,512]{1,0:T(8,128)(2,1)S(1)} collective-permute-done((bf16[392,512]{1,0:T(8,128)(2,1)S(1)}, bf16[392,512]{1,0:T(8,128)(2,1)S(1)}, u32[]{:S(2)}, u32[]{:S(2)}) %collective-permute-start.53) | collective-permute-done | bytes 401440 | tf_op jit(solution)/shard_map/ppermute | solution.py:58
  (346 shorter events, 91.0 us)
Async XLA Ops:
  2.5 8.2 %collective-permute-start = (bf16[136,512]{1,0:T(8,128)(2,1)S(1)}, bf16[136,512]{1,0:T(8,128)(2,1)S(1)}, u32[]{:S(2)}, u32[]{:S(2)}) collective-permute-start(bf16[136,512]{1,0:T(8,128)(2,1)S(1)} %get-tuple-element.163), channel_id=1, source_target_pairs={{0,4},{1,5},{2,6},{3,7},{4,12},{5,13},{6,14},{7,15},{8,0},{9,1},{1... | collective-permute-start | bytes 417800 | tf_op jit(solution)/shard_map/ppermute | solution.py:68
  3.0 12.2 %collective-permute-start.1 = (bf16[136,512]{1,0:T(8,128)(2,1)S(1)}, bf16[136,512]{1,0:T(8,128)(2,1)S(1)}, u32[]{:S(2)}, u32[]{:S(2)}) collective-permute-start(bf16[136,512]{1,0:T(8,128)(2,1)S(1)} %get-tuple-element.162), channel_id=1, source_target_pairs={{4,8},{5,9},{6,10},{7,11},{8,4},{9,5},{10,6},{11,7},{20,24},{21,25... | collective-permute-start | bytes 417800 | tf_op jit(solution)/shard_map/ppermute | solution.py:69
  16.1 14.7 %collective-permute-start.4 = (bf16[136,1024]{1,0:T(8,128)(2,1)S(1)}, bf16[136,1024]{1,0:T(8,128)(2,1)S(1)}, u32[]{:S(2)}, u32[]{:S(2)}) collective-permute-start(bf16[136,1024]{1,0:T(8,128)(2,1)S(1)} %add_convert_fusion.2), channel_id=1, source_target_pairs={{6,0},{0,2},{2,4},{4,6},{7,1},{1,3},{3,5},{5,7},{14,8},{8,10},{10,... | collective-permute-start | bytes 835592 | tf_op jit(solution)/shard_map/ppermute | solution.py:58
  16.8 14.1 %collective-permute-start.3 = (bf16[136,1024]{1,0:T(8,128)(2,1)S(1)}, bf16[136,1024]{1,0:T(8,128)(2,1)S(1)}, u32[]{:S(2)}, u32[]{:S(2)}) collective-permute-start(bf16[136,1024]{1,0:T(8,128)(2,1)S(1)} %add_convert_fusion.2), channel_id=1, source_target_pairs={{4,0},{6,2},{0,4},{2,6},{5,1},{7,3},{1,5},{3,7},{12,8},{14,10},{8,... | collective-permute-start | bytes 835592 | tf_op jit(solution)/shard_map/ppermute | solution.py:58
  16.8 14.7 %collective-permute-start.2 = (bf16[136,1024]{1,0:T(8,128)(2,1)S(1)}, bf16[136,1024]{1,0:T(8,128)(2,1)S(1)}, u32[]{:S(2)}, u32[]{:S(2)}) collective-permute-start(bf16[136,1024]{1,0:T(8,128)(2,1)S(1)} %add_convert_fusion.2), channel_id=1, source_target_pairs={{2,0},{4,2},{6,4},{0,6},{3,1},{5,3},{7,5},{1,7},{10,8},{12,10},{14... | collective-permute-start | bytes 835592 | tf_op jit(solution)/shard_map/ppermute | solution.py:58
  20.6 29.1 %collective-permute-start.5 = (bf16[528,512]{1,0:T(8,128)(2,1)}, bf16[528,512]{1,0:T(8,128)(2,1)}, u32[]{:S(2)}, u32[]{:S(2)}) collective-permute-start(bf16[528,512]{1,0:T(8,128)(2,1)} %fusion.35), channel_id=1, source_target_pairs={{0,8},{8,0},{1,9},{9,1},{2,10},{10,2},{3,11},{11,3},{4,12},{12,4},... | collective-permute-start | bytes 1622024 | tf_op jit(solution)/shard_map/ppermute | solution.py:54
  33.9 11.0 %collective-permute-start.9 = (bf16[136,512]{1,0:T(8,128)(2,1)S(1)}, bf16[136,512]{1,0:T(8,128)(2,1)S(1)}, u32[]{:S(2)}, u32[]{:S(2)}) collective-permute-start(bf16[136,512]{1,0:T(8,128)(2,1)S(1)} %get-tuple-element.164), channel_id=1, source_target_pairs={{4,8},{5,9},{6,10},{7,11},{8,4},{9,5},{10,6},{11,7},{20,24},{21,25... | collective-permute-start | bytes 417800 | tf_op jit(solution)/shard_map/ppermute | solution.py:69
  39.5 21.3 %collective-permute-start.6 = (bf16[544,1024]{1,0:T(8,128)(2,1)S(1)}, bf16[544,1024]{1,0:T(8,128)(2,1)}, u32[]{:S(2)}, u32[]{:S(2)}) collective-permute-start(bf16[544,1024]{1,0:T(8,128)(2,1)S(1)} %pad_maximum_fusion), channel_id=1, source_target_pairs={{0,1},{1,0},{2,3},{3,2},{4,5},{5,4},{6,7},{7,6},{8,9},{9,8},{10,11... | collective-permute-start | bytes 3342344 | tf_op jit(solution)/shard_map/ppermute | solution.py:54
  45.8 13.6 %collective-permute-start.12 = (bf16[136,1024]{1,0:T(8,128)(2,1)}, bf16[136,1024]{1,0:T(8,128)(2,1)}, u32[]{:S(2)}, u32[]{:S(2)}) collective-permute-start(bf16[136,1024]{1,0:T(8,128)(2,1)} %get-tuple-element.34), channel_id=1, source_target_pairs={{6,0},{0,2},{2,4},{4,6},{7,1},{1,3},{3,5},{5,7},{14,8},{8,10},{10,... | collective-permute-start | bytes 835592 | tf_op jit(solution)/shard_map/ppermute | solution.py:58
  47.0 12.5 %collective-permute-start.11 = (bf16[136,1024]{1,0:T(8,128)(2,1)}, bf16[136,1024]{1,0:T(8,128)(2,1)}, u32[]{:S(2)}, u32[]{:S(2)}) collective-permute-start(bf16[136,1024]{1,0:T(8,128)(2,1)} %get-tuple-element.34), channel_id=1, source_target_pairs={{4,0},{6,2},{0,4},{2,6},{5,1},{7,3},{1,5},{3,7},{12,8},{14,10},{8,... | collective-permute-start | bytes 835592 | tf_op jit(solution)/shard_map/ppermute | solution.py:58
  47.0 12.5 %collective-permute-start.10 = (bf16[136,1024]{1,0:T(8,128)(2,1)}, bf16[136,1024]{1,0:T(8,128)(2,1)}, u32[]{:S(2)}, u32[]{:S(2)}) collective-permute-start(bf16[136,1024]{1,0:T(8,128)(2,1)} %get-tuple-element.34), channel_id=1, source_target_pairs={{2,0},{4,2},{6,4},{0,6},{3,1},{5,3},{7,5},{1,7},{10,8},{12,10},{14... | collective-permute-start | bytes 835592 | tf_op jit(solution)/shard_map/ppermute | solution.py:58
  52.8 12.9 %collective-permute-start.7 = (bf16[512,512]{1,0:T(8,128)(2,1)S(1)}, bf16[512,512]{1,0:T(8,128)(2,1)S(1)}, u32[]{:S(2)}, u32[]{:S(2)}) collective-permute-start(bf16[512,512]{1,0:T(8,128)(2,1)S(1)} %bitcast.128), channel_id=1, source_target_pairs={{0,8},{8,0},{1,9},{9,1},{2,10},{10,2},{3,11},{11,3},{4,12},{12,4},... | collective-permute-start | bytes 1572872 | tf_op jit(solution)/shard_map/ppermute | solution.py:54
  74.3 9.6 %collective-permute-start.16 = (bf16[136,1024]{1,0:T(8,128)(2,1)S(1)}, bf16[136,1024]{1,0:T(8,128)(2,1)S(1)}, u32[]{:S(2)}, u32[]{:S(2)}) collective-permute-start(bf16[136,1024]{1,0:T(8,128)(2,1)S(1)} %get-tuple-element.146), channel_id=1, source_target_pairs={{2,0},{4,2},{6,4},{0,6},{3,1},{5,3},{7,5},{1,7},{10,8},{12,10},{14... | collective-permute-start | bytes 835592 | tf_op jit(solution)/shard_map/ppermute | solution.py:58
  75.5 11.1 %collective-permute-start.15 = (bf16[136,1024]{1,0:T(8,128)(2,1)S(1)}, bf16[136,1024]{1,0:T(8,128)(2,1)S(1)}, u32[]{:S(2)}, u32[]{:S(2)}) collective-permute-start(bf16[136,1024]{1,0:T(8,128)(2,1)S(1)} %get-tuple-element.147), channel_id=1, source_target_pairs={{4,0},{6,2},{0,4},{2,6},{5,1},{7,3},{1,5},{3,7},{12,8},{14,10},{8,... | collective-permute-start | bytes 835592 | tf_op jit(solution)/shard_map/ppermute | solution.py:58
  76.7 14.7 %collective-permute-start.14 = (bf16[136,1024]{1,0:T(8,128)(2,1)S(1)}, bf16[136,1024]{1,0:T(8,128)(2,1)S(1)}, u32[]{:S(2)}, u32[]{:S(2)}) collective-permute-start(bf16[136,1024]{1,0:T(8,128)(2,1)S(1)} %get-tuple-element.145), channel_id=1, source_target_pairs={{6,0},{0,2},{2,4},{4,6},{7,1},{1,3},{3,5},{5,7},{14,8},{8,10},{10,... | collective-permute-start | bytes 835592 | tf_op jit(solution)/shard_map/ppermute | solution.py:58
  76.7 15.9 %collective-permute-start.18 = (bf16[544,1024]{1,0:T(8,128)(2,1)S(1)}, bf16[544,1024]{1,0:T(8,128)(2,1)S(1)}, u32[]{:S(2)}, u32[]{:S(2)}) collective-permute-start(bf16[544,1024]{1,0:T(8,128)(2,1)S(1)} %pad_maximum_fusion.1), channel_id=1, source_target_pairs={{0,1},{1,0},{2,3},{3,2},{4,5},{5,4},{6,7},{7,6},{8,9},{9,8},{10,11... | collective-permute-start | bytes 3342344 | tf_op jit(solution)/shard_map/ppermute | solution.py:54
  76.7 15.9 %collective-permute-start.17 = (bf16[512,512]{1,0:T(8,128)(2,1)S(1)}, bf16[512,512]{1,0:T(8,128)(2,1)S(1)}, u32[]{:S(2)}, u32[]{:S(2)}) collective-permute-start(bf16[512,512]{1,0:T(8,128)(2,1)S(1)} %bitcast.111), channel_id=1, source_target_pairs={{0,8},{8,0},{1,9},{9,1},{2,10},{10,2},{3,11},{11,3},{4,12},{12,4},... | collective-permute-start | bytes 1572872 | tf_op jit(solution)/shard_map/ppermute | solution.py:54
  92.6 9.9 %collective-permute-start.21 = (bf16[136,1024]{1,0:T(8,128)(2,1)S(1)}, bf16[136,1024]{1,0:T(8,128)(2,1)S(1)}, u32[]{:S(2)}, u32[]{:S(2)}) collective-permute-start(bf16[136,1024]{1,0:T(8,128)(2,1)S(1)} %add_convert_fusion.1), channel_id=1, source_target_pairs={{6,0},{0,2},{2,4},{4,6},{7,1},{1,3},{3,5},{5,7},{14,8},{8,10},{10,... | collective-permute-start | bytes 835592 | tf_op jit(solution)/shard_map/ppermute | solution.py:58
  94.9 14.6 %collective-permute-start.20 = (bf16[136,1024]{1,0:T(8,128)(2,1)S(1)}, bf16[136,1024]{1,0:T(8,128)(2,1)S(1)}, u32[]{:S(2)}, u32[]{:S(2)}) collective-permute-start(bf16[136,1024]{1,0:T(8,128)(2,1)S(1)} %add_convert_fusion.1), channel_id=1, source_target_pairs={{4,0},{6,2},{0,4},{2,6},{5,1},{7,3},{1,5},{3,7},{12,8},{14,10},{8,... | collective-permute-start | bytes 835592 | tf_op jit(solution)/shard_map/ppermute | solution.py:58
  97.3 12.2 %collective-permute-start.19 = (bf16[136,1024]{1,0:T(8,128)(2,1)S(1)}, bf16[136,1024]{1,0:T(8,128)(2,1)S(1)}, u32[]{:S(2)}, u32[]{:S(2)}) collective-permute-start(bf16[136,1024]{1,0:T(8,128)(2,1)S(1)} %add_convert_fusion.1), channel_id=1, source_target_pairs={{2,0},{4,2},{6,4},{0,6},{3,1},{5,3},{7,5},{1,7},{10,8},{12,10},{14... | collective-permute-start | bytes 835592 | tf_op jit(solution)/shard_map/ppermute | solution.py:58
  120.8 14.7 %collective-permute-start.26 = (bf16[136,1024]{1,0:T(8,128)(2,1)S(1)}, bf16[136,1024]{1,0:T(8,128)(2,1)S(1)}, u32[]{:S(2)}, u32[]{:S(2)}) collective-permute-start(bf16[136,1024]{1,0:T(8,128)(2,1)S(1)} %get-tuple-element.143), channel_id=1, source_target_pairs={{2,0},{4,2},{6,4},{0,6},{3,1},{5,3},{7,5},{1,7},{10,8},{12,10},{14... | collective-permute-start | bytes 835592 | tf_op jit(solution)/shard_map/ppermute | solution.py:58
  123.1 12.4 %collective-permute-start.25 = (bf16[136,1024]{1,0:T(8,128)(2,1)S(1)}, bf16[136,1024]{1,0:T(8,128)(2,1)S(1)}, u32[]{:S(2)}, u32[]{:S(2)}) collective-permute-start(bf16[136,1024]{1,0:T(8,128)(2,1)S(1)} %get-tuple-element.144), channel_id=1, source_target_pairs={{4,0},{6,2},{0,4},{2,6},{5,1},{7,3},{1,5},{3,7},{12,8},{14,10},{8,... | collective-permute-start | bytes 835592 | tf_op jit(solution)/shard_map/ppermute | solution.py:58
  124.2 15.0 %collective-permute-start.24 = (bf16[136,1024]{1,0:T(8,128)(2,1)S(1)}, bf16[136,1024]{1,0:T(8,128)(2,1)S(1)}, u32[]{:S(2)}, u32[]{:S(2)}) collective-permute-start(bf16[136,1024]{1,0:T(8,128)(2,1)S(1)} %get-tuple-element.142), channel_id=1, source_target_pairs={{6,0},{0,2},{2,4},{4,6},{7,1},{1,3},{3,5},{5,7},{14,8},{8,10},{10,... | collective-permute-start | bytes 835592 | tf_op jit(solution)/shard_map/ppermute | solution.py:58
  127.4 14.9 %collective-permute-start.27 = (bf16[512,512]{1,0:T(8,128)(2,1)S(1)}, bf16[512,512]{1,0:T(8,128)(2,1)S(1)}, u32[]{:S(2)}, u32[]{:S(2)}) collective-permute-start(bf16[512,512]{1,0:T(8,128)(2,1)S(1)} %slice.601), channel_id=1, source_target_pairs={{0,8},{8,0},{1,9},{9,1},{2,10},{10,2},{3,11},{11,3},{4,12},{12,4},... | collective-permute-start | bytes 1572872 | tf_op jit(solution)/shard_map/ppermute | solution.py:54
  143.5 19.2 %collective-permute-start.31 = (bf16[512,512]{1,0:T(8,128)(2,1)}, bf16[512,512]{1,0:T(8,128)(2,1)}, u32[]{:S(2)}, u32[]{:S(2)}) collective-permute-start(bf16[512,512]{1,0:T(8,128)(2,1)} %slice.600), channel_id=1, source_target_pairs={{0,8},{8,0},{1,9},{9,1},{2,10},{10,2},{3,11},{11,3},{4,12},{12,4},... | collective-permute-start | bytes 1572872 | tf_op jit(solution)/shard_map/ppermute | solution.py:54
  146.1 10.4 %collective-permute-start.30 = (bf16[136,1024]{1,0:T(8,128)(2,1)S(1)}, bf16[136,1024]{1,0:T(8,128)(2,1)S(1)}, u32[]{:S(2)}, u32[]{:S(2)}) collective-permute-start(bf16[136,1024]{1,0:T(8,128)(2,1)S(1)} %pad.14), channel_id=1, source_target_pairs={{6,0},{0,2},{2,4},{4,6},{7,1},{1,3},{3,5},{5,7},{14,8},{8,10},{10,... | collective-permute-start | bytes 835592 | tf_op jit(solution)/shard_map/ppermute | solution.py:58
  148.4 13.1 %collective-permute-start.29 = (bf16[136,1024]{1,0:T(8,128)(2,1)S(1)}, bf16[136,1024]{1,0:T(8,128)(2,1)}, u32[]{:S(2)}, u32[]{:S(2)}) collective-permute-start(bf16[136,1024]{1,0:T(8,128)(2,1)S(1)} %pad.14), channel_id=1, source_target_pairs={{4,0},{6,2},{0,4},{2,6},{5,1},{7,3},{1,5},{3,7},{12,8},{14,10},{8,... | collective-permute-start | bytes 835592 | tf_op jit(solution)/shard_map/ppermute | solution.py:58
  150.6 10.9 %collective-permute-start.28 = (bf16[136,1024]{1,0:T(8,128)(2,1)S(1)}, bf16[136,1024]{1,0:T(8,128)(2,1)}, u32[]{:S(2)}, u32[]{:S(2)}) collective-permute-start(bf16[136,1024]{1,0:T(8,128)(2,1)S(1)} %pad.14), channel_id=1, source_target_pairs={{2,0},{4,2},{6,4},{0,6},{3,1},{5,3},{7,5},{1,7},{10,8},{12,10},{14... | collective-permute-start | bytes 835592 | tf_op jit(solution)/shard_map/ppermute | solution.py:58
  197.9 16.2 %collective-permute-start.38 = (bf16[519,512]{1,0:T(8,128)(2,1)}, bf16[519,512]{1,0:T(8,128)(2,1)S(1)}, u32[]{:S(2)}, u32[]{:S(2)}) collective-permute-start(bf16[519,512]{1,0:T(8,128)(2,1)} %pad_maximum_fusion.10), channel_id=1, source_target_pairs={{0,8},{8,0},{1,9},{9,1},{2,10},{10,2},{3,11},{11,3},{4,12},{12,4},... | collective-permute-start | bytes 1594376 | tf_op jit(solution)/shard_map/ppermute | solution.py:54
  201.2 15.0 %collective-permute-start.36 = (bf16[136,1024]{1,0:T(8,128)(2,1)S(1)}, bf16[136,1024]{1,0:T(8,128)(2,1)S(1)}, u32[]{:S(2)}, u32[]{:S(2)}) collective-permute-start(bf16[136,1024]{1,0:T(8,128)(2,1)S(1)} %get-tuple-element.140), channel_id=1, source_target_pairs={{2,0},{4,2},{6,4},{0,6},{3,1},{5,3},{7,5},{1,7},{10,8},{12,10},{14... | collective-permute-start | bytes 835592 | tf_op jit(solution)/shard_map/ppermute | solution.py:58
  203.9 12.3 %collective-permute-start.35 = (bf16[136,1024]{1,0:T(8,128)(2,1)S(1)}, bf16[136,1024]{1,0:T(8,128)(2,1)S(1)}, u32[]{:S(2)}, u32[]{:S(2)}) collective-permute-start(bf16[136,1024]{1,0:T(8,128)(2,1)S(1)} %get-tuple-element.141), channel_id=1, source_target_pairs={{4,0},{6,2},{0,4},{2,6},{5,1},{7,3},{1,5},{3,7},{12,8},{14,10},{8,... | collective-permute-start | bytes 835592 | tf_op jit(solution)/shard_map/ppermute | solution.py:58
  204.6 15.2 %collective-permute-start.34 = (bf16[136,1024]{1,0:T(8,128)(2,1)S(1)}, bf16[136,1024]{1,0:T(8,128)(2,1)S(1)}, u32[]{:S(2)}, u32[]{:S(2)}) collective-permute-start(bf16[136,1024]{1,0:T(8,128)(2,1)S(1)} %get-tuple-element.139), channel_id=1, source_target_pairs={{6,0},{0,2},{2,4},{4,6},{7,1},{1,3},{3,5},{5,7},{14,8},{8,10},{10,... | collective-permute-start | bytes 835592 | tf_op jit(solution)/shard_map/ppermute | solution.py:58
  222.0 14.5 %collective-permute-start.37 = (bf16[544,1024]{1,0:T(8,128)(2,1)S(1)}, bf16[544,1024]{1,0:T(8,128)(2,1)S(1)}, u32[]{:S(2)}, u32[]{:S(2)}) collective-permute-start(bf16[544,1024]{1,0:T(8,128)(2,1)S(1)} %convolution_convert_fusion), channel_id=1, source_target_pairs={{0,1},{1,0},{2,3},{3,2},{4,5},{5,4},{6,7},{7,6},{8,9},{9,8},{10,11... | collective-permute-start | bytes 3342344 | tf_op jit(solution)/shard_map/ppermute | solution.py:54
  222.1 9.1 %collective-permute-start.39 = (f32[2,512]{1,0:T(2,128)S(1)}, f32[2,512]{1,0:T(2,128)S(1)}, u32[]{:S(2)}, u32[]{:S(2)}) collective-permute-start(f32[2,512]{1,0:T(2,128)S(1)} %slice.461), channel_id=1, source_target_pairs={{0,8},{8,0},{1,9},{9,1},{2,10},{10,2},{3,11},{11,3},{4,12},{12,4},... | collective-permute-start | bytes 12296 | tf_op jit(solution)/shard_map/ppermute | solution.py:54
  225.0 13.7 %collective-permute-start.45 = (bf16[129,512]{1,0:T(8,128)(2,1)S(1)}, bf16[129,512]{1,0:T(8,128)(2,1)S(1)}, u32[]{:S(2)}, u32[]{:S(2)}) collective-permute-start(bf16[129,512]{1,0:T(8,128)(2,1)S(1)} %get-tuple-element.108), channel_id=1, source_target_pairs={{4,0},{5,1},{6,2},{7,3},{12,4},{13,5},{14,6},{15,7},{0,8},{1,9},{2... | collective-permute-start | bytes 396296 | tf_op jit(solution)/shard_map/ppermute | solution.py:75
  226.3 12.5 %collective-permute-start.46 = (bf16[129,512]{1,0:T(8,128)(2,1)S(1)}, bf16[129,512]{1,0:T(8,128)(2,1)S(1)}, u32[]{:S(2)}, u32[]{:S(2)}) collective-permute-start(bf16[129,512]{1,0:T(8,128)(2,1)S(1)} %get-tuple-element.109), channel_id=1, source_target_pairs={{8,4},{9,5},{10,6},{11,7},{4,8},{5,9},{6,10},{7,11},{24,20},{25,21... | collective-permute-start | bytes 396296 | tf_op jit(solution)/shard_map/ppermute | solution.py:76
  232.2 21.0 %collective-permute-start.49 = (bf16[392,512]{1,0:T(8,128)(2,1)S(1)}, bf16[392,512]{1,0:T(8,128)(2,1)S(1)}, u32[]{:S(2)}, u32[]{:S(2)}) collective-permute-start(bf16[392,512]{1,0:T(8,128)(2,1)S(1)} %pad_maximum_fusion.13), channel_id=1, source_target_pairs={{32,0},{64,32},{96,64},{0,96},{33,1},{65,33},{97,65},{1,97},{34,2}... | collective-permute-start | bytes 1204232 | tf_op jit(solution)/shard_map/ppermute | solution.py:58
  236.4 16.9 %collective-permute-start.48 = (bf16[392,512]{1,0:T(8,128)(2,1)S(1)}, bf16[392,512]{1,0:T(8,128)(2,1)S(1)}, u32[]{:S(2)}, u32[]{:S(2)}) collective-permute-start(bf16[392,512]{1,0:T(8,128)(2,1)S(1)} %pad_maximum_fusion.12), channel_id=1, source_target_pairs={{64,0},{96,32},{0,64},{32,96},{65,1},{97,33},{1,65},{33,97},{66,2}... | collective-permute-start | bytes 1204232 | tf_op jit(solution)/shard_map/ppermute | solution.py:58
  236.5 20.4 %collective-permute-start.47 = (bf16[392,512]{1,0:T(8,128)(2,1)S(1)}, bf16[392,512]{1,0:T(8,128)(2,1)S(1)}, u32[]{:S(2)}, u32[]{:S(2)}) collective-permute-start(bf16[392,512]{1,0:T(8,128)(2,1)S(1)} %pad_maximum_fusion.11), channel_id=1, source_target_pairs={{96,0},{0,32},{32,64},{64,96},{97,1},{1,33},{33,65},{65,97},{98,2}... | collective-permute-start | bytes 1204232 | tf_op jit(solution)/shard_map/ppermute | solution.py:58
  238.7 20.3 %collective-permute-start.42 = (bf16[136,1024]{1,0:T(8,128)(2,1)S(1)}, bf16[136,1024]{1,0:T(8,128)(2,1)S(1)}, u32[]{:S(2)}, u32[]{:S(2)}) collective-permute-start(bf16[136,1024]{1,0:T(8,128)(2,1)S(1)} %get-tuple-element.48), channel_id=1, source_target_pairs={{2,0},{4,2},{6,4},{0,6},{3,1},{5,3},{7,5},{1,7},{10,8},{12,10},{14... | collective-permute-start | bytes 835592 | tf_op jit(solution)/shard_map/ppermute | solution.py:58
  238.8 20.2 %collective-permute-start.41 = (bf16[136,1024]{1,0:T(8,128)(2,1)S(1)}, bf16[136,1024]{1,0:T(8,128)(2,1)S(1)}, u32[]{:S(2)}, u32[]{:S(2)}) collective-permute-start(bf16[136,1024]{1,0:T(8,128)(2,1)S(1)} %get-tuple-element.47), channel_id=1, source_target_pairs={{4,0},{6,2},{0,4},{2,6},{5,1},{7,3},{1,5},{3,7},{12,8},{14,10},{8,... | collective-permute-start | bytes 835592 | tf_op jit(solution)/shard_map/ppermute | solution.py:58
  253.2 8.3 %collective-permute-start.40 = (bf16[136,1024]{1,0:T(8,128)(2,1)S(1)}, bf16[136,1024]{1,0:T(8,128)(2,1)S(1)}, u32[]{:S(2)}, u32[]{:S(2)}) collective-permute-start(bf16[136,1024]{1,0:T(8,128)(2,1)S(1)} %get-tuple-element.46), channel_id=1, source_target_pairs={{6,0},{0,2},{2,4},{4,6},{7,1},{1,3},{3,5},{5,7},{14,8},{8,10},{10,... | collective-permute-start | bytes 835592 | tf_op jit(solution)/shard_map/ppermute | solution.py:58
  257.2 12.1 %collective-permute-start.50 = (bf16[392,512]{1,0:T(8,128)(2,1)S(1)}, bf16[392,512]{1,0:T(8,128)(2,1)S(1)}, u32[]{:S(2)}, u32[]{:S(2)}) collective-permute-start(bf16[392,512]{1,0:T(8,128)(2,1)S(1)} %fusion.20), channel_id=1, source_target_pairs={{0,16},{16,0},{1,17},{17,1},{2,18},{18,2},{3,19},{19,3},{4,20},{20... | collective-permute-start | bytes 1204232 | tf_op jit(solution)/shard_map/ppermute | solution.py:54
  261.8 11.7 %collective-permute-start.43 = (bf16[129,512]{1,0:T(8,128)(2,1)S(1)}, bf16[129,512]{1,0:T(8,128)(2,1)S(1)}, u32[]{:S(2)}, u32[]{:S(2)}) collective-permute-start(bf16[129,512]{1,0:T(8,128)(2,1)S(1)} %get-tuple-element.113), channel_id=1, source_target_pairs={{4,0},{5,1},{6,2},{7,3},{12,4},{13,5},{14,6},{15,7},{0,8},{1,9},{2... | collective-permute-start | bytes 396296 | tf_op jit(solution)/shard_map/ppermute | solution.py:75
  261.9 12.1 %collective-permute-start.44 = (bf16[129,512]{1,0:T(8,128)(2,1)S(1)}, bf16[129,512]{1,0:T(8,128)(2,1)S(1)}, u32[]{:S(2)}, u32[]{:S(2)}) collective-permute-start(bf16[129,512]{1,0:T(8,128)(2,1)S(1)} %get-tuple-element.114), channel_id=1, source_target_pairs={{8,4},{9,5},{10,6},{11,7},{4,8},{5,9},{6,10},{7,11},{24,20},{25,21... | collective-permute-start | bytes 396296 | tf_op jit(solution)/shard_map/ppermute | solution.py:76
  269.4 19.2 %collective-permute-start.53 = (bf16[392,512]{1,0:T(8,128)(2,1)S(1)}, bf16[392,512]{1,0:T(8,128)(2,1)S(1)}, u32[]{:S(2)}, u32[]{:S(2)}) collective-permute-start(bf16[392,512]{1,0:T(8,128)(2,1)S(1)} %add_convert_fusion), channel_id=1, source_target_pairs={{96,0},{0,32},{32,64},{64,96},{97,1},{1,33},{33,65},{65,97},{98,2}... | collective-permute-start | bytes 1204232 | tf_op jit(solution)/shard_map/ppermute | solution.py:58
  269.5 19.1 %collective-permute-start.52 = (bf16[392,512]{1,0:T(8,128)(2,1)S(1)}, bf16[392,512]{1,0:T(8,128)(2,1)S(1)}, u32[]{:S(2)}, u32[]{:S(2)}) collective-permute-start(bf16[392,512]{1,0:T(8,128)(2,1)S(1)} %add_convert_fusion), channel_id=1, source_target_pairs={{64,0},{96,32},{0,64},{32,96},{65,1},{97,33},{1,65},{33,97},{66,2}... | collective-permute-start | bytes 1204232 | tf_op jit(solution)/shard_map/ppermute | solution.py:58
  272.4 16.7 %collective-permute-start.51 = (bf16[392,512]{1,0:T(8,128)(2,1)S(1)}, bf16[392,512]{1,0:T(8,128)(2,1)S(1)}, u32[]{:S(2)}, u32[]{:S(2)}) collective-permute-start(bf16[392,512]{1,0:T(8,128)(2,1)S(1)} %add_convert_fusion), channel_id=1, source_target_pairs={{32,0},{64,32},{96,64},{0,96},{33,1},{65,33},{97,65},{1,97},{34,2}... | collective-permute-start | bytes 1204232 | tf_op jit(solution)/shard_map/ppermute | solution.py:58
  (57 other events, 582.7 us)
